TPU v7x, 32 devices: a whole 2x2x4 slice. The times are simulated.
32 devices in a mesh: ctx: 8 (over z, x), kvh: 4 (over y, core).
Axes of the slice: x: 2, y: 2, z: 4, core: 2. Of those that a mesh axis runs over, the one named last changes fastest.
Arguments:
- queries: bfloat16 [8192, 8192], P('ctx', 'kvh'), may hold values from -8 to 8
- keys: bfloat16 [8192, 1024], P(('ctx', 'kvh')), may hold values from -8 to 8
- values: bfloat16 [8192, 1024], P(('ctx', 'kvh')), may hold values from -6 to 6
- out_grad: bfloat16 [8192, 8192], P('ctx', 'kvh'), may hold values from -6 to 6
- random_blocks: int32 [64, 3], replicated, may hold values from 8 to 63, as said below
Outputs:
- attended: bfloat16 [8192, 8192], P('ctx', 'kvh')
- query_grad: bfloat16 [8192, 8192], P('ctx', 'kvh')
- key_grad: bfloat16 [8192, 1024], P(('ctx', 'kvh'))
- value_grad: bfloat16 [8192, 1024], P(('ctx', 'kvh'))
Inputs may be any that keep to these rules, and one draw needn't show every extreme that they name: `random_blocks`: block b lies on ctx index b // 8. For each query block the 3 named blocks lie on 3 different ctx indices, none of them 0, the index holding the query block, or its two neighbours. Over the 8 rows of one ctx index, the named blocks (repeats counted) fall on 4 ctx indices as evenly as possible: none holds more than 6 of them and some holds exactly 6.
All inputs are finite; a program needn't handle non-finite values.
Results may differ from a plain program's by a relative error of at most 0.014.
Values may be sent and summed in bfloat16 or wider, within the bound.
No kernel may reach another device: no remote copies, remote signals or barrier semaphores. Data moves between devices by JAX's collectives and lax.ppermute only.
A program may use at most 128 MiB of HBM per device.

v0:
```python
from functools import partial

import jax
import jax.numpy as jnp
from jax import lax
from jax.sharding import PartitionSpec as P

HD = 128
BLK = 128
GLOB = 2


def attend_block(operands, score_scale):
    query_rows, grad_rows, key_rows, value_rows, usable = operands
    scores = (
        jnp.einsum("bgqd,kgd->gqbk", query_rows, key_rows, preferred_element_type=jnp.float32)
        * score_scale
    )
    scores = jnp.where(usable, scores, -jnp.inf)
    largest = jnp.max(scores, axis=-1, keepdims=True)
    raised = jnp.exp(scores - largest)
    probs = raised / jnp.sum(raised, axis=-1, keepdims=True)
    weights = probs.astype(jnp.bfloat16)
    attended = jnp.einsum("gqbk,kgd->bgqd", weights, value_rows, preferred_element_type=jnp.float32)
    prob_grad = jnp.einsum(
        "bgqd,kgd->gqbk", grad_rows, value_rows, preferred_element_type=jnp.float32
    )
    centre = jnp.sum(probs * prob_grad, axis=-1, keepdims=True)
    score_grad = (probs * (prob_grad - centre) * score_scale).astype(jnp.bfloat16)
    query_grad = jnp.einsum(
        "gqbk,kgd->bgqd", score_grad, key_rows, preferred_element_type=jnp.float32
    )
    key_grad = jnp.einsum(
        "gqbk,bgqd->kgd", score_grad, query_rows, preferred_element_type=jnp.float32
    )
    value_grad = jnp.einsum(
        "gqbk,bgqd->kgd", weights, grad_rows, preferred_element_type=jnp.float32
    )
    return (attended.astype(jnp.bfloat16), query_grad.astype(jnp.bfloat16), key_grad, value_grad)


def per_device(queries, keys, values, out_grad, random_blocks):
    block_len = BLK
    ctx_count = lax.axis_size("ctx")
    ctx_index = lax.axis_index("ctx")
    stacked = jnp.stack([keys, values])
    local_kv = lax.all_to_all(stacked, "kvh", split_axis=2, concat_axis=1, tiled=True)
    tok_rows = local_kv.shape[1]
    row_width = local_kv.shape[2]
    groups = row_width // HD
    query_blocks = tok_rows // block_len
    all_blocks = query_blocks * ctx_count
    rand_count = random_blocks.shape[1]
    select_count = 3 + GLOB + rand_count
    first_block = ctx_index * query_blocks
    my_random = lax.dynamic_slice_in_dim(random_blocks, first_block, query_blocks, 0)
    block_ids = first_block + jnp.arange(query_blocks, dtype=jnp.int32)
    window_ids = block_ids[:, None] - 1 + jnp.arange(3, dtype=jnp.int32)[None, :]
    window_ok = (window_ids >= GLOB) & (window_ids < all_blocks)
    entry_ok = jnp.concatenate(
        [window_ok, jnp.ones((query_blocks, GLOB + rand_count), jnp.bool_)], axis=1
    )
    usable = jnp.repeat(entry_ok, block_len, axis=1)
    whole_kv = lax.all_gather(local_kv, "ctx", axis=1, tiled=True)
    whole_blocks = whole_kv.reshape(2, all_blocks, block_len, row_width)
    global_ids = jnp.broadcast_to(jnp.arange(GLOB, dtype=jnp.int32)[None, :], (query_blocks, GLOB))
    listed = jnp.concatenate([window_ids, global_ids, my_random], axis=1)
    listed = jnp.clip(listed, 0, all_blocks - 1)
    selected = whole_blocks[:, listed]
    query_rows = queries.reshape(query_blocks, block_len, groups, -1, HD)
    grad_rows = out_grad.reshape(query_blocks, block_len, groups, -1, HD)
    key_chosen = selected[0].reshape(query_blocks, select_count * block_len, groups, HD)
    value_chosen = selected[1].reshape(query_blocks, select_count * block_len, groups, HD)
    attended, query_grad, key_part, value_part = lax.map(
        partial(attend_block, score_scale=HD ** (-0.5)),
        (query_rows, grad_rows, key_chosen, value_chosen, usable),
    )
    grad_parts = jnp.stack([key_part, value_part]).reshape(
        2, query_blocks, select_count, block_len, row_width
    )
    listed_flat = listed.reshape(-1)
    entry_flat = entry_ok.reshape(-1)
    part_flat = grad_parts.reshape(2, query_blocks * select_count, block_len, row_width)
    kept_parts = jnp.where(entry_flat[None, :, None, None], part_flat, 0.0)
    placed = (
        jnp.zeros((2, all_blocks, block_len, row_width), jnp.float32)
        .at[:, listed_flat]
        .add(kept_parts)
    )
    placed_rows = jnp.moveaxis(placed, 0, 2).reshape(all_blocks * block_len, 2 * row_width)
    shares = lax.psum_scatter(
        placed_rows.astype(jnp.bfloat16), "ctx", scatter_dimension=0, tiled=True
    ).astype(jnp.float32)
    total_grad = jnp.moveaxis(shares.reshape(tok_rows, 2, row_width), 1, 0)
    rounded = total_grad.astype(jnp.bfloat16)
    home_grads = lax.all_to_all(rounded, "kvh", split_axis=1, concat_axis=2, tiled=True)
    return (
        attended.reshape(tok_rows, -1),
        query_grad.reshape(tok_rows, -1),
        home_grads[0],
        home_grads[1],
    )


def solution(mesh):
    in_specs = (
        P("ctx", "kvh"),
        P(("ctx", "kvh"), None),
        P(("ctx", "kvh"), None),
        P("ctx", "kvh"),
        P(),
    )
    out_specs = (P("ctx", "kvh"), P("ctx", "kvh"), P(("ctx", "kvh"), None), P(("ctx", "kvh"), None))
    return jax.shard_map(
        per_device, mesh=mesh, in_specs=in_specs, out_specs=out_specs, check_vma=False
    )
```

profile of v0, /device:TPU:0, one launch (start us, length us, event | category | flops | bytes accessed | tf_op | source)
XLA Modules:
  0.0 948.0 jit_solution(13000334820197842789)
XLA Ops:
  9.5 18.5 %all_to_all.33 = bf16[2,256,1024]{1,0,2:T(2,128)(2,1)S(1)} all-to-all(bf16[2,256,1024]{1,0,2:T(2,128)(2,1)S(1)} %copy.118), channel_id=1, replica_groups=mesh['ctx'=8,'kvh'=4] {'kvh'}, dimensions={2} | all-to-all | bytes 2097152 | tf_op jit(solution)/shard_map/all_to_all | solution.py:47
  30.7 5.8 copy.177
  40.4 114.4 %all-gather.2.cloned.1.call-done = bf16[2,8192,256]{2,1,0:T(8,128)(2,1)} async-done(((bf16[2,1024,256]{2,1,0:T(8,128)(2,1)}), bf16[2,8192,256]{2,1,0:T(8,128)(2,1)}) %all-gather.2.cloned.1.call-update) | async-done | bytes 8388624 | tf_op jit(solution)/shard_map/all_gather | solution.py:64
  154.8 8.8 gather_fusion
  163.6 6.0 fusion.50
  169.7 6.9 reshape.169
  176.5 6.9 reshape_squeeze.6
  183.4 459.8 %while.16 = (s32[]{:T(128)}, bf16[8,128,2,8,128]{4,3,2,1,0:T(8,128)(2,1)}, bf16[8,128,2,8,128]{4,3,2,1,0:T(8,128)(2,1)}, f32[8,1024,2,128]{3,2,1,0:T(2,128)}, f3...) while((s32[]{:T(128)}, ...), condition=%wide.region_4.5_spmd, body=%wide.region_0.4_spmd.sunk | while | flops 3267894272 | bytes 92318864 | solution.py:74
  193.6 4.8 fusion.67
  202.9 13.8 %fusion.68 = bf16[1,128,2,8,128]{1,4,3,2,0:T(8,128)(2,1)} fusion(f32[2,1024,128,8]{2,1,3,0:T(8,128)} %fusion.66, bf16[1,1024,2,128]{3,2,1,0:T(2,128)(2,1)S(1)} %constant_dynamic-slice_fusion.11, f32[2,8,128,1024]{2,3,1,0:T(8,128)} %get-tuple-element.215, f32[2,8,128]{2,1,0:T(8,128)S(1)} %get-tuple-element.216), kind=kOutput, calls=%fused_computation.29.clone.1 | convolution fusion | flops 551816192 | bytes 17833984 | tf_op jit(solution)/shard_map/while/body/eval_jaxpr/gqbk,kgd->bgqd/dot_general | solution.py:30
  216.7 13.2 %fusion.71 = f32[1,1024,2,128]{1,3,2,0:T(8,128)} fusion(f32[2,1024,128,8]{2,1,3,0:T(8,128)} %fusion.66, bf16[1,128,2,8,128]{4,3,2,1,0:T(8,128)(2,1)S(1)} %constant_dynamic-slice_fusion.12, f32[2,8,128,1024]{2,3,1,0:T(8,128)} %get-tuple-element.215, f32[2,8,128]{2,1,0:T(8,128)S(1)} %get-tuple-element.216), kind=kOutput, calls=%fused_computation.26.clone.1 | convolution fusion | flops 551554048 | bytes 18358272 | tf_op jit(solution)/shard_map/while/body/eval_jaxpr/gqbk,bgqd->kgd/dot_general | solution.py:33
  229.9 4.9 fusion.70
  260.4 13.8 %fusion.68 = bf16[1,128,2,8,128]{1,4,3,2,0:T(8,128)(2,1)} fusion(f32[2,1024,128,8]{2,1,3,0:T(8,128)} %fusion.66, bf16[1,1024,2,128]{3,2,1,0:T(2,128)(2,1)S(1)} %constant_dynamic-slice_fusion.11, f32[2,8,128,1024]{2,3,1,0:T(8,128)} %get-tuple-element.215, f32[2,8,128]{2,1,0:T(8,128)S(1)} %get-tuple-element.216), kind=kOutput, calls=%fused_computation.29.clone.1 | convolution fusion | flops 551816192 | bytes 17833984 | tf_op jit(solution)/shard_map/while/body/eval_jaxpr/gqbk,kgd->bgqd/dot_general | solution.py:30
  274.2 13.2 %fusion.71 = f32[1,1024,2,128]{1,3,2,0:T(8,128)} fusion(f32[2,1024,128,8]{2,1,3,0:T(8,128)} %fusion.66, bf16[1,128,2,8,128]{4,3,2,1,0:T(8,128)(2,1)S(1)} %constant_dynamic-slice_fusion.12, f32[2,8,128,1024]{2,3,1,0:T(8,128)} %get-tuple-element.215, f32[2,8,128]{2,1,0:T(8,128)S(1)} %get-tuple-element.216), kind=kOutput, calls=%fused_computation.26.clone.1 | convolution fusion | flops 551554048 | bytes 18358272 | tf_op jit(solution)/shard_map/while/body/eval_jaxpr/gqbk,bgqd->kgd/dot_general | solution.py:33
  287.4 4.9 fusion.70
  308.5 4.8 fusion.67
  317.9 13.8 %fusion.68 = bf16[1,128,2,8,128]{1,4,3,2,0:T(8,128)(2,1)} fusion(f32[2,1024,128,8]{2,1,3,0:T(8,128)} %fusion.66, bf16[1,1024,2,128]{3,2,1,0:T(2,128)(2,1)S(1)} %constant_dynamic-slice_fusion.11, f32[2,8,128,1024]{2,3,1,0:T(8,128)} %get-tuple-element.215, f32[2,8,128]{2,1,0:T(8,128)S(1)} %get-tuple-element.216), kind=kOutput, calls=%fused_computation.29.clone.1 | convolution fusion | flops 551816192 | bytes 17833984 | tf_op jit(solution)/shard_map/while/body/eval_jaxpr/gqbk,kgd->bgqd/dot_general | solution.py:30
  331.7 13.2 %fusion.71 = f32[1,1024,2,128]{1,3,2,0:T(8,128)} fusion(f32[2,1024,128,8]{2,1,3,0:T(8,128)} %fusion.66, bf16[1,128,2,8,128]{4,3,2,1,0:T(8,128)(2,1)S(1)} %constant_dynamic-slice_fusion.12, f32[2,8,128,1024]{2,3,1,0:T(8,128)} %get-tuple-element.215, f32[2,8,128]{2,1,0:T(8,128)S(1)} %get-tuple-element.216), kind=kOutput, calls=%fused_computation.26.clone.1 | convolution fusion | flops 551554048 | bytes 18358272 | tf_op jit(solution)/shard_map/while/body/eval_jaxpr/gqbk,bgqd->kgd/dot_general | solution.py:33
  344.9 4.9 fusion.70
  366.0 4.8 fusion.67
  375.3 13.8 %fusion.68 = bf16[1,128,2,8,128]{1,4,3,2,0:T(8,128)(2,1)} fusion(f32[2,1024,128,8]{2,1,3,0:T(8,128)} %fusion.66, bf16[1,1024,2,128]{3,2,1,0:T(2,128)(2,1)S(1)} %constant_dynamic-slice_fusion.11, f32[2,8,128,1024]{2,3,1,0:T(8,128)} %get-tuple-element.215, f32[2,8,128]{2,1,0:T(8,128)S(1)} %get-tuple-element.216), kind=kOutput, calls=%fused_computation.29.clone.1 | convolution fusion | flops 551816192 | bytes 17833984 | tf_op jit(solution)/shard_map/while/body/eval_jaxpr/gqbk,kgd->bgqd/dot_general | solution.py:30
  389.1 13.2 %fusion.71 = f32[1,1024,2,128]{1,3,2,0:T(8,128)} fusion(f32[2,1024,128,8]{2,1,3,0:T(8,128)} %fusion.66, bf16[1,128,2,8,128]{4,3,2,1,0:T(8,128)(2,1)S(1)} %constant_dynamic-slice_fusion.12, f32[2,8,128,1024]{2,3,1,0:T(8,128)} %get-tuple-element.215, f32[2,8,128]{2,1,0:T(8,128)S(1)} %get-tuple-element.216), kind=kOutput, calls=%fused_computation.26.clone.1 | convolution fusion | flops 551554048 | bytes 18358272 | tf_op jit(solution)/shard_map/while/body/eval_jaxpr/gqbk,bgqd->kgd/dot_general | solution.py:33
  402.3 4.9 fusion.70
  432.8 13.8 %fusion.68 = bf16[1,128,2,8,128]{1,4,3,2,0:T(8,128)(2,1)} fusion(f32[2,1024,128,8]{2,1,3,0:T(8,128)} %fusion.66, bf16[1,1024,2,128]{3,2,1,0:T(2,128)(2,1)S(1)} %constant_dynamic-slice_fusion.11, f32[2,8,128,1024]{2,3,1,0:T(8,128)} %get-tuple-element.215, f32[2,8,128]{2,1,0:T(8,128)S(1)} %get-tuple-element.216), kind=kOutput, calls=%fused_computation.29.clone.1 | convolution fusion | flops 551816192 | bytes 17833984 | tf_op jit(solution)/shard_map/while/body/eval_jaxpr/gqbk,kgd->bgqd/dot_general | solution.py:30
  446.6 13.2 %fusion.71 = f32[1,1024,2,128]{1,3,2,0:T(8,128)} fusion(f32[2,1024,128,8]{2,1,3,0:T(8,128)} %fusion.66, bf16[1,128,2,8,128]{4,3,2,1,0:T(8,128)(2,1)S(1)} %constant_dynamic-slice_fusion.12, f32[2,8,128,1024]{2,3,1,0:T(8,128)} %get-tuple-element.215, f32[2,8,128]{2,1,0:T(8,128)S(1)} %get-tuple-element.216), kind=kOutput, calls=%fused_computation.26.clone.1 | convolution fusion | flops 551554048 | bytes 18358272 | tf_op jit(solution)/shard_map/while/body/eval_jaxpr/gqbk,bgqd->kgd/dot_general | solution.py:33
  459.8 4.9 fusion.70
  490.2 13.8 %fusion.68 = bf16[1,128,2,8,128]{1,4,3,2,0:T(8,128)(2,1)} fusion(f32[2,1024,128,8]{2,1,3,0:T(8,128)} %fusion.66, bf16[1,1024,2,128]{3,2,1,0:T(2,128)(2,1)S(1)} %constant_dynamic-slice_fusion.11, f32[2,8,128,1024]{2,3,1,0:T(8,128)} %get-tuple-element.215, f32[2,8,128]{2,1,0:T(8,128)S(1)} %get-tuple-element.216), kind=kOutput, calls=%fused_computation.29.clone.1 | convolution fusion | flops 551816192 | bytes 17833984 | tf_op jit(solution)/shard_map/while/body/eval_jaxpr/gqbk,kgd->bgqd/dot_general | solution.py:30
  504.0 13.2 %fusion.71 = f32[1,1024,2,128]{1,3,2,0:T(8,128)} fusion(f32[2,1024,128,8]{2,1,3,0:T(8,128)} %fusion.66, bf16[1,128,2,8,128]{4,3,2,1,0:T(8,128)(2,1)S(1)} %constant_dynamic-slice_fusion.12, f32[2,8,128,1024]{2,3,1,0:T(8,128)} %get-tuple-element.215, f32[2,8,128]{2,1,0:T(8,128)S(1)} %get-tuple-element.216), kind=kOutput, calls=%fused_computation.26.clone.1 | convolution fusion | flops 551554048 | bytes 18358272 | tf_op jit(solution)/shard_map/while/body/eval_jaxpr/gqbk,bgqd->kgd/dot_general | solution.py:33
  517.2 4.9 fusion.70
  538.3 4.8 fusion.67
  547.7 13.8 %fusion.68 = bf16[1,128,2,8,128]{1,4,3,2,0:T(8,128)(2,1)} fusion(f32[2,1024,128,8]{2,1,3,0:T(8,128)} %fusion.66, bf16[1,1024,2,128]{3,2,1,0:T(2,128)(2,1)S(1)} %constant_dynamic-slice_fusion.11, f32[2,8,128,1024]{2,3,1,0:T(8,128)} %get-tuple-element.215, f32[2,8,128]{2,1,0:T(8,128)S(1)} %get-tuple-element.216), kind=kOutput, calls=%fused_computation.29.clone.1 | convolution fusion | flops 551816192 | bytes 17833984 | tf_op jit(solution)/shard_map/while/body/eval_jaxpr/gqbk,kgd->bgqd/dot_general | solution.py:30
  561.5 13.2 %fusion.71 = f32[1,1024,2,128]{1,3,2,0:T(8,128)} fusion(f32[2,1024,128,8]{2,1,3,0:T(8,128)} %fusion.66, bf16[1,128,2,8,128]{4,3,2,1,0:T(8,128)(2,1)S(1)} %constant_dynamic-slice_fusion.12, f32[2,8,128,1024]{2,3,1,0:T(8,128)} %get-tuple-element.215, f32[2,8,128]{2,1,0:T(8,128)S(1)} %get-tuple-element.216), kind=kOutput, calls=%fused_computation.26.clone.1 | convolution fusion | flops 551554048 | bytes 18358272 | tf_op jit(solution)/shard_map/while/body/eval_jaxpr/gqbk,bgqd->kgd/dot_general | solution.py:33
  574.7 4.9 fusion.70
  605.1 13.8 %fusion.68 = bf16[1,128,2,8,128]{1,4,3,2,0:T(8,128)(2,1)} fusion(f32[2,1024,128,8]{2,1,3,0:T(8,128)} %fusion.66, bf16[1,1024,2,128]{3,2,1,0:T(2,128)(2,1)S(1)} %constant_dynamic-slice_fusion.11, f32[2,8,128,1024]{2,3,1,0:T(8,128)} %get-tuple-element.215, f32[2,8,128]{2,1,0:T(8,128)S(1)} %get-tuple-element.216), kind=kOutput, calls=%fused_computation.29.clone.1 | convolution fusion | flops 551816192 | bytes 17833984 | tf_op jit(solution)/shard_map/while/body/eval_jaxpr/gqbk,kgd->bgqd/dot_general | solution.py:30
  618.9 13.2 %fusion.71 = f32[1,1024,2,128]{1,3,2,0:T(8,128)} fusion(f32[2,1024,128,8]{2,1,3,0:T(8,128)} %fusion.66, bf16[1,128,2,8,128]{4,3,2,1,0:T(8,128)(2,1)S(1)} %constant_dynamic-slice_fusion.12, f32[2,8,128,1024]{2,3,1,0:T(8,128)} %get-tuple-element.215, f32[2,8,128]{2,1,0:T(8,128)S(1)} %get-tuple-element.216), kind=kOutput, calls=%fused_computation.26.clone.1 | convolution fusion | flops 551554048 | bytes 18358272 | tf_op jit(solution)/shard_map/while/body/eval_jaxpr/gqbk,bgqd->kgd/dot_general | solution.py:33
  632.1 4.9 fusion.70
  643.2 11.7 %reshape.171 = f32[1,64,128,256]{3,2,1,0:T(8,128)} reshape(f32[8,1024,2,128]{3,2,1,0:T(2,128)} %get-tuple-element.62) | data formatting | bytes 16777216 | tf_op jit(solution)/shard_map/stack | solution.py:78
  654.9 11.5 %reshape.170 = f32[1,64,128,256]{3,2,1,0:T(8,128)} reshape(f32[8,1024,2,128]{3,2,1,0:T(2,128)} %get-tuple-element.61) | data formatting | bytes 16777216 | tf_op jit(solution)/shard_map/stack | solution.py:78
  666.4 6.9 fusion.43
  673.3 6.1 copy.135
  679.4 7.8 broadcast_in_dim.58
  687.2 36.4 %scatter_fusion = f32[2,64,128,256]{3,2,1,0:T(8,128)} fusion(f32[2,64,128,256]{3,2,1,0:T(8,128)} %broadcast_in_dim.58, s32[64]{0:T(128)S(1)} %copy-done.3, f32[64,2,128,256]{3,2,1,0:T(8,128)} %copy.135), kind=kCustom, calls=%fused_computation.1 | custom fusion | flops 4194304 | bytes 50331904 | tf_op jit(solution)/shard_map/scatter-add | solution.py:88
  723.7 9.0 convert_bitcast_fusion
  732.7 12.0 %copy.136 = bf16[64,128,2,256]{1,0,3,2:T(8,128)(2,1)} copy(bf16[64,128,2,256]{3,1,0,2:T(8,128)(2,1)} %convert_bitcast_fusion) | data formatting | bytes 16777216 | tf_op jit(solution)/shard_map/convert_element_type | solution.py:92
  744.7 23.8 %copy.206 = bf16[64,8,64,128]{3,1,2,0:T(8,128)(2,1)} copy(bf16[64,8,64,128]{3,2,1,0:T(8,128)(2,1)} %bitcast.205) | data formatting | bytes 16777216
  768.5 148.1 %reduce-scatter.2.cloned.1.call-done = bf16[1024,512]{0,1:T(8,128)(2,1)} async-done(((bf16[8192,512]{0,1:T(8,128)(2,1)}), bf16[1024,512]{0,1:T(8,128)(2,1)}) %reduce-scatter.2.cloned.1.call-update) | async-done | bytes 1048592 | tf_op jit(solution)/shard_map/reduce_scatter | solution.py:91
  923.8 7.3 reshape.144
  931.1 7.3 reshape.145
  (163 shorter events, 203.2 us)
Async XLA Ops:
  7.2 23.1 %copy-start.1 = (s32[64,3]{0,1:T(4,128)S(1)}, s32[64,3]{0,1:T(4,128)}, u32[]{:S(2)}) copy-start(s32[64,3]{0,1:T(4,128)} %param.11) | copy-start | bytes 2308
  7.2 147.6 %all-gather.2.cloned.1.call-start = ((), (), s32[]{:S(2)}) async-start(), calls=%async_computation.3 | async-start | bytes 9437184 | tf_op jit(solution)/shard_map/all_gather | solution.py:64
  29.4 887.2 %reduce-scatter.2.cloned.1.call-start = ((), (), s32[]{:S(2)}) async-start(), calls=%async_computation.4 | async-start | bytes 9437184 | tf_op jit(solution)/shard_map/reduce_scatter | solution.py:91
  30.7 5.8 copy-start
  654.9 11.5 %copy-start.2 = (pred[64]{0:T(512)(128)(4,1)S(1)}, pred[64]{0:T(512)(128)(4,1)}, u32[]{:S(2)}) copy-start(pred[64]{0:T(512)(128)(4,1)} %broadcast_in_dim.60) | copy-start | bytes 196
  679.4 7.8 copy-start.3
  920.3 18.1 %all-to-all-start.1 = ((bf16[2,1024,256]{2,0,1:T(2,128)(2,1)}), bf16[2,1024,256]{2,0,1:T(2,128)(2,1)S(1)}, u32[]{:S(2)}, u32[]{:S(2)}) async-start(bf16[2,1024,256]{2,0,1:T(2,128)(2,1)} %bitcast.40), calls=%async_computation.2 | async-start | bytes 2097152 | tf_op jit(solution)/shard_map/all_to_all | solution.py:96
Sparse Core Ops, SparseCore 0:
  29.6 125.1 all-gather.1
  768.6 147.9 reduce-scatter.1
where the time goes:
time: 962 us; the launch traced here: 948 us
  matrix products  363 us (38%)
  waiting for transfers between devices  263 us (27%)
  local copies, waits for them, and re-layouts  231 us (24%)
  other arithmetic  54.3 us (6%)
  blocking collectives  18.5 us (2%)
  between operations  14.3 us (1%)
    reduce_scatter x1, waiting for transfers between devices, per_device(): lax.psum_scatter(placed_rows.astype(jnp.bfloat16), 'ctx', scatter_dimensi...  148 us
    all_gather x1, waiting for transfers between devices, per_device(): whole_kv = lax.all_gather(local_kv, 'ctx', axis=1, tiled=True)  114 us
    dot_general x8, matrix products, attend_block(): jnp.einsum('gqbk,kgd->bgqd', score_grad, key_rows, preferred_element_type...  111 us
    dot_general x8, matrix products, attend_block(): jnp.einsum('gqbk,bgqd->kgd', score_grad, query_rows, preferred_element_ty...  106 us
    dynamic_update_slice x48, local copies, waits for them, and re-layouts, per_device(): lax.map(partial(attend_block, score_scale=HD ** (-0.5)), (query_rows, gra...  52.9 us
    dynamic_slice x48, local copies, waits for them, and re-layouts, per_device(): lax.map(partial(attend_block, score_scale=HD ** (-0.5)), (query_rows, gra...  43.4 us
    dot_general x8, matrix products, attend_block(): jnp.einsum('gqbk,bgqd->kgd', weights, grad_rows, preferred_element_type=j...  39.2 us
    sub x8, matrix products, attend_block(): raised = jnp.exp(scores - largest)  38.1 us
  transfers between devices with their start and end apart: 3, of which 2 were waited for; matrix products, arithmetic and copies ran while one was open for 3% of the time, Pallas kernels for 0%

commit v1 on v0

v1 whole, which is shorter than its diff:
```python
import functools

import jax
import jax.numpy as jnp
from jax import lax
from jax.experimental import pallas as pl
from jax.experimental.pallas import tpu as pltpu
from jax.sharding import PartitionSpec as P

HD = 128
BLK = 128
GLOB = 2
DEPTH = 4
LOG2E = 1.4426950408889634
NN = (((1,), (0,)), ((), ()))
NT = (((1,), (1,)), ((), ()))
VMEM_LIMIT = 56 * 1024 * 1024


class Plan:
    def __init__(self, ctx, query_blocks, rand):
        self.ctx, self.qb, self.rand = ctx, query_blocks, rand
        self.depth = DEPTH if ctx % DEPTH == 0 else ctx
        self.lanes = ctx // self.depth
        named = query_blocks * rand
        per_owner = -(-named // max(1, ctx - 4))
        most = 0
        for device in range(ctx):
            far = [s for s in range(1, ctx) if abs(s - device) > 1]
            for lane in range(self.lanes):
                if lane != device % self.lanes:
                    most = max(most, sum(s % self.lanes == lane for s in far))
        self.slots = 2 + GLOB + min(named, per_owner * most)
        self.own = self.depth * query_blocks
        self.pool = self.own + (self.lanes - 1) * self.slots

    def column_place(self, me, owner, offset):
        row = lax.rem(me // self.lanes - owner // self.lanes + self.depth, self.depth)
        return row * self.qb + offset

    def place(self, me, owner, offset, slot):
        mine, theirs = lax.rem(me, self.lanes), lax.rem(owner, self.lanes)
        pack = lax.rem(theirs - mine + self.lanes, self.lanes) - 1
        return jnp.where(
            mine == theirs, self.column_place(me, owner, offset), self.own + pack * self.slots + slot
        )


def dot(a, b, dims):
    return lax.dot_general(a, b, dims, preferred_element_type=jnp.float32)


def fill_table(plan, me, named, table, counts):
    qb, rand, lanes = plan.qb, plan.rand, plan.lanes
    sel = 3 + GLOB + rand
    left, right = jnp.maximum(me - 1, 0), jnp.minimum(me + 1, plan.ctx - 1)
    for lane in range(lanes):
        counts[lane] = 2 + GLOB
    for i in range(qb):
        table[i * sel] = plan.place(me, left, qb - 1, 0) if i == 0 else jnp.int32(i - 1)
        table[i * sel + 1] = jnp.int32(i)
        table[i * sel + 2] = plan.place(me, right, 0, 1) if i == qb - 1 else jnp.int32(i + 1)
        for j in range(GLOB):
            table[i * sel + 3 + j] = plan.place(me, jnp.int32(0), j, 2 + j)

    def entry(n, carry):
        block = named[me * (qb * rand) + n]
        owner = block // qb
        lane = lax.rem(owner, lanes)
        slot = counts[lane]
        table[(n // rand) * sel + 3 + GLOB + lax.rem(n, rand)] = plan.place(
            me, owner, lax.rem(block, qb), slot
        )
        counts[lane] = slot + 1
        return carry

    lax.fori_loop(0, qb * rand, entry, 0)


def walk_pack(plan, me, other, named, visit):
    qb, rand, lanes = plan.qb, plan.rand, plan.lanes
    mine = lax.rem(me, lanes)

    @pl.when((other >= 1) & (lax.rem(other - 1 + lanes, lanes) == mine))
    def _():
        visit(0, plan.column_place(me, other - 1, qb - 1))

    @pl.when((other + 1 < plan.ctx) & (lax.rem(other + 1, lanes) == mine))
    def _():
        visit(1, plan.column_place(me, other + 1, 0))

    @pl.when(mine == 0)
    def _():
        for j in range(GLOB):
            visit(2 + j, plan.column_place(me, jnp.int32(0), j))

    def entry(n, slot):
        block = named[other * (qb * rand) + n]
        owner = block // qb
        hit = lax.rem(owner, lanes) == mine

        @pl.when(hit)
        def _():
            visit(slot, plan.column_place(me, owner, lax.rem(block, qb)))

        return slot + hit.astype(jnp.int32)

    lax.fori_loop(0, qb * rand, entry, jnp.int32(2 + GLOB))


def rows_of(place):
    return pl.ds(pl.multiple_of(place * BLK, BLK), BLK)


def pack_kernel(where, named, *refs, plan, step):
    shards, out = refs[: plan.depth], refs[plan.depth]
    me = where[0]
    lane = lax.rem(me, plan.lanes)
    other = me - lane + lax.rem(lane + step, plan.lanes)
    rows = plan.qb * BLK
    out[...] = jnp.zeros_like(out)

    def visit(slot, place):
        at = lax.rem(place, plan.qb)
        for k in range(plan.depth):

            @pl.when(place // plan.qb == k)
            def _():
                out[rows_of(slot), :] = shards[k][rows_of(at), :]

    walk_pack(plan, me, other, named, visit)


def pack(plan, where, named, shards, step):
    rows = plan.qb * BLK
    return pl.pallas_call(
        functools.partial(pack_kernel, plan=plan, step=step),
        grid_spec=pltpu.PrefetchScalarGridSpec(
            num_scalar_prefetch=2,
            grid=(1,),
            in_specs=[pl.BlockSpec((rows, HD), lambda n, *_: (0, 0))] * plan.depth,
            out_specs=pl.BlockSpec((plan.slots * BLK, HD), lambda n, *_: (0, 0)),
        ),
        out_shape=jax.ShapeDtypeStruct((plan.slots * BLK, HD), jnp.bfloat16),
        compiler_params=pltpu.CompilerParams(vmem_limit_bytes=VMEM_LIMIT),
        cost_estimate=pl.CostEstimate(flops=0, bytes_accessed=4 << 20, transcendentals=0),
        name="pack_blocks",
    )(where, named, *shards)


def merge_kernel(where, named, column, *refs, plan):
    packs, outs, total = refs[: plan.lanes - 1], refs[plan.lanes - 1 : -1], refs[-1]
    me = where[0]
    lane = lax.rem(me, plan.lanes)
    total[...] = column[...]
    for step in range(1, plan.lanes):
        other = me - lane + lax.rem(lane + step, plan.lanes)

        def visit(slot, place):
            total[rows_of(place), :] += packs[step - 1][rows_of(slot), :].astype(jnp.float32)

        walk_pack(plan, me, other, named, visit)
    rows = plan.qb * BLK
    for k in range(plan.depth):
        outs[k][...] = total[k * rows : (k + 1) * rows, :].astype(outs[k].dtype)


def merge(plan, where, named, column, packs):
    rows = plan.qb * BLK
    kinds = [jnp.float32] + [jnp.bfloat16] * (plan.depth - 1)
    return pl.pallas_call(
        functools.partial(merge_kernel, plan=plan),
        grid_spec=pltpu.PrefetchScalarGridSpec(
            num_scalar_prefetch=2,
            grid=(1,),
            in_specs=[pl.BlockSpec((plan.own * BLK, HD), lambda n, *_: (0, 0))]
            + [pl.BlockSpec((plan.slots * BLK, HD), lambda n, *_: (0, 0))] * len(packs),
            out_specs=[pl.BlockSpec((rows, HD), lambda n, *_: (0, 0))] * plan.depth,
            scratch_shapes=[pltpu.VMEM((plan.own * BLK, HD), jnp.float32)],
        ),
        out_shape=[jax.ShapeDtypeStruct((rows, HD), kind) for kind in kinds],
        compiler_params=pltpu.CompilerParams(vmem_limit_bytes=VMEM_LIMIT),
        cost_estimate=pl.CostEstimate(flops=0, bytes_accessed=6 << 20, transcendentals=0),
        name="merge_terms",
    )(where, named, column, *packs)


def attend_kernel(where, named, *refs, plan, qpk, per):
    parts = plan.depth + plan.lanes - 1
    q_ref, do_ref = refs[:2]
    k_parts, v_parts = refs[2 : 2 + parts], refs[2 + parts : 2 + 2 * parts]
    refs = refs[2 + 2 * parts :]
    o_ref, dq_ref, dk_col, dv_col = refs[:4]
    dk_packs, dv_packs = refs[4 : 3 + plan.lanes], refs[3 + plan.lanes : 2 + 2 * plan.lanes]
    kpool, vpool, keys, values, dk_sum, dv_sum, dk_far, dv_far, table, counts = refs[2 + 2 * plan.lanes :]
    me = where[0]
    i = pl.program_id(0)
    rows = plan.qb * BLK
    sel = 3 + GLOB + plan.rand
    scale = HD ** -0.5

    @pl.when(i == 0)
    def _():
        fill_table(plan, me, named, table, counts)
        for pool, given in ((kpool, k_parts), (vpool, v_parts)):
            at = 0
            for part in given:
                pool[at : at + part.shape[0], :] = part[...]
                at += part.shape[0]
        for total in (dk_col, dv_col, dk_far, dv_far):
            total[...] = jnp.zeros_like(total)

    for j in range(sel):
        place = rows_of(table[i * sel + j])
        keys[j * BLK : (j + 1) * BLK, :] = kpool[place, :]
        values[j * BLK : (j + 1) * BLK, :] = vpool[place, :]
    block = me * plan.qb + i
    counted = [(block - 1 + j >= GLOB) & (block - 1 + j < plan.ctx * plan.qb) for j in range(3)]
    K, V = keys[...], values[...]
    KT, VT = K.T, V.T
    for h in range(0, qpk, per):

        def stacked(ref):
            return jnp.concatenate([ref[:, (h + t) * HD : (h + t + 1) * HD] for t in range(per)], axis=0)

        q, do = stacked(q_ref), stacked(do_ref)
        scores = dot(K, q, NT)
        scores = jnp.concatenate(
            [jnp.where(counted[j], scores[j * BLK : (j + 1) * BLK], -jnp.inf) for j in range(3)]
            + [scores[3 * BLK :]],
            axis=0,
        )
        largest = jnp.max(scores, axis=0, keepdims=True)
        raised = jnp.exp2((scores - largest) * (scale * LOG2E))
        inverse = 1.0 / jnp.sum(raised, axis=0, keepdims=True)
        raised_b = raised.astype(jnp.bfloat16)
        attended = dot(VT, raised_b, NN) * inverse
        prob_grad = dot(V, do, NT)
        do_t, q_t = do.T.astype(jnp.float32), q.T.astype(jnp.float32)
        centre = jnp.sum(attended * do_t, axis=0, keepdims=True)
        score_grad = (raised * (prob_grad - centre)).astype(jnp.bfloat16)
        query_grad = dot(KT, score_grad, NN) * (inverse * scale)
        value_grad = dot(raised_b, (do_t * inverse).astype(jnp.bfloat16), NT)
        key_grad = dot(score_grad, (q_t * (inverse * scale)).astype(jnp.bfloat16), NT)
        attended, query_grad = attended.T, query_grad.T
        for t in range(per):
            o_ref[:, (h + t) * HD : (h + t + 1) * HD] = attended[t * BLK : (t + 1) * BLK].astype(jnp.bfloat16)
            dq_ref[:, (h + t) * HD : (h + t + 1) * HD] = query_grad[t * BLK : (t + 1) * BLK].astype(jnp.bfloat16)
        if h == 0:
            dk_sum[...], dv_sum[...] = key_grad, value_grad
        else:
            dk_sum[...] += key_grad
            dv_sum[...] += value_grad
    for j in range(sel):
        place = table[i * sel + j]
        part = slice(j * BLK, (j + 1) * BLK)

        @pl.when(place < plan.own)
        def _():
            dk_col[rows_of(place), :] += dk_sum[part, :]
            dv_col[rows_of(place), :] += dv_sum[part, :]

        @pl.when(place >= plan.own)
        def _():
            dk_far[rows_of(place - plan.own), :] += dk_sum[part, :]
            dv_far[rows_of(place - plan.own), :] += dv_sum[part, :]

    @pl.when(i == pl.num_programs(0) - 1)
    def _():
        size = plan.slots * BLK
        for n in range(plan.lanes - 1):
            dk_packs[n][...] = dk_far[n * size : (n + 1) * size, :].astype(jnp.bfloat16)
            dv_packs[n][...] = dv_far[n * size : (n + 1) * size, :].astype(jnp.bfloat16)


def attend(plan, where, named, queries, out_grad, k_parts, v_parts, group, qpk):
    width = qpk * HD
    sel = 3 + GLOB + plan.rand
    far = (plan.lanes - 1) * plan.slots * BLK
    whole = lambda a: pl.BlockSpec(a.shape, lambda n, *_: (0, 0))
    q_spec = pl.BlockSpec((BLK, width), lambda n, *_: (n, group))
    o_spec = pl.BlockSpec((BLK, width), lambda n, *_: (n, 0))
    o_shape = jax.ShapeDtypeStruct((plan.qb * BLK, width), jnp.bfloat16)
    column = jax.ShapeDtypeStruct((plan.own * BLK, HD), jnp.float32)
    packed = jax.ShapeDtypeStruct((plan.slots * BLK, HD), jnp.bfloat16)
    out_shape = [o_shape, o_shape, column, column] + [packed] * (2 * (plan.lanes - 1))
    pairs = plan.qb * qpk * BLK * sel * BLK
    out = pl.pallas_call(
        functools.partial(attend_kernel, plan=plan, qpk=qpk, per=4 if qpk % 4 == 0 else 1),
        grid_spec=pltpu.PrefetchScalarGridSpec(
            num_scalar_prefetch=2,
            grid=(plan.qb,),
            in_specs=[q_spec, q_spec] + [whole(a) for a in k_parts] + [whole(a) for a in v_parts],
            out_specs=[o_spec, o_spec] + [whole(s) for s in out_shape[2:]],
            scratch_shapes=[
                pltpu.VMEM((plan.pool * BLK, HD), jnp.bfloat16),
                pltpu.VMEM((plan.pool * BLK, HD), jnp.bfloat16),
                pltpu.VMEM((sel * BLK, HD), jnp.bfloat16),
                pltpu.VMEM((sel * BLK, HD), jnp.bfloat16),
                pltpu.VMEM((sel * BLK, HD), jnp.float32),
                pltpu.VMEM((sel * BLK, HD), jnp.float32),
                pltpu.VMEM((far, HD), jnp.float32),
                pltpu.VMEM((far, HD), jnp.float32),
                pltpu.SMEM((plan.qb * sel,), jnp.int32),
                pltpu.SMEM((plan.lanes,), jnp.int32),
            ],
        ),
        out_shape=out_shape,
        compiler_params=pltpu.CompilerParams(vmem_limit_bytes=VMEM_LIMIT),
        cost_estimate=pl.CostEstimate(
            flops=12 * pairs * HD, bytes_accessed=24 << 20, transcendentals=pairs
        ),
        name="attend_head",
    )(where, named, queries, out_grad, *k_parts, *v_parts)
    return out[0], out[1], out[2:4], (out[4 : 3 + plan.lanes], out[3 + plan.lanes :])


def column_shift(array, plan, rows):
    return lax.ppermute(array, "ctx", [(n, (n + rows * plan.lanes) % plan.ctx) for n in range(plan.ctx)])


def row_shift(array, plan, lanes):
    return lax.ppermute(
        array, "ctx", [(n, n - n % plan.lanes + (n + lanes) % plan.lanes) for n in range(plan.ctx)]
    )


def after(array, *others):
    return lax.optimization_barrier((array, *others))[0]


def per_device(queries, keys, values, out_grad, random_blocks):
    stacked = jnp.stack([keys, values])
    local_kv = lax.all_to_all(stacked, "kvh", split_axis=2, concat_axis=1, tiled=True)
    tok_rows = local_kv.shape[1]
    groups = local_kv.shape[2] // HD
    qpk = queries.shape[1] // (groups * HD)
    plan = Plan(lax.axis_size("ctx"), tok_rows // BLK, random_blocks.shape[1])
    lanes, depth = plan.lanes, plan.depth
    where = lax.axis_index("ctx").astype(jnp.int32).reshape(1)
    named = random_blocks.reshape(-1)

    parts, waits = [], []
    for g in range(groups):
        both = []
        for n in range(2):
            own = local_kv[n, :, g * HD : (g + 1) * HD]
            if g:
                own = after(own, *waits)
            shards = [own] + [column_shift(own, plan, k) for k in range(1, depth)]
            both.append(shards)
        waits = both[0][1:] + both[1][1:]
        for shards in both:
            packs = [row_shift(pack(plan, where, named, shards[:depth], lanes - t), plan, lanes - t) for t in range(1, lanes)]
            shards.extend(packs)
        parts.append(both)

    attended, query_grad, grads = [], [], []
    for g in range(groups):
        o, dq, columns, packs = attend(plan, where, named, queries, out_grad, *parts[g], g, qpk)
        attended.append(o)
        query_grad.append(dq)
        for column, far in zip(columns, packs):
            back = [row_shift(far[t - 1], plan, t) for t in range(1, lanes)]
            shards = merge(plan, where, named, column, back[::-1])
            total = shards[0]
            for k in range(1, depth):
                total = total + column_shift(shards[k], plan, depth - k).astype(jnp.float32)
            grads.append(total.astype(jnp.bfloat16))
    home = jnp.stack(
        [jnp.concatenate(grads[0::2], axis=1), jnp.concatenate(grads[1::2], axis=1)]
    )
    home = lax.all_to_all(home, "kvh", split_axis=1, concat_axis=2, tiled=True)
    return (
        jnp.concatenate(attended, axis=1),
        jnp.concatenate(query_grad, axis=1),
        home[0],
        home[1],
    )


def solution(mesh):
    split = P("ctx", "kvh")
    home = P(("ctx", "kvh"), None)
    return jax.shard_map(
        per_device,
        mesh=mesh,
        in_specs=(split, home, home, split, P()),
        out_specs=(split, split, home, home),
        check_vma=False,
    )
```

time: 962 us -> 337 us (0.35); the launches traced: 948 us -> 336 us
  matrix products: 363 us -> 0 us
  local copies, waits for them, and re-layouts: 231 us -> 18.4 us
  waiting for transfers between devices: 263 us -> 120 us
  Pallas kernels: 0 us -> 112 us
  starting transfers between devices: 3.6 us -> 58.9 us
  other arithmetic: 54.3 us -> 7.73 us
  between operations: 14.3 us -> 0.95 us
    dot_general x40 -> x0, matrix products: 325 us -> none  [the longest x8 111 us: attend_block(): jnp.einsum('gqbk,kgd->bgqd', score_grad, key_rows, preferred_element_type...]
    reduce_scatter x1 -> x0, waiting for transfers between devices: 148 us -> none  [per_device(): lax.psum_scatter(placed_rows.astype(jnp.bfloat16), 'ctx', scatter_dimensi...]
    all_gather x1 -> x0, waiting for transfers between devices: 114 us -> none  [per_device(): whole_kv = lax.all_gather(local_kv, 'ctx', axis=1, tiled=True)]
    pallas_call x0 -> x10, Pallas kernels: none -> 112 us  [the longest x2 78 us: attend(): pl.pallas_call(functools.partial(attend_kernel, plan=plan, qpk=qpk, per=4...]
    ppermute x0 -> x32, waiting for transfers between devices: none -> 111 us  [the longest x24 97.4 us: column_shift(): lax.ppermute(array, 'ctx', [(n, (n + rows * plan.lanes) % plan.ctx) for n...]
    ppermute x0 -> x32, starting transfers between devices: none -> 55.4 us  [the longest x24 47.9 us: column_shift(): lax.ppermute(array, 'ctx', [(n, (n + rows * plan.lanes) % plan.ctx) for n...]
    dynamic_update_slice x48 -> x0, local copies, waits for them, and re-layouts: 52.9 us -> none  [per_device(): lax.map(partial(attend_block, score_scale=HD ** (-0.5)), (query_rows, gra...]
    dynamic_slice x48 -> x0, local copies, waits for them, and re-layouts: 43.4 us -> none  [per_device(): lax.map(partial(attend_block, score_scale=HD ** (-0.5)), (query_rows, gra...]
  transfers between devices with their start and end apart: 3 -> 33, of which waited for: 2 -> 13; matrix products, arithmetic and copies ran while one was open for 3% -> 2% of each run, Pallas kernels for 0% -> 33%
where the time goes in v1:
time: 337 us; the launch traced here: 336 us
  waiting for transfers between devices  120 us (36%)
  Pallas kernels  112 us (33%)
  starting transfers between devices  58.9 us (17%)
  blocking collectives  18.5 us (5%)
  local copies, waits for them, and re-layouts  18.4 us (5%)
  other arithmetic  7.73 us (2%)
    ppermute x24, waiting for transfers between devices, column_shift(): lax.ppermute(array, 'ctx', [(n, (n + rows * plan.lanes) % plan.ctx) for n...  97.4 us
    pallas_call x2, Pallas kernels, attend(): pl.pallas_call(functools.partial(attend_kernel, plan=plan, qpk=qpk, per=4...  78 us
    ppermute x24, starting transfers between devices, column_shift(): lax.ppermute(array, 'ctx', [(n, (n + rows * plan.lanes) % plan.ctx) for n...  47.9 us
    all_to_all x1, blocking collectives, per_device(): lax.all_to_all(stacked, 'kvh', split_axis=2, concat_axis=1, tiled=True)  18.5 us
    pallas_call x4, Pallas kernels, merge(): pl.pallas_call(functools.partial(merge_kernel, plan=plan), grid_spec=pltp...  18 us
    pallas_call x4, Pallas kernels, pack(): pl.pallas_call(functools.partial(pack_kernel, plan=plan, step=step), grid...  16.1 us
    ppermute x8, waiting for transfers between devices, row_shift(): lax.ppermute(array, 'ctx', [(n, n - n % plan.lanes + (n + lanes) % plan.l...  13.6 us
    unnamed x67, local copies, waits for them, and re-layouts  10.9 us
  transfers between devices with their start and end apart: 33, of which 13 were waited for; matrix products, arithmetic and copies ran while one was open for 2% of the time, Pallas kernels for 33%

profile of v1, /device:TPU:0, one launch (start us, length us, event | category | flops | bytes accessed | tf_op | source)
XLA Modules:
  0.0 336.3 jit_solution(4967790443318040157)
XLA Ops:
  0.6 1.3 pad_maximum_fusion.2
  1.9 0.9 copy.24
  2.9 18.5 %all_to_all.33 = bf16[2,256,1024]{1,0,2:T(2,128)(2,1)S(1)} all-to-all(bf16[2,256,1024]{1,0,2:T(2,128)(2,1)S(1)} %copy.24), channel_id=1, replica_groups=mesh['ctx'=8,'kvh'=4] {'kvh'}, dimensions={2} | all-to-all | bytes 2097152 | tf_op jit(solution)/shard_map/all_to_all | solution.py:334
  22.4 1.6 collective-permute-start
  24.0 2.6 collective-permute-start.1
  26.6 1.3 collective-permute-start.2
  29.0 4.6 %collective-permute-done.refs_1_.refs_3_ = bf16[1024,128]{1,0:T(8,128)(2,1)S(1)} collective-permute-done((bf16[1024,128]{1,0:T(8,128)(2,1)S(1)}, bf16[1024,128]{1,0:T(8,128)(2,1)S(1)}, u32[]{:S(2)}, u32[]{:S(2)}) %collective-permute-start) | collective-permute-done | bytes 262176 | tf_op jit(solution)/shard_map/ppermute | solution.py:319
  33.6 2.4 collective-permute-start.6
  36.9 8.0 %collective-permute-done.1.refs_2_.refs_4_ = bf16[1024,128]{1,0:T(8,128)(2,1)S(1)} collective-permute-done((bf16[1024,128]{1,0:T(8,128)(2,1)S(1)}, bf16[1024,128]{1,0:T(8,128)(2,1)S(1)}, u32[]{:S(2)}, u32[]{:S(2)}) %collective-permute-start.1) | collective-permute-done | bytes 262176 | tf_op jit(solution)/shard_map/ppermute | solution.py:319
  45.7 4.0 %pack_blocks.4 = bf16[2816,128]{1,0:T(8,128)(2,1)} custom-call(s32[1]{0:T(128)} %bitcast.where, s32[192]{0:T(256)} %reshape.19.named, bf16[1024,128]{1,0:T(8,128)(2,1)} %copy-done.4, bf16[1024,128]{1,0:T(8,128)(2,1)} %copy-done.13, bf16[1024,128]{1,0:T(8,128)(2,1)} %copy-done.14, bf16[1024,128]{1,0:T(8,128)(2,1)} %copy-done.15), custom_call_target="tpu_custom_call" | custom-call | bytes 4194304 | tf_op jit(solution)/shard_map/pack_blocks/pallas_call | solution.py:136
  49.7 1.4 collective-permute-start.3
  51.1 14.8 %collective-permute-done.5.refs_2_.refs_9_ = bf16[1024,128]{1,0:T(8,128)(2,1)S(1)} collective-permute-done((bf16[1024,128]{1,0:T(8,128)(2,1)S(1)}, bf16[1024,128]{1,0:T(8,128)(2,1)S(1)}, u32[]{:S(2)}, u32[]{:S(2)}) %collective-permute-start.5) | collective-permute-done | bytes 262176 | tf_op jit(solution)/shard_map/ppermute | solution.py:319
  67.3 4.0 %pack_blocks.5 = bf16[2816,128]{1,0:T(8,128)(2,1)} custom-call(s32[1]{0:T(128)} %bitcast.where, s32[192]{0:T(256)} %reshape.19.named, bf16[1024,128]{1,0:T(8,128)(2,1)} %copy-done.3, bf16[1024,128]{1,0:T(8,128)(2,1)} %copy-done.16, bf16[1024,128]{1,0:T(8,128)(2,1)} %copy-done.17, bf16[1024,128]{1,0:T(8,128)(2,1)} %copy-done.18), custom_call_target="tpu_custom_call" | custom-call | bytes 4194304 | tf_op jit(solution)/shard_map/pack_blocks/pallas_call | solution.py:136
  71.3 1.4 collective-permute-start.7
  72.7 5.4 %collective-permute-start.12 = (bf16[1024,128]{1,0:T(8,128)(2,1)S(1)}, bf16[1024,128]{1,0:T(8,128)(2,1)S(1)}, u32[]{:S(2)}, u32[]{:S(2)}) collective-permute-start(bf16[1024,128]{1,0:T(8,128)(2,1)S(1)} %get-tuple-element.36.refs_0_.refs_7_), channel_id=1, source_target_pairs={{0,8},{4,12},{8,16},{12,20},{16,24},{20,28},{24,0},{28,4},{1,9},{5... | collective-permute-start | bytes 786440 | tf_op jit(solution)/shard_map/ppermute | solution.py:319
  78.1 2.3 collective-permute-start.13
  80.4 6.7 %collective-permute-done.12.refs_1_.refs_8_ = bf16[1024,128]{1,0:T(8,128)(2,1)S(1)} collective-permute-done((bf16[1024,128]{1,0:T(8,128)(2,1)S(1)}, bf16[1024,128]{1,0:T(8,128)(2,1)S(1)}, u32[]{:S(2)}, u32[]{:S(2)}) %collective-permute-start.12) | collective-permute-done | bytes 262176 | tf_op jit(solution)/shard_map/ppermute | solution.py:319
  87.1 8.8 %collective-permute-done.13.refs_2_.refs_9_ = bf16[1024,128]{1,0:T(8,128)(2,1)S(1)} collective-permute-done((bf16[1024,128]{1,0:T(8,128)(2,1)S(1)}, bf16[1024,128]{1,0:T(8,128)(2,1)S(1)}, u32[]{:S(2)}, u32[]{:S(2)}) %collective-permute-start.13) | collective-permute-done | bytes 262176 | tf_op jit(solution)/shard_map/ppermute | solution.py:319
  95.9 10.7 %collective-permute-start.8 = (bf16[1024,128]{1,0:T(8,128)(2,1)S(1)}, bf16[1024,128]{1,0:T(8,128)(2,1)S(1)}, u32[]{:S(2)}, u32[]{:S(2)}) collective-permute-start(bf16[1024,128]{1,0:T(8,128)(2,1)S(1)} %get-tuple-element.35.refs_0_.refs_2_), channel_id=1, source_target_pairs={{0,8},{4,12},{8,16},{12,20},{16,24},{20,28},{24,0},{28,4},{1,9},{5... | collective-permute-start | bytes 786440 | tf_op jit(solution)/shard_map/ppermute | solution.py:319
  106.7 3.4 %collective-permute-start.9 = (bf16[1024,128]{1,0:T(8,128)(2,1)S(1)}, bf16[1024,128]{1,0:T(8,128)(2,1)S(1)}, u32[]{:S(2)}, u32[]{:S(2)}) collective-permute-start(bf16[1024,128]{1,0:T(8,128)(2,1)S(1)} %get-tuple-element.35.refs_0_.refs_2_), channel_id=1, source_target_pairs={{0,16},{4,20},{8,24},{12,28},{16,0},{20,4},{24,8},{28,12},{1,17},{... | collective-permute-start | bytes 786440 | tf_op jit(solution)/shard_map/ppermute | solution.py:319
  110.1 4.0 %pack_blocks.7 = bf16[2816,128]{1,0:T(8,128)(2,1)} custom-call(s32[1]{0:T(128)} %bitcast.where, s32[192]{0:T(256)} %reshape.19.named, bf16[1024,128]{1,0:T(8,128)(2,1)} %copy-done.1, bf16[1024,128]{1,0:T(8,128)(2,1)} %copy-done.19, bf16[1024,128]{1,0:T(8,128)(2,1)} %copy-done.20, bf16[1024,128]{1,0:T(8,128)(2,1)} %copy-done.21), custom_call_target="tpu_custom_call" | custom-call | bytes 4194304 | tf_op jit(solution)/shard_map/pack_blocks/pallas_call | solution.py:136
  114.3 2.5 collective-permute-done.8.refs_1_.refs_3_
  116.8 9.2 %collective-permute-done.9.refs_2_.refs_4_ = bf16[1024,128]{1,0:T(8,128)(2,1)S(1)} collective-permute-done((bf16[1024,128]{1,0:T(8,128)(2,1)S(1)}, bf16[1024,128]{1,0:T(8,128)(2,1)S(1)}, u32[]{:S(2)}, u32[]{:S(2)}) %collective-permute-start.9) | collective-permute-done | bytes 262176 | tf_op jit(solution)/shard_map/ppermute | solution.py:319
  126.7 4.1 %pack_blocks.6 = bf16[2816,128]{1,0:T(8,128)(2,1)} custom-call(s32[1]{0:T(128)} %bitcast.where, s32[192]{0:T(256)} %reshape.19.named, bf16[1024,128]{1,0:T(8,128)(2,1)} %copy-done.2, bf16[1024,128]{1,0:T(8,128)(2,1)} %copy-done.23, bf16[1024,128]{1,0:T(8,128)(2,1)} %copy-done.24, bf16[1024,128]{1,0:T(8,128)(2,1)} %copy-done.22), custom_call_target="tpu_custom_call" | custom-call | bytes 4194304 | tf_op jit(solution)/shard_map/pack_blocks/pallas_call | solution.py:136
  132.9 39.0 %attend_head.2 = (bf16[1024,1024]{1,0:T(8,128)(2,1)}, bf16[1024,1024]{1,0:T(8,128)(2,1)}, f32[4096,128]{1,0:T(8,128)}, f32[4096,128]{1,0:T(8,128)}, bf16[2816,12...) custom-call(s32[1]{0:T(128)} %bitcast.where, s32[192]{0:T(256)} %reshape.19.named, bf16[1024,2048]{1,0:T(8,128)(2,1)} %refs_0_.3, ...), custom_call_target="tpu_custom_call" | custom-call | flops 12884901888 | bytes 25165824 | tf_op jit(solution)/shard_map/attend_head/pallas_call | solution.py:288
  172.0 1.8 collective-permute-start.16
  175.8 39.0 %attend_head.3 = (bf16[1024,1024]{1,0:T(8,128)(2,1)}, bf16[1024,1024]{1,0:T(8,128)(2,1)}, f32[4096,128]{1,0:T(8,128)}, f32[4096,128]{1,0:T(8,128)}, bf16[2816,12...) custom-call(s32[1]{0:T(128)} %bitcast.where, s32[192]{0:T(256)} %reshape.19.named, bf16[1024,2048]{1,0:T(8,128)(2,1)} %refs_0_.3, ...), custom_call_target="tpu_custom_call" | custom-call | flops 12884901888 | bytes 25165824 | tf_op jit(solution)/shard_map/attend_head/pallas_call | solution.py:288
  214.8 1.9 collective-permute-start.20
  217.8 4.5 %merge_terms.4 = (f32[1024,128]{1,0:T(8,128)}, bf16[1024,128]{1,0:T(8,128)(2,1)}, bf16[1024,128]{1,0:T(8,128)(2,1)}, bf16[1024,128]{1,0:T(8,128)(2,1)}) custom-call(s32[1]{0:T(128)} %bitcast.where, s32[192]{0:T(256)} %reshape.19.named, f32[4096,128]{1,0:T(8,128)} %get-tuple-element.40.column, bf16[2816,128]{1,0:T(8,128)(2,1)} %copy-done.8), custom_call_target="tpu_custom_call" | custom-call | bytes 6291456 | tf_op jit(solution)/shard_map/merge_terms/pallas_call | solution.py:171
  222.3 2.1 collective-permute-start.19
  224.3 4.6 %merge_terms.6 = (f32[1024,128]{1,0:T(8,128)}, bf16[1024,128]{1,0:T(8,128)(2,1)}, bf16[1024,128]{1,0:T(8,128)(2,1)}, bf16[1024,128]{1,0:T(8,128)(2,1)}) custom-call(s32[1]{0:T(128)} %bitcast.where, s32[192]{0:T(256)} %reshape.19.named, f32[4096,128]{1,0:T(8,128)} %get-tuple-element.52.column, bf16[2816,128]{1,0:T(8,128)(2,1)} %copy-done.5), custom_call_target="tpu_custom_call" | custom-call | bytes 6291456 | tf_op jit(solution)/shard_map/merge_terms/pallas_call | solution.py:171
  228.9 5.2 %collective-permute-done.20.refs_0_ = bf16[2816,128]{1,0:T(8,128)(2,1)S(1)} collective-permute-done((bf16[2816,128]{1,0:T(8,128)(2,1)}, bf16[2816,128]{1,0:T(8,128)(2,1)S(1)}, u32[]{:S(2)}, u32[]{:S(2)}) %collective-permute-start.20) | collective-permute-done | bytes 720928 | tf_op jit(solution)/shard_map/ppermute | solution.py:323
  235.0 4.5 %merge_terms.5 = (f32[1024,128]{1,0:T(8,128)}, bf16[1024,128]{1,0:T(8,128)(2,1)}, bf16[1024,128]{1,0:T(8,128)(2,1)}, bf16[1024,128]{1,0:T(8,128)(2,1)}) custom-call(s32[1]{0:T(128)} %bitcast.where, s32[192]{0:T(256)} %reshape.19.named, f32[4096,128]{1,0:T(8,128)} %get-tuple-element.46.column, bf16[2816,128]{1,0:T(8,128)(2,1)} %copy-done.7), custom_call_target="tpu_custom_call" | custom-call | bytes 6291456 | tf_op jit(solution)/shard_map/merge_terms/pallas_call | solution.py:171
  239.5 8.3 %collective-permute-done.28.refs_0_ = bf16[2816,128]{1,0:T(8,128)(2,1)S(1)} collective-permute-done((bf16[2816,128]{1,0:T(8,128)(2,1)}, bf16[2816,128]{1,0:T(8,128)(2,1)S(1)}, u32[]{:S(2)}, u32[]{:S(2)}) %collective-permute-start.28) | collective-permute-done | bytes 720928 | tf_op jit(solution)/shard_map/ppermute | solution.py:323
  248.7 4.4 %merge_terms.7 = (f32[1024,128]{1,0:T(8,128)}, bf16[1024,128]{1,0:T(8,128)(2,1)}, bf16[1024,128]{1,0:T(8,128)(2,1)}, bf16[1024,128]{1,0:T(8,128)(2,1)}) custom-call(s32[1]{0:T(128)} %bitcast.where, s32[192]{0:T(256)} %reshape.19.named, f32[4096,128]{1,0:T(8,128)} %get-tuple-element.58.column, bf16[2816,128]{1,0:T(8,128)(2,1)} %copy-done.6), custom_call_target="tpu_custom_call" | custom-call | bytes 6291456 | tf_op jit(solution)/shard_map/merge_terms/pallas_call | solution.py:171
  253.3 3.8 %collective-permute-start.21 = (bf16[1024,128]{1,0:T(8,128)(2,1)}, bf16[1024,128]{1,0:T(8,128)(2,1)S(1)}, u32[]{:S(2)}, u32[]{:S(2)}) collective-permute-start(bf16[1024,128]{1,0:T(8,128)(2,1)} %get-tuple-element.49), channel_id=1, source_target_pairs={{0,24},{4,28},{8,0},{12,4},{16,8},{20,12},{24,16},{28,20},{1,25},{... | collective-permute-start | bytes 786440 | tf_op jit(solution)/shard_map/ppermute | solution.py:319
  257.1 1.8 collective-permute-start.22
  259.0 3.1 collective-permute-start.23
  262.1 17.6 %collective-permute-done.26 = bf16[1024,128]{1,0:T(8,128)(2,1)S(1)} collective-permute-done((bf16[1024,128]{1,0:T(8,128)(2,1)}, bf16[1024,128]{1,0:T(8,128)(2,1)S(1)}, u32[]{:S(2)}, u32[]{:S(2)}) %collective-permute-start.26) | collective-permute-done | bytes 262176 | tf_op jit(solution)/shard_map/ppermute | solution.py:319
  279.8 4.4 %collective-permute-start.30 = (bf16[1024,128]{1,0:T(8,128)(2,1)}, bf16[1024,128]{1,0:T(8,128)(2,1)S(1)}, u32[]{:S(2)}, u32[]{:S(2)}) collective-permute-start(bf16[1024,128]{1,0:T(8,128)(2,1)} %get-tuple-element.62), channel_id=1, source_target_pairs={{0,16},{4,20},{8,24},{12,28},{16,0},{20,4},{24,8},{28,12},{1,17},{... | collective-permute-start | bytes 786440 | tf_op jit(solution)/shard_map/ppermute | solution.py:319
  284.3 1.7 collective-permute-start.31
  286.0 16.3 %collective-permute-done.22 = bf16[1024,128]{1,0:T(8,128)(2,1)S(1)} collective-permute-done((bf16[1024,128]{1,0:T(8,128)(2,1)}, bf16[1024,128]{1,0:T(8,128)(2,1)S(1)}, u32[]{:S(2)}, u32[]{:S(2)}) %collective-permute-start.22) | collective-permute-done | bytes 262176 | tf_op jit(solution)/shard_map/ppermute | solution.py:319
  302.5 8.9 %collective-permute-done.30 = bf16[1024,128]{1,0:T(8,128)(2,1)S(1)} collective-permute-done((bf16[1024,128]{1,0:T(8,128)(2,1)}, bf16[1024,128]{1,0:T(8,128)(2,1)S(1)}, u32[]{:S(2)}, u32[]{:S(2)}) %collective-permute-start.30) | collective-permute-done | bytes 262176 | tf_op jit(solution)/shard_map/ppermute | solution.py:319
  311.7 2.0 copy.26
  313.7 3.5 %all-to-all-start.1 = ((bf16[2,1024,256]{2,0,1:T(2,128)(2,1)}), bf16[2,1024,256]{2,0,1:T(2,128)(2,1)S(1)}, u32[]{:S(2)}, u32[]{:S(2)}) async-start(bf16[2,1024,256]{2,0,1:T(2,128)(2,1)} %copy.26), calls=%async_computation.1 | async-start | bytes 2097152 | tf_op jit(solution)/shard_map/all_to_all | solution.py:373
  317.2 5.7 %pad_maximum_fusion = (bf16[1024,2048]{1,0:T(8,128)(2,1)}, bf16[1024,2048]{1,0:T(8,128)(2,1)}) fusion(bf16[1024,1024]{1,0:T(8,128)(2,1)} %get-tuple-element.37, bf16[1024,1024]{1,0:T(8,128)(2,1)S(1)} %copy-done, bf16[1024,1024]{1,0:T(8,128)(2,1)} %get-tuple-element.39, bf16[1024,1024]{1,0:T(8,128)(2,1)} %get-tuple-element.38), kind=kLoop, calls=%fused_computation | loop fusion | flops 16777216 | bytes 16777216 | tf_op jit(solution)/shard_map/concatenate | solution.py:375
  323.0 8.7 %all-to-all-done.1 = bf16[2,1024,256]{2,0,1:T(2,128)(2,1)S(1)} async-done(((bf16[2,1024,256]{2,0,1:T(2,128)(2,1)}), bf16[2,1024,256]{2,0,1:T(2,128)(2,1)S(1)}, u32[]{:S(2)}, u32[]{:S(2)}) %all-to-all-start.1) | async-done | bytes 1048608 | tf_op jit(solution)/shard_map/all_to_all | solution.py:373
  331.7 1.5 fusion
  (113 shorter events, 16.9 us)
Async XLA Ops:
  1.9 34.1 %copy-start.25 = (s32[64,3]{0,1:T(4,128)S(1)}, s32[64,3]{0,1:T(4,128)}, u32[]{:S(2)}) copy-start(s32[64,3]{0,1:T(4,128)} %param.9) | copy-start | bytes 2308
  22.3 22.6 %copy-start.4 = (bf16[1024,128]{1,0:T(8,128)(2,1)}, bf16[1024,128]{1,0:T(8,128)(2,1)S(1)}, u32[]{:S(2)}) copy-start(bf16[1024,128]{1,0:T(8,128)(2,1)S(1)} %get-tuple-element.69.refs_0_.refs_2_) | copy-start | bytes 786436
  22.3 43.5 %copy-start.3 = (bf16[1024,128]{1,0:T(8,128)(2,1)}, bf16[1024,128]{1,0:T(8,128)(2,1)S(1)}, u32[]{:S(2)}) copy-start(bf16[1024,128]{1,0:T(8,128)(2,1)S(1)} %get-tuple-element.68.refs_0_.refs_7_) | copy-start | bytes 786436
  22.4 87.7 %copy-start.1 = (bf16[1024,128]{1,0:T(8,128)(2,1)}, bf16[1024,128]{1,0:T(8,128)(2,1)S(1)}, u32[]{:S(2)}) copy-start(bf16[1024,128]{1,0:T(8,128)(2,1)S(1)} %get-tuple-element.36.refs_0_.refs_7_) | copy-start | bytes 786436
  22.4 103.6 %copy-start.2 = (bf16[1024,128]{1,0:T(8,128)(2,1)}, bf16[1024,128]{1,0:T(8,128)(2,1)S(1)}, u32[]{:S(2)}) copy-start(bf16[1024,128]{1,0:T(8,128)(2,1)S(1)} %get-tuple-element.35.refs_0_.refs_2_) | copy-start | bytes 786436
  22.4 11.2 %collective-permute-start = (bf16[1024,128]{1,0:T(8,128)(2,1)S(1)}, bf16[1024,128]{1,0:T(8,128)(2,1)S(1)}, u32[]{:S(2)}, u32[]{:S(2)}) collective-permute-start(bf16[1024,128]{1,0:T(8,128)(2,1)S(1)} %get-tuple-element.69.refs_0_.refs_2_), channel_id=1, source_target_pairs={{0,8},{4,12},{8,16},{12,20},{16,24},{20,28},{24,0},{28,4},{1,9},{5... | collective-permute-start | bytes 786440 | tf_op jit(solution)/shard_map/ppermute | solution.py:319
  24.0 20.9 %collective-permute-start.1 = (bf16[1024,128]{1,0:T(8,128)(2,1)S(1)}, bf16[1024,128]{1,0:T(8,128)(2,1)S(1)}, u32[]{:S(2)}, u32[]{:S(2)}) collective-permute-start(bf16[1024,128]{1,0:T(8,128)(2,1)S(1)} %get-tuple-element.69.refs_0_.refs_2_), channel_id=1, source_target_pairs={{0,16},{4,20},{8,24},{12,28},{16,0},{20,4},{24,8},{28,12},{1,17},{... | collective-permute-start | bytes 786440 | tf_op jit(solution)/shard_map/ppermute | solution.py:319
  26.6 18.3 %collective-permute-start.2 = (bf16[1024,128]{1,0:T(8,128)(2,1)S(1)}, bf16[1024,128]{1,0:T(8,128)(2,1)S(1)}, u32[]{:S(2)}, u32[]{:S(2)}) collective-permute-start(bf16[1024,128]{1,0:T(8,128)(2,1)S(1)} %get-tuple-element.69.refs_0_.refs_2_), channel_id=1, source_target_pairs={{0,24},{4,28},{8,0},{12,4},{16,8},{20,12},{24,16},{28,20},{1,25},{... | collective-permute-start | bytes 786440 | tf_op jit(solution)/shard_map/ppermute | solution.py:319
  27.9 23.1 %collective-permute-start.4 = (bf16[1024,128]{1,0:T(8,128)(2,1)S(1)}, bf16[1024,128]{1,0:T(8,128)(2,1)S(1)}, u32[]{:S(2)}, u32[]{:S(2)}) collective-permute-start(bf16[1024,128]{1,0:T(8,128)(2,1)S(1)} %get-tuple-element.68.refs_0_.refs_7_), channel_id=1, source_target_pairs={{0,8},{4,12},{8,16},{12,20},{16,24},{20,28},{24,0},{28,4},{1,9},{5... | collective-permute-start | bytes 786440 | tf_op jit(solution)/shard_map/ppermute | solution.py:319
  28.6 37.2 %collective-permute-start.5 = (bf16[1024,128]{1,0:T(8,128)(2,1)S(1)}, bf16[1024,128]{1,0:T(8,128)(2,1)S(1)}, u32[]{:S(2)}, u32[]{:S(2)}) collective-permute-start(bf16[1024,128]{1,0:T(8,128)(2,1)S(1)} %get-tuple-element.68.refs_0_.refs_7_), channel_id=1, source_target_pairs={{0,16},{4,20},{8,24},{12,28},{16,0},{20,4},{24,8},{28,12},{1,17},{... | collective-permute-start | bytes 786440 | tf_op jit(solution)/shard_map/ppermute | solution.py:319
  33.6 32.3 %collective-permute-start.6 = (bf16[1024,128]{1,0:T(8,128)(2,1)S(1)}, bf16[1024,128]{1,0:T(8,128)(2,1)S(1)}, u32[]{:S(2)}, u32[]{:S(2)}) collective-permute-start(bf16[1024,128]{1,0:T(8,128)(2,1)S(1)} %get-tuple-element.68.refs_0_.refs_7_), channel_id=1, source_target_pairs={{0,24},{4,28},{8,0},{12,4},{16,8},{20,12},{24,16},{28,20},{1,25},{... | collective-permute-start | bytes 786440 | tf_op jit(solution)/shard_map/ppermute | solution.py:319
  49.7 81.4 %collective-permute-start.3 = (bf16[2816,128]{1,0:T(8,128)(2,1)}, bf16[2816,128]{1,0:T(8,128)(2,1)S(1)}, u32[]{:S(2)}, u32[]{:S(2)}) collective-permute-start(bf16[2816,128]{1,0:T(8,128)(2,1)} %pack_blocks.4), channel_id=1, source_target_pairs={{0,4},{4,0},{8,12},{12,8},{16,20},{20,16},{24,28},{28,24},{1,5},{5... | collective-permute-start | bytes 2162696 | tf_op jit(solution)/shard_map/ppermute | solution.py:323
  51.1 14.8 %copy-start.16 = (bf16[1024,128]{1,0:T(8,128)(2,1)}, bf16[1024,128]{1,0:T(8,128)(2,1)S(1)}, u32[]{:S(2)}) copy-start(bf16[1024,128]{1,0:T(8,128)(2,1)S(1)} %collective-permute-done.4.refs_1_.refs_8_) | copy-start | bytes 786436
  71.3 59.9 %collective-permute-start.7 = (bf16[2816,128]{1,0:T(8,128)(2,1)}, bf16[2816,128]{1,0:T(8,128)(2,1)S(1)}, u32[]{:S(2)}, u32[]{:S(2)}) collective-permute-start(bf16[2816,128]{1,0:T(8,128)(2,1)} %pack_blocks.5), channel_id=1, source_target_pairs={{0,4},{4,0},{8,12},{12,8},{16,20},{20,16},{24,28},{28,24},{1,5},{5... | collective-permute-start | bytes 2162696 | tf_op jit(solution)/shard_map/ppermute | solution.py:323
  72.7 14.5 %collective-permute-start.12 = (bf16[1024,128]{1,0:T(8,128)(2,1)S(1)}, bf16[1024,128]{1,0:T(8,128)(2,1)S(1)}, u32[]{:S(2)}, u32[]{:S(2)}) collective-permute-start(bf16[1024,128]{1,0:T(8,128)(2,1)S(1)} %get-tuple-element.36.refs_0_.refs_7_), channel_id=1, source_target_pairs={{0,8},{4,12},{8,16},{12,20},{16,24},{20,28},{24,0},{28,4},{1,9},{5... | collective-permute-start | bytes 786440 | tf_op jit(solution)/shard_map/ppermute | solution.py:319
  78.1 17.8 %collective-permute-start.13 = (bf16[1024,128]{1,0:T(8,128)(2,1)S(1)}, bf16[1024,128]{1,0:T(8,128)(2,1)S(1)}, u32[]{:S(2)}, u32[]{:S(2)}) collective-permute-start(bf16[1024,128]{1,0:T(8,128)(2,1)S(1)} %get-tuple-element.36.refs_0_.refs_7_), channel_id=1, source_target_pairs={{0,16},{4,20},{8,24},{12,28},{16,0},{20,4},{24,8},{28,12},{1,17},{... | collective-permute-start | bytes 786440 | tf_op jit(solution)/shard_map/ppermute | solution.py:319
  80.4 26.3 %collective-permute-start.14 = (bf16[1024,128]{1,0:T(8,128)(2,1)S(1)}, bf16[1024,128]{1,0:T(8,128)(2,1)S(1)}, u32[]{:S(2)}, u32[]{:S(2)}) collective-permute-start(bf16[1024,128]{1,0:T(8,128)(2,1)S(1)} %get-tuple-element.36.refs_0_.refs_7_), channel_id=1, source_target_pairs={{0,24},{4,28},{8,0},{12,4},{16,8},{20,12},{24,16},{28,20},{1,25},{... | collective-permute-start | bytes 786440 | tf_op jit(solution)/shard_map/ppermute | solution.py:319
  87.1 22.9 %copy-start.19 = (bf16[1024,128]{1,0:T(8,128)(2,1)}, bf16[1024,128]{1,0:T(8,128)(2,1)S(1)}, u32[]{:S(2)}) copy-start(bf16[1024,128]{1,0:T(8,128)(2,1)S(1)} %collective-permute-done.12.refs_1_.refs_8_) | copy-start | bytes 786436
  87.1 26.9 %collective-permute-start.10 = (bf16[1024,128]{1,0:T(8,128)(2,1)S(1)}, bf16[1024,128]{1,0:T(8,128)(2,1)S(1)}, u32[]{:S(2)}, u32[]{:S(2)}) collective-permute-start(bf16[1024,128]{1,0:T(8,128)(2,1)S(1)} %get-tuple-element.35.refs_0_.refs_2_), channel_id=1, source_target_pairs={{0,24},{4,28},{8,0},{12,4},{16,8},{20,12},{24,16},{28,20},{1,25},{... | collective-permute-start | bytes 786440 | tf_op jit(solution)/shard_map/ppermute | solution.py:319
  95.9 14.1 %copy-start.20 = (bf16[1024,128]{1,0:T(8,128)(2,1)}, bf16[1024,128]{1,0:T(8,128)(2,1)S(1)}, u32[]{:S(2)}) copy-start(bf16[1024,128]{1,0:T(8,128)(2,1)S(1)} %collective-permute-done.13.refs_2_.refs_9_) | copy-start | bytes 786436
  95.9 20.9 %collective-permute-start.8 = (bf16[1024,128]{1,0:T(8,128)(2,1)S(1)}, bf16[1024,128]{1,0:T(8,128)(2,1)S(1)}, u32[]{:S(2)}, u32[]{:S(2)}) collective-permute-start(bf16[1024,128]{1,0:T(8,128)(2,1)S(1)} %get-tuple-element.35.refs_0_.refs_2_), channel_id=1, source_target_pairs={{0,8},{4,12},{8,16},{12,20},{16,24},{20,28},{24,0},{28,4},{1,9},{5... | collective-permute-start | bytes 786440 | tf_op jit(solution)/shard_map/ppermute | solution.py:319
  106.7 19.3 %collective-permute-start.9 = (bf16[1024,128]{1,0:T(8,128)(2,1)S(1)}, bf16[1024,128]{1,0:T(8,128)(2,1)S(1)}, u32[]{:S(2)}, u32[]{:S(2)}) collective-permute-start(bf16[1024,128]{1,0:T(8,128)(2,1)S(1)} %get-tuple-element.35.refs_0_.refs_2_), channel_id=1, source_target_pairs={{0,16},{4,20},{8,24},{12,28},{16,0},{20,4},{24,8},{28,12},{1,17},{... | collective-permute-start | bytes 786440 | tf_op jit(solution)/shard_map/ppermute | solution.py:319
  114.0 12.0 %copy-start.22 = (bf16[1024,128]{1,0:T(8,128)(2,1)}, bf16[1024,128]{1,0:T(8,128)(2,1)S(1)}, u32[]{:S(2)}) copy-start(bf16[1024,128]{1,0:T(8,128)(2,1)S(1)} %collective-permute-done.10.refs_3_.refs_5_) | copy-start | bytes 786436
  114.0 60.0 %collective-permute-start.15 = (bf16[2816,128]{1,0:T(8,128)(2,1)}, bf16[2816,128]{1,0:T(8,128)(2,1)S(1)}, u32[]{:S(2)}, u32[]{:S(2)}) collective-permute-start(bf16[2816,128]{1,0:T(8,128)(2,1)} %pack_blocks.7), channel_id=1, source_target_pairs={{0,4},{4,0},{8,12},{12,8},{16,20},{20,16},{24,28},{28,24},{1,5},{5... | collective-permute-start | bytes 2162696 | tf_op jit(solution)/shard_map/ppermute | solution.py:323
  130.8 43.2 %collective-permute-start.11 = (bf16[2816,128]{1,0:T(8,128)(2,1)}, bf16[2816,128]{1,0:T(8,128)(2,1)S(1)}, u32[]{:S(2)}, u32[]{:S(2)}) collective-permute-start(bf16[2816,128]{1,0:T(8,128)(2,1)} %pack_blocks.6), channel_id=1, source_target_pairs={{0,4},{4,0},{8,12},{12,8},{16,20},{20,16},{24,28},{28,24},{1,5},{5... | collective-permute-start | bytes 2162696 | tf_op jit(solution)/shard_map/ppermute | solution.py:323
  172.0 45.0 %collective-permute-start.16 = (bf16[2816,128]{1,0:T(8,128)(2,1)}, bf16[2816,128]{1,0:T(8,128)(2,1)S(1)}, u32[]{:S(2)}, u32[]{:S(2)}) collective-permute-start(bf16[2816,128]{1,0:T(8,128)(2,1)} %get-tuple-element.41), channel_id=1, source_target_pairs={{0,4},{4,0},{8,12},{12,8},{16,20},{20,16},{24,28},{28,24},{1,5},{5... | collective-permute-start | bytes 2162696 | tf_op jit(solution)/shard_map/ppermute | solution.py:323
  173.8 48.5 %collective-permute-start.24 = (bf16[2816,128]{1,0:T(8,128)(2,1)}, bf16[2816,128]{1,0:T(8,128)(2,1)S(1)}, u32[]{:S(2)}, u32[]{:S(2)}) collective-permute-start(bf16[2816,128]{1,0:T(8,128)(2,1)} %get-tuple-element.53), channel_id=1, source_target_pairs={{0,4},{4,0},{8,12},{12,8},{16,20},{20,16},{24,28},{28,24},{1,5},{5... | collective-permute-start | bytes 2162696 | tf_op jit(solution)/shard_map/ppermute | solution.py:323
  214.8 19.4 %collective-permute-start.20 = (bf16[2816,128]{1,0:T(8,128)(2,1)}, bf16[2816,128]{1,0:T(8,128)(2,1)S(1)}, u32[]{:S(2)}, u32[]{:S(2)}) collective-permute-start(bf16[2816,128]{1,0:T(8,128)(2,1)} %get-tuple-element.47), channel_id=1, source_target_pairs={{0,4},{4,0},{8,12},{12,8},{16,20},{20,16},{24,28},{28,24},{1,5},{5... | collective-permute-start | bytes 2162696 | tf_op jit(solution)/shard_map/ppermute | solution.py:323
  216.7 31.2 %collective-permute-start.28 = (bf16[2816,128]{1,0:T(8,128)(2,1)}, bf16[2816,128]{1,0:T(8,128)(2,1)S(1)}, u32[]{:S(2)}, u32[]{:S(2)}) collective-permute-start(bf16[2816,128]{1,0:T(8,128)(2,1)} %get-tuple-element.59), channel_id=1, source_target_pairs={{0,4},{4,0},{8,12},{12,8},{16,20},{20,16},{24,28},{28,24},{1,5},{5... | collective-permute-start | bytes 2162696 | tf_op jit(solution)/shard_map/ppermute | solution.py:323
  222.2 30.9 %collective-permute-start.17 = (bf16[1024,128]{1,0:T(8,128)(2,1)}, bf16[1024,128]{1,0:T(8,128)(2,1)S(1)}, u32[]{:S(2)}, u32[]{:S(2)}) collective-permute-start(bf16[1024,128]{1,0:T(8,128)(2,1)} %get-tuple-element.43), channel_id=1, source_target_pairs={{0,24},{4,28},{8,0},{12,4},{16,8},{20,12},{24,16},{28,20},{1,25},{... | collective-permute-start | bytes 786440 | tf_op jit(solution)/shard_map/ppermute | solution.py:319
  222.3 31.0 %collective-permute-start.18 = (bf16[1024,128]{1,0:T(8,128)(2,1)}, bf16[1024,128]{1,0:T(8,128)(2,1)S(1)}, u32[]{:S(2)}, u32[]{:S(2)}) collective-permute-start(bf16[1024,128]{1,0:T(8,128)(2,1)} %get-tuple-element.44), channel_id=1, source_target_pairs={{0,16},{4,20},{8,24},{12,28},{16,0},{20,4},{24,8},{28,12},{1,17},{... | collective-permute-start | bytes 786440 | tf_op jit(solution)/shard_map/ppermute | solution.py:319
  222.3 34.8 %collective-permute-start.19 = (bf16[1024,128]{1,0:T(8,128)(2,1)}, bf16[1024,128]{1,0:T(8,128)(2,1)S(1)}, u32[]{:S(2)}, u32[]{:S(2)}) collective-permute-start(bf16[1024,128]{1,0:T(8,128)(2,1)} %get-tuple-element.45), channel_id=1, source_target_pairs={{0,8},{4,12},{8,16},{12,20},{16,24},{20,28},{24,0},{28,4},{1,9},{5... | collective-permute-start | bytes 786440 | tf_op jit(solution)/shard_map/ppermute | solution.py:319
  224.3 34.5 %copy-start.12 = (f32[1024,128]{1,0:T(8,128)S(1)}, f32[1024,128]{1,0:T(8,128)}, u32[]{:S(2)}) copy-start(f32[1024,128]{1,0:T(8,128)} %get-tuple-element.42) | copy-start | bytes 1572868
  228.9 24.3 %copy-start.31 = (bf16[1024,128]{1,0:T(8,128)(2,1)S(1)}, bf16[1024,128]{1,0:T(8,128)(2,1)}, u32[]{:S(2)}) copy-start(bf16[1024,128]{1,0:T(8,128)(2,1)} %get-tuple-element.57) | copy-start | bytes 786436
  228.9 55.3 %copy-start.11 = (f32[1024,128]{1,0:T(8,128)S(1)}, f32[1024,128]{1,0:T(8,128)}, u32[]{:S(2)}) copy-start(f32[1024,128]{1,0:T(8,128)} %get-tuple-element.54) | copy-start | bytes 1572868
  234.2 24.8 %collective-permute-start.25 = (bf16[1024,128]{1,0:T(8,128)(2,1)}, bf16[1024,128]{1,0:T(8,128)(2,1)S(1)}, u32[]{:S(2)}, u32[]{:S(2)}) collective-permute-start(bf16[1024,128]{1,0:T(8,128)(2,1)} %get-tuple-element.55), channel_id=1, source_target_pairs={{0,24},{4,28},{8,0},{12,4},{16,8},{20,12},{24,16},{28,20},{1,25},{... | collective-permute-start | bytes 786440 | tf_op jit(solution)/shard_map/ppermute | solution.py:319
  239.5 19.4 %copy-start.30 = (bf16[1024,128]{1,0:T(8,128)(2,1)S(1)}, bf16[1024,128]{1,0:T(8,128)(2,1)}, u32[]{:S(2)}) copy-start(bf16[1024,128]{1,0:T(8,128)(2,1)} %get-tuple-element.51) | copy-start | bytes 786436
  239.5 62.7 %copy-start.10 = (f32[1024,128]{1,0:T(8,128)S(1)}, f32[1024,128]{1,0:T(8,128)}, u32[]{:S(2)}) copy-start(f32[1024,128]{1,0:T(8,128)} %get-tuple-element.48) | copy-start | bytes 1572868
  247.9 31.9 %collective-permute-start.26 = (bf16[1024,128]{1,0:T(8,128)(2,1)}, bf16[1024,128]{1,0:T(8,128)(2,1)S(1)}, u32[]{:S(2)}, u32[]{:S(2)}) collective-permute-start(bf16[1024,128]{1,0:T(8,128)(2,1)} %get-tuple-element.56), channel_id=1, source_target_pairs={{0,16},{4,20},{8,24},{12,28},{16,0},{20,4},{24,8},{28,12},{1,17},{... | collective-permute-start | bytes 786440 | tf_op jit(solution)/shard_map/ppermute | solution.py:319
  253.2 58.2 %copy-start.9 = (f32[1024,128]{1,0:T(8,128)S(1)}, f32[1024,128]{1,0:T(8,128)}, u32[]{:S(2)}) copy-start(f32[1024,128]{1,0:T(8,128)} %get-tuple-element.60) | copy-start | bytes 1572868
  253.2 26.6 %collective-permute-start.27 = (bf16[1024,128]{1,0:T(8,128)(2,1)S(1)}, bf16[1024,128]{1,0:T(8,128)(2,1)S(1)}, u32[]{:S(2)}, u32[]{:S(2)}) collective-permute-start(bf16[1024,128]{1,0:T(8,128)(2,1)S(1)} %copy-done.31), channel_id=1, source_target_pairs={{0,8},{4,12},{8,16},{12,20},{16,24},{20,28},{24,0},{28,4},{1,9},{5... | collective-permute-start | bytes 786440 | tf_op jit(solution)/shard_map/ppermute | solution.py:319
  253.3 31.0 %collective-permute-start.21 = (bf16[1024,128]{1,0:T(8,128)(2,1)}, bf16[1024,128]{1,0:T(8,128)(2,1)S(1)}, u32[]{:S(2)}, u32[]{:S(2)}) collective-permute-start(bf16[1024,128]{1,0:T(8,128)(2,1)} %get-tuple-element.49), channel_id=1, source_target_pairs={{0,24},{4,28},{8,0},{12,4},{16,8},{20,12},{24,16},{28,20},{1,25},{... | collective-permute-start | bytes 786440 | tf_op jit(solution)/shard_map/ppermute | solution.py:319
  257.1 45.2 %collective-permute-start.22 = (bf16[1024,128]{1,0:T(8,128)(2,1)}, bf16[1024,128]{1,0:T(8,128)(2,1)S(1)}, u32[]{:S(2)}, u32[]{:S(2)}) collective-permute-start(bf16[1024,128]{1,0:T(8,128)(2,1)} %get-tuple-element.50), channel_id=1, source_target_pairs={{0,16},{4,20},{8,24},{12,28},{16,0},{20,4},{24,8},{28,12},{1,17},{... | collective-permute-start | bytes 786440 | tf_op jit(solution)/shard_map/ppermute | solution.py:319
  259.0 43.3 %collective-permute-start.23 = (bf16[1024,128]{1,0:T(8,128)(2,1)S(1)}, bf16[1024,128]{1,0:T(8,128)(2,1)S(1)}, u32[]{:S(2)}, u32[]{:S(2)}) collective-permute-start(bf16[1024,128]{1,0:T(8,128)(2,1)S(1)} %copy-done.30), channel_id=1, source_target_pairs={{0,8},{4,12},{8,16},{12,20},{16,24},{20,28},{24,0},{28,4},{1,9},{5... | collective-permute-start | bytes 786440 | tf_op jit(solution)/shard_map/ppermute | solution.py:319
  279.8 22.7 %collective-permute-start.29 = (bf16[1024,128]{1,0:T(8,128)(2,1)}, bf16[1024,128]{1,0:T(8,128)(2,1)S(1)}, u32[]{:S(2)}, u32[]{:S(2)}) collective-permute-start(bf16[1024,128]{1,0:T(8,128)(2,1)} %get-tuple-element.61), channel_id=1, source_target_pairs={{0,24},{4,28},{8,0},{12,4},{16,8},{20,12},{24,16},{28,20},{1,25},{... | collective-permute-start | bytes 786440 | tf_op jit(solution)/shard_map/ppermute | solution.py:319
  279.8 31.6 %collective-permute-start.30 = (bf16[1024,128]{1,0:T(8,128)(2,1)}, bf16[1024,128]{1,0:T(8,128)(2,1)S(1)}, u32[]{:S(2)}, u32[]{:S(2)}) collective-permute-start(bf16[1024,128]{1,0:T(8,128)(2,1)} %get-tuple-element.62), channel_id=1, source_target_pairs={{0,16},{4,20},{8,24},{12,28},{16,0},{20,4},{24,8},{28,12},{1,17},{... | collective-permute-start | bytes 786440 | tf_op jit(solution)/shard_map/ppermute | solution.py:319
  284.3 27.0 %collective-permute-start.31 = (bf16[1024,128]{1,0:T(8,128)(2,1)}, bf16[1024,128]{1,0:T(8,128)(2,1)S(1)}, u32[]{:S(2)}, u32[]{:S(2)}) collective-permute-start(bf16[1024,128]{1,0:T(8,128)(2,1)} %get-tuple-element.63), channel_id=1, source_target_pairs={{0,8},{4,12},{8,16},{12,20},{16,24},{20,28},{24,0},{28,4},{1,9},{5... | collective-permute-start | bytes 786440 | tf_op jit(solution)/shard_map/ppermute | solution.py:319
  313.7 18.0 %all-to-all-start.1 = ((bf16[2,1024,256]{2,0,1:T(2,128)(2,1)}), bf16[2,1024,256]{2,0,1:T(2,128)(2,1)S(1)}, u32[]{:S(2)}, u32[]{:S(2)}) async-start(bf16[2,1024,256]{2,0,1:T(2,128)(2,1)} %copy.26), calls=%async_computation.1 | async-start | bytes 2097152 | tf_op jit(solution)/shard_map/all_to_all | solution.py:373
  (17 other events, 41.6 us)

commit v2 on v1

v2 whole, which is shorter than its diff:
```python
import functools

import jax
import jax.numpy as jnp
from jax import lax
from jax.experimental import pallas as pl
from jax.experimental.pallas import tpu as pltpu
from jax.sharding import PartitionSpec as P

HD = 128
BLK = 128
GLOB = 2
DEPTH = 4
LOG2E = 1.4426950408889634
NN = (((1,), (0,)), ((), ()))
NT = (((1,), (1,)), ((), ()))
VMEM_LIMIT = 56 * 1024 * 1024
SMALL_VMEM = 16 * 1024 * 1024
COST = pl.CostEstimate(flops=0, bytes_accessed=1 << 10, transcendentals=0)


class Plan:
    def __init__(self, ctx, query_blocks, rand):
        self.ctx, self.qb, self.rand = ctx, query_blocks, rand
        self.sel = 3 + GLOB + rand
        self.depth = DEPTH if ctx % DEPTH == 0 else ctx
        self.lanes = ctx // self.depth
        per_owner = -(-query_blocks * rand // max(1, ctx - 4))
        most, first = 0, []
        for device in range(ctx):
            far = [s for s in range(1, ctx) if abs(s - device) > 1]
            for lane in range(self.lanes):
                there = [s for s in far if s % self.lanes == lane]
                if lane == device % self.lanes:
                    continue
                if device == 0:
                    first.append(there)
                else:
                    most = max(most, len(there))
        over = [there for there in first if len(there) > most]
        self.direct = None
        if len(over) == 1 and len(over[0]) == most + 1:
            self.direct = over[0][0]
        elif over:
            most = max(len(there) for there in over)
        self.slots = 2 + GLOB + min(query_blocks * rand, per_owner * most)
        self.direct_slots = 0 if self.direct is None else min(query_blocks, per_owner)
        self.own = self.depth * query_blocks
        self.far = (self.lanes - 1) * self.slots + self.direct_slots
        self.pool = self.own + self.far

    def column_place(self, me, owner, offset):
        row = lax.rem(me // self.lanes - owner // self.lanes + self.depth, self.depth)
        return row * self.qb + offset

    def place(self, me, owner, offset, slot):
        mine, theirs = lax.rem(me, self.lanes), lax.rem(owner, self.lanes)
        pack = lax.rem(theirs - mine + self.lanes, self.lanes) - 1
        return jnp.where(
            mine == theirs, self.column_place(me, owner, offset), self.own + pack * self.slots + slot
        )


def dot(a, b, dims):
    return lax.dot_general(a, b, dims, preferred_element_type=jnp.float32)


def rows_of(place):
    return pl.ds(pl.multiple_of(place * BLK, BLK), BLK)


def tables_kernel(where, named, table, walk, counts, *, plan):
    qb, rand, lanes = plan.qb, plan.rand, plan.lanes
    sel, named_each = plan.sel, plan.qb * plan.rand
    me = where[0]
    mine = lax.rem(me, lanes)
    left, right = jnp.maximum(me - 1, 0), jnp.minimum(me + 1, plan.ctx - 1)
    for lane in range(lanes):
        counts[lane] = jnp.int32(2 + GLOB)
    counts[lanes] = jnp.int32(0)
    for i in range(qb):
        table[i * sel] = plan.place(me, left, qb - 1, 0) if i == 0 else jnp.int32(i - 1)
        table[i * sel + 1] = jnp.int32(i)
        table[i * sel + 2] = plan.place(me, right, 0, 1) if i == qb - 1 else jnp.int32(i + 1)
        for j in range(GLOB):
            table[i * sel + 3 + j] = plan.place(me, jnp.int32(0), j, 2 + j)
        for j in range(3):
            block = me * qb + i - 1 + j
            counted = (block >= GLOB) & (block < plan.ctx * qb)
            table[qb * sel + i * 3 + j] = counted.astype(jnp.int32)

    def straight(device, owner):
        return jnp.bool_(False) if plan.direct is None else (device == 0) & (owner == plan.direct)

    def entry(n, carry):
        block = named[me * named_each + n]
        owner = block // qb
        apart = straight(me, owner)
        lane = jnp.where(apart, lanes, lax.rem(owner, lanes))
        slot = counts[lane]
        place = plan.place(me, owner, lax.rem(block, qb), slot)
        place = jnp.where(apart, plan.own + (lanes - 1) * plan.slots + slot, place)
        table[(n // rand) * sel + 3 + GLOB + lax.rem(n, rand)] = place
        counts[lane] = slot + 1
        return carry

    lax.fori_loop(0, named_each, entry, 0)

    def clear(n, carry):
        walk[n] = jnp.int32(0)
        return carry

    lax.fori_loop(0, plan.far, clear, 0)
    for step in range(1, lanes):
        base = (step - 1) * plan.slots
        other = me - mine + lax.rem(mine + step, lanes)

        @pl.when((other >= 1) & (lax.rem(other - 1 + lanes, lanes) == mine))
        def _():
            walk[base] = plan.column_place(me, other - 1, qb - 1)

        @pl.when((other + 1 < plan.ctx) & (lax.rem(other + 1, lanes) == mine))
        def _():
            walk[base + 1] = plan.column_place(me, other + 1, 0)

        @pl.when(mine == 0)
        def _():
            for j in range(GLOB):
                walk[base + 2 + j] = plan.column_place(me, jnp.int32(0), j)

        def theirs(n, slot):
            block = named[other * named_each + n]
            owner = block // qb
            hit = (lax.rem(owner, lanes) == mine) & jnp.logical_not(straight(other, owner))

            @pl.when(hit)
            def _():
                walk[base + slot] = plan.column_place(me, owner, lax.rem(block, qb))

            return slot + hit.astype(jnp.int32)

        lax.fori_loop(0, named_each, theirs, jnp.int32(2 + GLOB))
    if plan.direct is not None:

        @pl.when(me == plan.direct)
        def _():
            def zeroth(n, slot):
                block = named[n]
                hit = block // qb == plan.direct

                @pl.when(hit)
                def _():
                    walk[(lanes - 1) * plan.slots + slot] = lax.rem(block, qb)

                return slot + hit.astype(jnp.int32)

            lax.fori_loop(0, named_each, zeroth, jnp.int32(0))


def tables(plan, where, named):
    smem = pl.BlockSpec(memory_space=pltpu.SMEM)
    return pl.pallas_call(
        functools.partial(tables_kernel, plan=plan),
        in_specs=[smem, smem],
        out_specs=[smem, smem],
        out_shape=[
            jax.ShapeDtypeStruct((plan.qb * (plan.sel + 3),), jnp.int32),
            jax.ShapeDtypeStruct((max(1, plan.far),), jnp.int32),
        ],
        scratch_shapes=[pltpu.SMEM((plan.lanes + 1,), jnp.int32)],
        cost_estimate=COST,
        name="list_tables",
    )(where, named)


def whole(a):
    return pl.BlockSpec(a.shape, lambda n, *_: (0, 0))


ANYWHERE = pl.BlockSpec(memory_space=pl.ANY)


def gate_kernel(*refs):
    del refs


def gate(array, *waits):
    return pl.pallas_call(
        gate_kernel,
        in_specs=[ANYWHERE] * (1 + len(waits)),
        out_specs=ANYWHERE,
        out_shape=jax.ShapeDtypeStruct(array.shape, array.dtype),
        input_output_aliases={0: 0},
        cost_estimate=COST,
        name="gate",
    )(array, *waits)


def pack_kernel(walk, *refs, plan, sources, base, slots, size):
    out, pool = refs[-2:]
    rows = plan.qb * BLK
    for t, some in enumerate(sources):
        for k, (n, at) in enumerate(some):
            pool[k * rows : (k + 1) * rows, :] = refs[n][at : at + rows, :]
        for slot in range(slots):
            place = walk[base + slot]
            out[(t * slots + slot) * BLK : (t * slots + slot + 1) * BLK, :] = pool[rows_of(place), :]


def pack(plan, walk, units, step, waits=()):
    rows = plan.qb * BLK
    arrays = [a for unit in units for a in (unit if step else unit[:1])]
    per = plan.depth if step else 1
    halves = units[0][0].shape[0] // rows
    sources = [
        [(u * per + k, half * rows) for k in range(per)] for u in range(len(units)) for half in range(halves)
    ]
    slots = plan.slots if step else plan.direct_slots
    base = (step - 1 if step else plan.lanes - 1) * plan.slots
    size = len(sources) * slots * BLK
    return pl.pallas_call(
        functools.partial(pack_kernel, plan=plan, sources=sources, base=base, slots=slots, size=size),
        grid_spec=pltpu.PrefetchScalarGridSpec(
            num_scalar_prefetch=1,
            grid=(1,),
            in_specs=[whole(a) for a in arrays] + [ANYWHERE] * len(waits),
            out_specs=pl.BlockSpec((size, HD), lambda n, *_: (0, 0)),
            scratch_shapes=[pltpu.VMEM((per * rows, HD), jnp.bfloat16)],
        ),
        out_shape=jax.ShapeDtypeStruct((size, HD), jnp.bfloat16),
        compiler_params=pltpu.CompilerParams(vmem_limit_bytes=SMALL_VMEM),
        cost_estimate=COST,
        name="pack_blocks",
    )(walk, *arrays, *waits)


def merge_kernel(walk, *refs, plan, halves, direct_first):
    rows = plan.qb * BLK
    columns, refs = refs[:halves], refs[halves:]
    packs, refs = refs[: plan.lanes - 1], refs[plan.lanes - 1 :]
    direct = refs[0]
    outs, total = refs[-1 - plan.depth : -1], refs[-1]
    for t in range(halves):
        total[...] = columns[t][...]

        def add(given, slots, first, base):
            for slot in range(slots):
                at = (first + slot) * BLK
                total[rows_of(walk[base + slot]), :] += given[at : at + BLK, :].astype(jnp.float32)

        for step in range(1, plan.lanes):
            add(packs[step - 1], plan.slots, t * plan.slots, (step - 1) * plan.slots)
        if plan.direct is not None:
            add(direct, plan.direct_slots, (direct_first + t) * plan.direct_slots, (plan.lanes - 1) * plan.slots)
        for k in range(plan.depth):
            outs[k][t * rows : (t + 1) * rows, :] = total[k * rows : (k + 1) * rows, :].astype(outs[k].dtype)


def merge(plan, walk, columns, packs, direct, direct_first=0, waits=()):
    halves = len(columns)
    shape = (halves * plan.qb * BLK, HD)
    kinds = [jnp.float32] + [jnp.bfloat16] * (plan.depth - 1)
    args = list(columns) + list(packs) + ([] if direct is None else [direct])
    return pl.pallas_call(
        functools.partial(
            merge_kernel, plan=plan, halves=halves, direct_first=direct_first
        ),
        grid_spec=pltpu.PrefetchScalarGridSpec(
            num_scalar_prefetch=1,
            grid=(1,),
            in_specs=[whole(a) for a in args] + [ANYWHERE] * len(waits),
            out_specs=[pl.BlockSpec(shape, lambda n, *_: (0, 0))] * plan.depth,
            scratch_shapes=[pltpu.VMEM((plan.own * BLK, HD), jnp.float32)],
        ),
        out_shape=[jax.ShapeDtypeStruct(shape, kind) for kind in kinds],
        compiler_params=pltpu.CompilerParams(vmem_limit_bytes=VMEM_LIMIT),
        cost_estimate=COST,
        name="merge_terms",
    )(walk, *args, *waits)


def attend_kernel(table, *refs, plan, qpk, per, given, sources, split):
    q_ref, do_ref = refs[:2]
    parts, refs = refs[2 : 2 + given], refs[2 + given :]
    refs = refs[-(12 + (2 if split else 1) * (plan.lanes - 1) + (plan.direct is not None)) :]
    o_ref, dq_ref, dk_col, dv_col = refs[:4]
    packed, refs = refs[4:-8], refs[-8:]
    kpool, vpool, keys, values, dk_sum, dv_sum, dk_far, dv_far = refs
    i = pl.program_id(0)
    sel = plan.sel
    scale = HD ** -0.5

    @pl.when(i == 0)
    def _():
        for pool, some in zip((kpool, vpool), sources):
            at = 0
            for source, start, size in some:
                pool[at : at + size, :] = parts[source][start : start + size, :]
                at += size
        for total in (dk_col, dv_col, dk_far, dv_far):
            total[...] = jnp.zeros_like(total)

    for j in range(sel):
        place = rows_of(table[i * sel + j])
        keys[j * BLK : (j + 1) * BLK, :] = kpool[place, :]
        values[j * BLK : (j + 1) * BLK, :] = vpool[place, :]
    counted = [table[plan.qb * sel + i * 3 + j] != 0 for j in range(3)]
    K, V = keys[...], values[...]
    KT, VT = K.T, V.T
    for h in range(0, qpk, per):

        def stacked(ref):
            return jnp.concatenate([ref[:, (h + t) * HD : (h + t + 1) * HD] for t in range(per)], axis=0)

        q, do = stacked(q_ref), stacked(do_ref)
        scores = dot(K, q, NT)
        scores = jnp.concatenate(
            [jnp.where(counted[j], scores[j * BLK : (j + 1) * BLK], -jnp.inf) for j in range(3)]
            + [scores[3 * BLK :]],
            axis=0,
        )
        largest = jnp.max(scores, axis=0, keepdims=True)
        raised = jnp.exp2((scores - largest) * (scale * LOG2E))
        inverse = 1.0 / jnp.sum(raised, axis=0, keepdims=True)
        raised_b = raised.astype(jnp.bfloat16)
        attended = dot(VT, raised_b, NN) * inverse
        prob_grad = dot(V, do, NT)
        do_t, q_t = do.T.astype(jnp.float32), q.T.astype(jnp.float32)
        centre = jnp.sum(attended * do_t, axis=0, keepdims=True)
        score_grad = (raised * (prob_grad - centre)).astype(jnp.bfloat16)
        query_grad = dot(KT, score_grad, NN) * (inverse * scale)
        value_grad = dot(raised_b, (do_t * inverse).astype(jnp.bfloat16), NT)
        key_grad = dot(score_grad, (q_t * (inverse * scale)).astype(jnp.bfloat16), NT)
        attended, query_grad = attended.T, query_grad.T
        for t in range(per):
            o_ref[:, (h + t) * HD : (h + t + 1) * HD] = attended[t * BLK : (t + 1) * BLK].astype(jnp.bfloat16)
            dq_ref[:, (h + t) * HD : (h + t + 1) * HD] = query_grad[t * BLK : (t + 1) * BLK].astype(jnp.bfloat16)
        if h == 0:
            dk_sum[...], dv_sum[...] = key_grad, value_grad
        else:
            dk_sum[...] += key_grad
            dv_sum[...] += value_grad
    for j in range(sel):
        place = table[i * sel + j]
        part = slice(j * BLK, (j + 1) * BLK)

        @pl.when(place < plan.own)
        def _():
            dk_col[rows_of(place), :] += dk_sum[part, :]
            dv_col[rows_of(place), :] += dv_sum[part, :]

        @pl.when(place >= plan.own)
        def _():
            dk_far[rows_of(place - plan.own), :] += dk_sum[part, :]
            dv_far[rows_of(place - plan.own), :] += dv_sum[part, :]

    @pl.when(i == plan.qb - 1)
    def _():
        size = plan.slots * BLK
        for t in range(plan.lanes - 1):
            part = slice(t * size, (t + 1) * size)
            if split:
                packed[t][...] = dk_far[part, :].astype(jnp.bfloat16)
                packed[plan.lanes - 1 + t][...] = dv_far[part, :].astype(jnp.bfloat16)
            else:
                packed[t][:size, :] = dk_far[part, :].astype(jnp.bfloat16)
                packed[t][size:, :] = dv_far[part, :].astype(jnp.bfloat16)
        if plan.direct is not None:
            rest = slice((plan.lanes - 1) * size, plan.far * BLK)
            packed[-1][: plan.direct_slots * BLK, :] = dk_far[rest, :].astype(jnp.bfloat16)
            packed[-1][plan.direct_slots * BLK :, :] = dv_far[rest, :].astype(jnp.bfloat16)


def attend(plan, table, queries, out_grad, units, packs, direct, group, qpk, outs, split, waits=()):
    width = qpk * HD
    rows, size = plan.qb * BLK, plan.slots * BLK
    parts, sources = [], [[], []]
    for u, (unit, some) in enumerate(zip(units, packs)):
        for array, step in [(a, rows) for a in unit] + [(a, size) for a in some]:
            for half in range(array.shape[0] // step):
                sources[u + half].append((len(parts), half * step, step))
            parts.append(array)
    if direct is not None:
        step = plan.direct_slots * BLK
        for half in range(2):
            sources[half].append((len(parts), half * step, step))
        parts.append(direct)
    q_spec = pl.BlockSpec((BLK, width), lambda n, *_: (n, group))
    shape = lambda blocks, kind: jax.ShapeDtypeStruct((blocks * BLK, HD), kind)
    o_shape = jax.ShapeDtypeStruct(queries.shape, jnp.bfloat16)
    out_shape = [o_shape, o_shape] + [shape(plan.own, jnp.float32)] * 2
    out_shape += [shape(plan.slots, jnp.bfloat16)] * (2 * (plan.lanes - 1)) if split else [
        shape(2 * plan.slots, jnp.bfloat16)
    ] * (plan.lanes - 1)
    if plan.direct is not None:
        out_shape.append(shape(2 * plan.direct_slots, jnp.bfloat16))
    args = [queries, out_grad, *parts]
    in_specs = [q_spec, q_spec] + [whole(a) for a in args[2:]]
    aliases = {1 + len(args) + t: t for t in range(len(outs))}
    listed = pltpu.VMEM((plan.sel * BLK, HD), jnp.bfloat16)
    listed_sum = pltpu.VMEM((plan.sel * BLK, HD), jnp.float32)
    out = pl.pallas_call(
        functools.partial(
            attend_kernel, plan=plan, qpk=qpk, per=4 if qpk % 4 == 0 else 1, given=len(parts), sources=sources, split=split
        ),
        grid_spec=pltpu.PrefetchScalarGridSpec(
            num_scalar_prefetch=1,
            grid=(plan.qb,),
            in_specs=in_specs + [ANYWHERE] * (len(outs) + len(waits)),
            out_specs=[q_spec, q_spec] + [whole(s) for s in out_shape[2:]],
            scratch_shapes=[pltpu.VMEM((plan.pool * BLK, HD), jnp.bfloat16)] * 2
            + [listed, listed, listed_sum, listed_sum]
            + [pltpu.VMEM((plan.far * BLK, HD), jnp.float32)] * 2,
        ),
        out_shape=out_shape,
        input_output_aliases=aliases,
        compiler_params=pltpu.CompilerParams(vmem_limit_bytes=VMEM_LIMIT),
        cost_estimate=COST,
        name="attend_head",
    )(table, *args, *outs, *waits)
    outs, columns, far = out[:2], out[2:4], list(out[4:])
    straight = far.pop() if plan.direct is not None else None
    return outs, columns, ([far[: plan.lanes - 1], far[plan.lanes - 1 :]] if split else [far], straight)


def column_shift(array, plan, rows):
    return lax.ppermute(array, "ctx", [(n, (n + rows * plan.lanes) % plan.ctx) for n in range(plan.ctx)])


def row_shift(array, plan, lanes):
    return lax.ppermute(
        array, "ctx", [(n, n - n % plan.lanes + (n + lanes) % plan.lanes) for n in range(plan.ctx)]
    )


def straight_shift(array, plan, there, back):
    return lax.ppermute(array, "ctx", [(there, back)])


def to_heads(arrays, group, groups):
    size = lax.axis_size("kvh")
    parts = jnp.stack([a.reshape(a.shape[0], size, groups, HD)[:, :, group] for a in arrays])
    parts = lax.all_to_all(parts.transpose(2, 0, 1, 3), "kvh", split_axis=0, concat_axis=0, tiled=True)
    return jnp.moveaxis(parts, 1, 0).reshape(-1, HD)


def to_tokens(array, count):
    size = lax.axis_size("kvh")
    parts = jnp.moveaxis(array.reshape(count, size, -1, HD), 1, 0)
    parts = lax.all_to_all(parts, "kvh", split_axis=0, concat_axis=0, tiled=True)
    return [parts[:, t] for t in range(count)]


def per_device(queries, keys, values, out_grad, random_blocks):
    kvh = lax.axis_size("kvh")
    groups = keys.shape[1] // (kvh * HD)
    qpk = queries.shape[1] // (groups * HD)
    plan = Plan(lax.axis_size("ctx"), queries.shape[0] // BLK, random_blocks.shape[1])
    lanes, depth, qb = plan.lanes, plan.depth, plan.qb
    where = lax.axis_index("ctx").astype(jnp.int32).reshape(1)
    table, walk = tables(plan, where, random_blocks.reshape(-1))

    def spread(own):
        return [own] + [column_shift(own, plan, k) for k in range(1, depth)]

    def across(units, waits=()):
        return [row_shift(pack(plan, walk, units, lanes - t, waits), plan, lanes - t) for t in range(1, lanes)]

    def straight(units, waits=()):
        if plan.direct is None:
            return None
        return straight_shift(pack(plan, walk, units, 0, waits), plan, plan.direct, 0)

    def send_back(packs):
        return [row_shift(packs[t - 1], plan, t) for t in range(1, lanes)][::-1]

    def home(terms, count):
        arrived = [column_shift(terms[k], plan, depth - k) for k in range(1, depth)]
        total = terms[0]
        for array in arrived:
            total = total + array.astype(jnp.float32)
        return to_tokens(total.astype(jnp.bfloat16), count), arrived

    own = [to_heads([a], 0, groups) for a in (keys, values)]
    units = [spread(a) for a in own]
    direct = straight([[a] for a in own], tuple(units[0][1:]))
    packs = [across([unit]) for unit in units]
    homes, outs, waits, arrived = [], [], (), []
    for g in range(groups):
        last = g + 1 == groups
        if not last:
            ready = [a for unit in units for a in unit[1:]]
            coming = gate(to_heads([keys, values], g + 1, groups), *ready)
            coming_units = [spread(coming)]
            coming_direct = straight([[coming]])
        outs, columns, (far, far_direct) = attend(
            plan, table, queries, out_grad, units, packs, direct, g, qpk, outs, last, waits
        )
        if far_direct is not None:
            far_direct = straight_shift(far_direct, plan, 0, plan.direct)
        if not last:
            far = [[gate(a, *coming_units[0][1:]) for a in far[0]]]
        backs = [send_back(some) for some in far]
        if last:
            for t in range(2):
                terms = merge(plan, walk, [columns[t]], backs[t], far_direct, direct_first=t, waits=tuple(arrived))
                homes.append(home(terms, 1)[0])
        else:
            terms = merge(plan, walk, columns, backs[0], far_direct, waits=tuple(arrived))
            total, arrived = home(terms, 2)
            homes.append(total)
            waits = (terms[1],)
            units, direct = coming_units, coming_direct
            packs = [across(units, tuple(backs[0]))]
    homes[-2:] = [homes[-2] + homes[-1]]
    key_grad, value_grad = (
        jnp.stack([some[n] for some in homes], axis=2).transpose(1, 0, 2, 3).reshape(keys.shape) for n in range(2)
    )
    return outs[0], outs[1], key_grad, value_grad


def solution(mesh):
    split = P("ctx", "kvh")
    home = P(("ctx", "kvh"), None)
    return jax.shard_map(
        per_device,
        mesh=mesh,
        in_specs=(split, home, home, split, P()),
        out_specs=(split, split, home, home),
        check_vma=False,
    )
```

time: 337 us -> 294 us (0.87)
  waiting for transfers between devices: 120 us -> 101 us
  Pallas kernels: 112 us -> 99 us
  blocking collectives: 18.5 us -> 10.1 us
    ppermute x24 -> x18, waiting for transfers between devices: 97.4 us -> 39.7 us  [column_shift(): lax.ppermute(array, 'ctx', [(n, (n + rows * plan.lanes) % plan.ctx) for n...]
    ppermute x8 -> x6, waiting for transfers between devices: 13.6 us -> 46.8 us  [row_shift(): lax.ppermute(array, 'ctx', [(n, n - n % plan.lanes + (n + lanes) % plan.l...]
    ppermute x24 -> x18, starting transfers between devices: 47.9 us -> 25.1 us  [column_shift(): lax.ppermute(array, 'ctx', [(n, (n + rows * plan.lanes) % plan.ctx) for n...]
    all_to_all x1 -> x5, starting transfers between devices: 3.51 us -> 21.5 us  [the longest x3 14.6 us: to_tokens(): lax.all_to_all(parts, 'kvh', split_axis=0, concat_axis=0, tiled=True)]
    pallas_call x8 -> x11, Pallas kernels: 34.1 us -> 20.9 us  [the longest x3 13.2 us: merge(): pl.pallas_call(functools.partial(merge_kernel, plan=plan, halves=halves,...]
    all_to_all x1, blocking collectives: 18.5 us -> 10.1 us  [to_heads(): lax.all_to_all(parts.transpose(2, 0, 1, 3), 'kvh', split_axis=0, concat_a...]
    ppermute x0 -> x4, waiting for transfers between devices: none -> 8.15 us  [straight_shift(): return lax.ppermute(array, 'ctx', [(there, back)])]
    concatenate x1 -> x0, other arithmetic: 5.72 us -> none  [per_device(): jnp.concatenate(attended, axis=1)]
  transfers between devices with their start and end apart: 33 -> 33, of which waited for: 13 -> 13; matrix products, arithmetic and copies ran while one was open for 2% -> 3% of each run, Pallas kernels for 33% -> 34%
where the time goes in v2:
time: 294 us; the launch traced here: 293 us
  waiting for transfers between devices  101 us (34%)
  Pallas kernels  99 us (34%)
  starting transfers between devices  59.4 us (20%)
  local copies, waits for them, and re-layouts  18 us (6%)
  blocking collectives  10.1 us (3%)
  other arithmetic  4.5 us (2%)
    pallas_call x2, Pallas kernels, attend(): pl.pallas_call(functools.partial(attend_kernel, plan=plan, qpk=qpk, per=4...  78.1 us
    ppermute x6, waiting for transfers between devices, row_shift(): lax.ppermute(array, 'ctx', [(n, n - n % plan.lanes + (n + lanes) % plan.l...  46.8 us
    ppermute x18, waiting for transfers between devices, column_shift(): lax.ppermute(array, 'ctx', [(n, (n + rows * plan.lanes) % plan.ctx) for n...  39.7 us
    ppermute x18, starting transfers between devices, column_shift(): lax.ppermute(array, 'ctx', [(n, (n + rows * plan.lanes) % plan.ctx) for n...  25.1 us
    all_to_all x3, starting transfers between devices, to_tokens(): lax.all_to_all(parts, 'kvh', split_axis=0, concat_axis=0, tiled=True)  14.6 us
    pallas_call x3, Pallas kernels, merge(): pl.pallas_call(functools.partial(merge_kernel, plan=plan, halves=halves,...  13.2 us
    unnamed x71, local copies, waits for them, and re-layouts  13.2 us
    all_to_all x1, blocking collectives, to_heads(): lax.all_to_all(parts.transpose(2, 0, 1, 3), 'kvh', split_axis=0, concat_a...  10.1 us
  transfers between devices with their start and end apart: 33, of which 13 were waited for; matrix products, arithmetic and copies ran while one was open for 3% of the time, Pallas kernels for 34%

profile of v2, /device:TPU:0, one launch (start us, length us, event | category | flops | bytes accessed | tf_op | source)
XLA Modules:
  0.0 292.6 jit_solution(3898160626547014666)
XLA Ops:
  0.6 1.2 copy.34
  1.9 1.2 copy.35
  3.4 10.1 %all_to_all.30 = bf16[4,1,256,128]{3,2,1,0:T(8,128)(2,1)S(1)} all-to-all(bf16[4,1,256,128]{3,2,1,0:T(8,128)(2,1)S(1)} %copy.39), channel_id=1, replica_groups=mesh['ctx'=8,'kvh'=4] {'kvh'}, dimensions={0} | all-to-all | bytes 524288 | tf_op jit(solution)/shard_map/all_to_all | solution.py:443
  13.5 3.6 %collective-permute-start.2 = (bf16[1024,128]{1,0:T(8,128)(2,1)S(1)}, bf16[1024,128]{1,0:T(8,128)(2,1)S(1)}, u32[]{:S(2)}, u32[]{:S(2)}) collective-permute-start(bf16[1024,128]{1,0:T(8,128)(2,1)S(1)} %bitcast.44), channel_id=1, source_target_pairs={{0,24},{4,28},{8,0},{12,4},{16,8},{20,12},{24,16},{28,20},{1,25},{... | collective-permute-start | bytes 786440 | tf_op jit(solution)/shard_map/ppermute | solution.py:427
  17.1 1.0 collective-permute-start
  18.9 3.4 %all-to-all-start.2 = ((bf16[4,1,256,128]{3,2,1,0:T(8,128)(2,1)}), bf16[4,1,256,128]{3,2,1,0:T(8,128)(2,1)S(1)}, u32[]{:S(2)}, u32[]{:S(2)}) async-start(bf16[4,1,256,128]{3,2,1,0:T(8,128)(2,1)} %copy.40), calls=%async_computation.2 | async-start | bytes 524288 | tf_op jit(solution)/shard_map/all_to_all | solution.py:443
  24.2 2.7 list_tables.1
  26.9 1.4 all-to-all-done.2
  28.4 3.5 %all-to-all-start = ((bf16[4,2,256,128]{3,2,1,0:T(8,128)(2,1)}), bf16[4,2,256,128]{3,2,1,0:T(8,128)(2,1)S(1)}, u32[]{:S(2)}, u32[]{:S(2)}) async-start(bf16[4,2,256,128]{3,2,1,0:T(8,128)(2,1)} %copy.37), calls=%async_computation | async-start | bytes 1048576 | tf_op jit(solution)/shard_map/all_to_all | solution.py:443
  31.9 7.2 %collective-permute-done.1.refs_2_.refs_3_.refs_4_ = bf16[1024,128]{1,0:T(8,128)(2,1)S(1)} collective-permute-done((bf16[1024,128]{1,0:T(8,128)(2,1)S(1)}, bf16[1024,128]{1,0:T(8,128)(2,1)S(1)}, u32[]{:S(2)}, u32[]{:S(2)}) %collective-permute-start.1) | collective-permute-done | bytes 262176 | tf_op jit(solution)/shard_map/ppermute | solution.py:427
  40.3 1.3 collective-permute-start.11
  41.7 2.9 collective-permute-start.4
  44.6 2.0 collective-permute-start.3
  46.6 1.4 pack_blocks.5
  48.0 1.5 collective-permute-start.9
  49.5 17.6 %collective-permute-done.4.refs_5_.refs_2_.refs_9_ = bf16[1024,128]{1,0:T(8,128)(2,1)S(1)} collective-permute-done((bf16[1024,128]{1,0:T(8,128)(2,1)S(1)}, bf16[1024,128]{1,0:T(8,128)(2,1)S(1)}, u32[]{:S(2)}, u32[]{:S(2)}) %collective-permute-start.4) | collective-permute-done | bytes 262176 | tf_op jit(solution)/shard_map/ppermute | solution.py:427
  67.1 1.4 pack_blocks.6
  68.6 3.0 %collective-permute-start.10 = (bf16[2048,128]{1,0:T(8,128)(2,1)}, bf16[2048,128]{1,0:T(8,128)(2,1)}, u32[]{:S(2)}, u32[]{:S(2)}) collective-permute-start(bf16[2048,128]{1,0:T(8,128)(2,1)} %pack_blocks.6), channel_id=1, source_target_pairs={{0,4},{4,0},{8,12},{12,8},{16,20},{20,16},{24,28},{28,24},{1,5},{5... | collective-permute-start | bytes 1572872 | tf_op jit(solution)/shard_map/ppermute | solution.py:431
  73.5 1.0 collective-permute-start.6
  74.6 6.7 %collective-permute-done.10.refs_11_ = bf16[2048,128]{1,0:T(8,128)(2,1)} collective-permute-done((bf16[2048,128]{1,0:T(8,128)(2,1)}, bf16[2048,128]{1,0:T(8,128)(2,1)}, u32[]{:S(2)}, u32[]{:S(2)}) %collective-permute-start.10) | collective-permute-done | bytes 524320 | tf_op jit(solution)/shard_map/ppermute | solution.py:431
  81.3 39.1 %attend_head.2 = (bf16[1024,2048]{1,0:T(8,128)(2,1)}, bf16[1024,2048]{1,0:T(8,128)(2,1)}, f32[4096,128]{1,0:T(8,128)}, f32[4096,128]{1,0:T(8,128)}, bf16[4096,12...) custom-call(s32[88]{0:T(128)} %get-tuple-element.31.table, bf16[1024,2048]{1,0:T(8,128)(2,1)} %refs_0_.3, ...), custom_call_target="tpu_custom_call" | custom-call | bytes 1024 | tf_op jit(solution)/shard_map/attend_head/pallas_call | solution.py:402
  122.6 21.0 %collective-permute-done.12.refs_4_.refs_2_ = bf16[4096,128]{1,0:T(8,128)(2,1)S(1)} collective-permute-done((bf16[4096,128]{1,0:T(8,128)(2,1)}, bf16[4096,128]{1,0:T(8,128)(2,1)S(1)}, u32[]{:S(2)}, u32[]{:S(2)}) %collective-permute-start.12) | collective-permute-done | bytes 1048608 | tf_op jit(solution)/shard_map/ppermute | solution.py:431
  143.5 1.0 copy-done.2
  144.6 1.0 copy-done.4
  145.6 1.0 copy-done.6
  147.8 1.6 collective-permute-start.15
  150.1 1.3 collective-permute-start.14
  151.4 3.4 %collective-permute-done.15.refs_3_ = bf16[1536,128]{1,0:T(8,128)(2,1)S(1)} collective-permute-done((bf16[1536,128]{1,0:T(8,128)(2,1)S(1)}, bf16[1536,128]{1,0:T(8,128)(2,1)S(1)}, u32[]{:S(2)}, u32[]{:S(2)}) %collective-permute-start.15) | collective-permute-done | bytes 393248 | tf_op jit(solution)/shard_map/ppermute | solution.py:437
  155.5 5.6 %merge_terms.3 = (f32[2048,128]{1,0:T(8,128)}, bf16[2048,128]{1,0:T(8,128)(2,1)}, bf16[2048,128]{1,0:T(8,128)(2,1)}, bf16[2048,128]{1,0:T(8,128)(2,1)}) custom-call(s32[22]{0:T(128)} %get-tuple-element.32.walk, f32[4096,128]{1,0:T(8,128)} %get-tuple-element.36.refs_0_, f32[4096,128]{1,0:T(8,128)} %get-tuple-element.37.refs_1_, bf16[4096,128]{1,0:T(8,128)(2,1)} %copy-done.12, ...), custom_call_target="tpu_custom_call" | custom-call | bytes 1024 | tf_op jit(solution)/shard_map/merge_terms/pallas_call | solution.py:264
  161.0 3.8 %collective-permute-start.16 = (bf16[2048,128]{1,0:T(8,128)(2,1)}, bf16[2048,128]{1,0:T(8,128)(2,1)S(1)}, u32[]{:S(2)}, u32[]{:S(2)}) collective-permute-start(bf16[2048,128]{1,0:T(8,128)(2,1)} %get-tuple-element.39.refs_10_), channel_id=1, source_target_pairs={{0,24},{4,28},{8,0},{12,4},{16,8},{20,12},{24,16},{28,20},{1,25},{... | collective-permute-start | bytes 1572872 | tf_op jit(solution)/shard_map/ppermute | solution.py:427
  165.4 11.4 %collective-permute-done.13.refs_6_ = bf16[4096,128]{1,0:T(8,128)(2,1)S(1)} collective-permute-done((bf16[4096,128]{1,0:T(8,128)(2,1)S(1)}, bf16[4096,128]{1,0:T(8,128)(2,1)S(1)}, u32[]{:S(2)}, u32[]{:S(2)}) %collective-permute-start.13) | collective-permute-done | bytes 1048608 | tf_op jit(solution)/shard_map/ppermute | solution.py:431
  177.8 39.0 %attend_head.3 = (bf16[1024,2048]{1,0:T(8,128)(2,1)}, bf16[1024,2048]{1,0:T(8,128)(2,1)}, f32[4096,128]{1,0:T(8,128)}, f32[4096,128]{1,0:T(8,128)}, bf16[2048,12...) custom-call(s32[88]{0:T(128)} %get-tuple-element.31.table, ...), custom_call_target="tpu_custom_call", output_to_operand_aliasing={{0}: (9, {}), {1}: (10, {})} | custom-call | bytes 1024 | tf_op jit(solution)/shard_map/attend_head/pallas_call | solution.py:402
  216.8 1.4 collective-permute-start.20
  218.3 1.3 collective-permute-start.24
  219.6 4.3 %collective-permute-done.20.refs_2_ = bf16[1536,128]{1,0:T(8,128)(2,1)S(1)} collective-permute-done((bf16[1536,128]{1,0:T(8,128)(2,1)}, bf16[1536,128]{1,0:T(8,128)(2,1)S(1)}, u32[]{:S(2)}, u32[]{:S(2)}) %collective-permute-start.20) | collective-permute-done | bytes 393248 | tf_op jit(solution)/shard_map/ppermute | solution.py:437
  223.9 7.7 %collective-permute-done.19.refs_1_ = bf16[2048,128]{1,0:T(8,128)(2,1)S(1)} collective-permute-done((bf16[2048,128]{1,0:T(8,128)(2,1)}, bf16[2048,128]{1,0:T(8,128)(2,1)S(1)}, u32[]{:S(2)}, u32[]{:S(2)}) %collective-permute-start.19) | collective-permute-done | bytes 524320 | tf_op jit(solution)/shard_map/ppermute | solution.py:431
  232.4 3.8 %merge_terms.4 = (f32[1024,128]{1,0:T(8,128)}, bf16[1024,128]{1,0:T(8,128)(2,1)}, bf16[1024,128]{1,0:T(8,128)(2,1)}, bf16[1024,128]{1,0:T(8,128)(2,1)}) custom-call(s32[22]{0:T(128)} %get-tuple-element.32.walk, f32[4096,128]{1,0:T(8,128)} %get-tuple-element.45.refs_0_, bf16[2048,128]{1,0:T(8,128)(2,1)} %copy-done.27, bf16[1536,128]{1,0:T(8,128)(2,1)} %copy-done.21, ...), custom_call_target="tpu_custom_call" | custom-call | bytes 1024 | tf_op jit(solution)/shard_map/merge_terms/pallas_call | solution.py:264
  236.3 5.2 %collective-permute-start.22 = (bf16[1024,128]{1,0:T(8,128)(2,1)}, bf16[1024,128]{1,0:T(8,128)(2,1)S(1)}, u32[]{:S(2)}, u32[]{:S(2)}) collective-permute-start(bf16[1024,128]{1,0:T(8,128)(2,1)} %get-tuple-element.50), channel_id=1, source_target_pairs={{0,16},{4,20},{8,24},{12,28},{16,0},{20,4},{24,8},{28,12},{1,17},{... | collective-permute-start | bytes 786440 | tf_op jit(solution)/shard_map/ppermute | solution.py:427
  241.5 1.7 add_convert_fusion
  244.0 3.5 %all-to-all-start.3 = ((bf16[4,2,256,128]{3,2,1,0:T(8,128)(2,1)}), bf16[4,2,256,128]{3,2,1,0:T(8,128)(2,1)S(1)}, u32[]{:S(2)}, u32[]{:S(2)}) async-start(bf16[4,2,256,128]{3,2,1,0:T(8,128)(2,1)} %bitcast.42), calls=%async_computation.3 | async-start | bytes 1048576 | tf_op jit(solution)/shard_map/all_to_all | solution.py:450
  248.3 3.8 %merge_terms.5 = (f32[1024,128]{1,0:T(8,128)}, bf16[1024,128]{1,0:T(8,128)(2,1)}, bf16[1024,128]{1,0:T(8,128)(2,1)}, bf16[1024,128]{1,0:T(8,128)(2,1)}) custom-call(s32[22]{0:T(128)} %get-tuple-element.32.walk, f32[4096,128]{1,0:T(8,128)} %get-tuple-element.52.refs_0_, bf16[2048,128]{1,0:T(8,128)(2,1)} %copy-done.26, bf16[1536,128]{1,0:T(8,128)(2,1)} %copy-done.21, ...), custom_call_target="tpu_custom_call" | custom-call | bytes 1024 | tf_op jit(solution)/shard_map/merge_terms/pallas_call | solution.py:264
  252.2 3.8 %collective-permute-start.25 = (bf16[1024,128]{1,0:T(8,128)(2,1)}, bf16[1024,128]{1,0:T(8,128)(2,1)S(1)}, u32[]{:S(2)}, u32[]{:S(2)}) collective-permute-start(bf16[1024,128]{1,0:T(8,128)(2,1)} %get-tuple-element.55), channel_id=1, source_target_pairs={{0,24},{4,28},{8,0},{12,4},{16,8},{20,12},{24,16},{28,20},{1,25},{... | collective-permute-start | bytes 786440 | tf_op jit(solution)/shard_map/ppermute | solution.py:427
  257.9 6.5 %all-to-all-start.4 = ((bf16[4,1,256,128]{3,2,1,0:T(8,128)(2,1)}), bf16[4,1,256,128]{3,2,1,0:T(8,128)(2,1)S(1)}, u32[]{:S(2)}, u32[]{:S(2)}) async-start(bf16[4,1,256,128]{3,2,1,0:T(8,128)(2,1)} %bitcast.18), calls=%async_computation.4 | async-start | bytes 524288 | tf_op jit(solution)/shard_map/all_to_all | solution.py:450
  264.4 14.4 %collective-permute-done.26 = bf16[1024,128]{1,0:T(8,128)(2,1)S(1)} collective-permute-done((bf16[1024,128]{1,0:T(8,128)(2,1)}, bf16[1024,128]{1,0:T(8,128)(2,1)S(1)}, u32[]{:S(2)}, u32[]{:S(2)}) %collective-permute-start.26) | collective-permute-done | bytes 262176 | tf_op jit(solution)/shard_map/ppermute | solution.py:427
  278.8 1.9 add_convert_fusion.1
  280.6 4.7 %all-to-all-start.5 = ((bf16[4,1,256,128]{3,2,1,0:T(8,128)(2,1)}), bf16[4,1,256,128]{3,2,1,0:T(8,128)(2,1)S(1)}, u32[]{:S(2)}, u32[]{:S(2)}) async-start(bf16[4,1,256,128]{3,2,1,0:T(8,128)(2,1)} %bitcast.24), calls=%async_computation.5 | async-start | bytes 524288 | tf_op jit(solution)/shard_map/all_to_all | solution.py:450
  285.9 1.0 copy.48
  286.9 4.5 %all-to-all-done.5 = bf16[4,1,256,128]{3,2,1,0:T(8,128)(2,1)S(1)} async-done(((bf16[4,1,256,128]{3,2,1,0:T(8,128)(2,1)}), bf16[4,1,256,128]{3,2,1,0:T(8,128)(2,1)S(1)}, u32[]{:S(2)}, u32[]{:S(2)}) %all-to-all-start.5) | async-done | bytes 262176 | tf_op jit(solution)/shard_map/all_to_all | solution.py:450
  (119 shorter events, 18.6 us)
Async XLA Ops:
  0.6 21.7 %copy-start.30 = (s32[64,3]{0,1:T(4,128)S(1)}, s32[64,3]{0,1:T(4,128)}, u32[]{:S(2)}) copy-start(s32[64,3]{0,1:T(4,128)} %param.9) | copy-start | bytes 2308
  13.5 55.1 %copy-start.10 = (bf16[4,1,256,128]{3,2,1,0:T(8,128)(2,1)}, bf16[4,1,256,128]{3,2,1,0:T(8,128)(2,1)S(1)}, u32[]{:S(2)}) copy-start(bf16[4,1,256,128]{3,2,1,0:T(8,128)(2,1)S(1)} %all_to_all.30) | copy-start | bytes 786436
  13.5 18.4 %collective-permute-start.2 = (bf16[1024,128]{1,0:T(8,128)(2,1)S(1)}, bf16[1024,128]{1,0:T(8,128)(2,1)S(1)}, u32[]{:S(2)}, u32[]{:S(2)}) collective-permute-start(bf16[1024,128]{1,0:T(8,128)(2,1)S(1)} %bitcast.44), channel_id=1, source_target_pairs={{0,24},{4,28},{8,0},{12,4},{16,8},{20,12},{24,16},{28,20},{1,25},{... | collective-permute-start | bytes 786440 | tf_op jit(solution)/shard_map/ppermute | solution.py:427
  17.1 21.9 %collective-permute-start.1 = (bf16[1024,128]{1,0:T(8,128)(2,1)S(1)}, bf16[1024,128]{1,0:T(8,128)(2,1)S(1)}, u32[]{:S(2)}, u32[]{:S(2)}) collective-permute-start(bf16[1024,128]{1,0:T(8,128)(2,1)S(1)} %bitcast.45), channel_id=1, source_target_pairs={{0,16},{4,20},{8,24},{12,28},{16,0},{20,4},{24,8},{28,12},{1,17},{... | collective-permute-start | bytes 786440 | tf_op jit(solution)/shard_map/ppermute | solution.py:427
  17.1 21.9 %collective-permute-start = (bf16[1024,128]{1,0:T(8,128)(2,1)S(1)}, bf16[1024,128]{1,0:T(8,128)(2,1)S(1)}, u32[]{:S(2)}, u32[]{:S(2)}) collective-permute-start(bf16[1024,128]{1,0:T(8,128)(2,1)S(1)} %bitcast.46), channel_id=1, source_target_pairs={{0,8},{4,12},{8,16},{12,20},{16,24},{20,28},{24,0},{28,4},{1,9},{5... | collective-permute-start | bytes 786440 | tf_op jit(solution)/shard_map/ppermute | solution.py:427
  18.9 9.4 %all-to-all-start.2 = ((bf16[4,1,256,128]{3,2,1,0:T(8,128)(2,1)}), bf16[4,1,256,128]{3,2,1,0:T(8,128)(2,1)S(1)}, u32[]{:S(2)}, u32[]{:S(2)}) async-start(bf16[4,1,256,128]{3,2,1,0:T(8,128)(2,1)} %copy.40), calls=%async_computation.2 | async-start | bytes 524288 | tf_op jit(solution)/shard_map/all_to_all | solution.py:443
  28.4 44.1 %copy-start.11 = (bf16[4,1,256,128]{3,2,1,0:T(8,128)(2,1)}, bf16[4,1,256,128]{3,2,1,0:T(8,128)(2,1)S(1)}, u32[]{:S(2)}) copy-start(bf16[4,1,256,128]{3,2,1,0:T(8,128)(2,1)S(1)} %all-to-all-done.2) | copy-start | bytes 786436
  28.4 43.2 %all-to-all-start = ((bf16[4,2,256,128]{3,2,1,0:T(8,128)(2,1)}), bf16[4,2,256,128]{3,2,1,0:T(8,128)(2,1)S(1)}, u32[]{:S(2)}, u32[]{:S(2)}) async-start(bf16[4,2,256,128]{3,2,1,0:T(8,128)(2,1)} %copy.37), calls=%async_computation | async-start | bytes 1048576 | tf_op jit(solution)/shard_map/all_to_all | solution.py:443
  31.8 40.6 %copy-start.7 = (bf16[1024,128]{1,0:T(8,128)(2,1)}, bf16[1024,128]{1,0:T(8,128)(2,1)S(1)}, u32[]{:S(2)}) copy-start(bf16[1024,128]{1,0:T(8,128)(2,1)S(1)} %collective-permute-done.2.refs_3_.refs_4_.refs_5_) | copy-start | bytes 786436
  39.0 33.4 %copy-start.8 = (bf16[1024,128]{1,0:T(8,128)(2,1)}, bf16[1024,128]{1,0:T(8,128)(2,1)S(1)}, u32[]{:S(2)}) copy-start(bf16[1024,128]{1,0:T(8,128)(2,1)S(1)} %collective-permute-done.1.refs_2_.refs_3_.refs_4_) | copy-start | bytes 786436
  39.0 33.4 %copy-start.9 = (bf16[1024,128]{1,0:T(8,128)(2,1)}, bf16[1024,128]{1,0:T(8,128)(2,1)S(1)}, u32[]{:S(2)}) copy-start(bf16[1024,128]{1,0:T(8,128)(2,1)S(1)} %collective-permute-done.refs_1_.refs_2_.refs_3_) | copy-start | bytes 786436
  40.3 33.2 %collective-permute-start.11 = (bf16[1536,128]{1,0:T(8,128)(2,1)S(1)}, bf16[1536,128]{1,0:T(8,128)(2,1)}, u32[]{:S(2)}, u32[]{:S(2)}) collective-permute-start(bf16[1536,128]{1,0:T(8,128)(2,1)S(1)} %pack_blocks.7), channel_id=1, source_target_pairs={{12,0},{13,1},{14,2},{15,3}} | collective-permute-start | bytes 1179656 | tf_op jit(solution)/shard_map/ppermute | solution.py:437
  41.6 7.9 %collective-permute-start.5 = (bf16[1024,128]{1,0:T(8,128)(2,1)S(1)}, bf16[1024,128]{1,0:T(8,128)(2,1)S(1)}, u32[]{:S(2)}, u32[]{:S(2)}) collective-permute-start(bf16[1024,128]{1,0:T(8,128)(2,1)S(1)} %bitcast.51), channel_id=1, source_target_pairs={{0,24},{4,28},{8,0},{12,4},{16,8},{20,12},{24,16},{28,20},{1,25},{... | collective-permute-start | bytes 786440 | tf_op jit(solution)/shard_map/ppermute | solution.py:427
  41.7 25.4 %collective-permute-start.4 = (bf16[1024,128]{1,0:T(8,128)(2,1)S(1)}, bf16[1024,128]{1,0:T(8,128)(2,1)S(1)}, u32[]{:S(2)}, u32[]{:S(2)}) collective-permute-start(bf16[1024,128]{1,0:T(8,128)(2,1)S(1)} %bitcast.52), channel_id=1, source_target_pairs={{0,16},{4,20},{8,24},{12,28},{16,0},{20,4},{24,8},{28,12},{1,17},{... | collective-permute-start | bytes 786440 | tf_op jit(solution)/shard_map/ppermute | solution.py:427
  44.6 22.5 %collective-permute-start.3 = (bf16[1024,128]{1,0:T(8,128)(2,1)S(1)}, bf16[1024,128]{1,0:T(8,128)(2,1)S(1)}, u32[]{:S(2)}, u32[]{:S(2)}) collective-permute-start(bf16[1024,128]{1,0:T(8,128)(2,1)S(1)} %bitcast.53), channel_id=1, source_target_pairs={{0,8},{4,12},{8,16},{12,20},{16,24},{20,28},{24,0},{28,4},{1,9},{5... | collective-permute-start | bytes 786440 | tf_op jit(solution)/shard_map/ppermute | solution.py:427
  48.0 26.5 %collective-permute-start.9 = (bf16[2048,128]{1,0:T(8,128)(2,1)}, bf16[2048,128]{1,0:T(8,128)(2,1)S(1)}, u32[]{:S(2)}, u32[]{:S(2)}) collective-permute-start(bf16[2048,128]{1,0:T(8,128)(2,1)} %pack_blocks.5), channel_id=1, source_target_pairs={{0,4},{4,0},{8,12},{12,8},{16,20},{20,16},{24,28},{28,24},{1,5},{5... | collective-permute-start | bytes 1572872 | tf_op jit(solution)/shard_map/ppermute | solution.py:431
  49.5 22.9 %copy-start.13 = (bf16[1024,128]{1,0:T(8,128)(2,1)}, bf16[1024,128]{1,0:T(8,128)(2,1)S(1)}, u32[]{:S(2)}) copy-start(bf16[1024,128]{1,0:T(8,128)(2,1)S(1)} %collective-permute-done.5.refs_6_.refs_3_.refs_10_) | copy-start | bytes 786436
  68.6 12.7 %collective-permute-start.10 = (bf16[2048,128]{1,0:T(8,128)(2,1)}, bf16[2048,128]{1,0:T(8,128)(2,1)}, u32[]{:S(2)}, u32[]{:S(2)}) collective-permute-start(bf16[2048,128]{1,0:T(8,128)(2,1)} %pack_blocks.6), channel_id=1, source_target_pairs={{0,4},{4,0},{8,12},{12,8},{16,20},{20,16},{24,28},{28,24},{1,5},{5... | collective-permute-start | bytes 1572872 | tf_op jit(solution)/shard_map/ppermute | solution.py:431
  72.5 48.0 %collective-permute-start.8 = (bf16[2048,128]{1,0:T(8,128)(2,1)}, bf16[2048,128]{1,0:T(8,128)(2,1)S(1)}, u32[]{:S(2)}, u32[]{:S(2)}) collective-permute-start(bf16[2048,128]{1,0:T(8,128)(2,1)} %gate.2.refs_0_.refs_2_), channel_id=1, source_target_pairs={{0,24},{4,28},{8,0},{12,4},{16,8},{20,12},{24,16},{28,20},{1,25},{... | collective-permute-start | bytes 1572872 | tf_op jit(solution)/shard_map/ppermute | solution.py:427
  72.5 47.9 %collective-permute-start.7 = (bf16[2048,128]{1,0:T(8,128)(2,1)}, bf16[2048,128]{1,0:T(8,128)(2,1)S(1)}, u32[]{:S(2)}, u32[]{:S(2)}) collective-permute-start(bf16[2048,128]{1,0:T(8,128)(2,1)} %gate.2.refs_0_.refs_2_), channel_id=1, source_target_pairs={{0,16},{4,20},{8,24},{12,28},{16,0},{20,4},{24,8},{28,12},{1,17},{... | collective-permute-start | bytes 1572872 | tf_op jit(solution)/shard_map/ppermute | solution.py:427
  73.5 46.9 %collective-permute-start.6 = (bf16[2048,128]{1,0:T(8,128)(2,1)}, bf16[2048,128]{1,0:T(8,128)(2,1)S(1)}, u32[]{:S(2)}, u32[]{:S(2)}) collective-permute-start(bf16[2048,128]{1,0:T(8,128)(2,1)} %gate.2.refs_0_.refs_2_), channel_id=1, source_target_pairs={{0,8},{4,12},{8,16},{12,20},{16,24},{20,28},{24,0},{28,4},{1,9},{5... | collective-permute-start | bytes 1572872 | tf_op jit(solution)/shard_map/ppermute | solution.py:427
  81.3 62.2 %copy-start = (bf16[2048,128]{1,0:T(8,128)(2,1)S(1)}, bf16[2048,128]{1,0:T(8,128)(2,1)}, u32[]{:S(2)}) copy-start(bf16[2048,128]{1,0:T(8,128)(2,1)} %gate.2.refs_0_.refs_2_) | copy-start | bytes 1572868
  81.3 62.2 %copy-start.17 = (s32[22]{0:T(128)S(1)}, s32[22]{0:T(128)}, u32[]{:S(2)}) copy-start(s32[22]{0:T(128)} %get-tuple-element.32.walk) | copy-start | bytes 268
  120.4 27.4 %copy-start.31 = (bf16[1536,128]{1,0:T(8,128)(2,1)S(1)}, bf16[1536,128]{1,0:T(8,128)(2,1)}, u32[]{:S(2)}) copy-start(bf16[1536,128]{1,0:T(8,128)(2,1)} %get-tuple-element.38) | copy-start | bytes 1179652
  121.6 21.9 %collective-permute-start.12 = (bf16[4096,128]{1,0:T(8,128)(2,1)}, bf16[4096,128]{1,0:T(8,128)(2,1)S(1)}, u32[]{:S(2)}, u32[]{:S(2)}) collective-permute-start(bf16[4096,128]{1,0:T(8,128)(2,1)} %gate.3), channel_id=1, source_target_pairs={{0,4},{4,0},{8,12},{12,8},{16,20},{20,16},{24,28},{28,24},{1,5},{5... | collective-permute-start | bytes 3145736 | tf_op jit(solution)/shard_map/ppermute | solution.py:431
  147.5 29.3 %collective-permute-start.13 = (bf16[4096,128]{1,0:T(8,128)(2,1)S(1)}, bf16[4096,128]{1,0:T(8,128)(2,1)S(1)}, u32[]{:S(2)}, u32[]{:S(2)}) collective-permute-start(bf16[4096,128]{1,0:T(8,128)(2,1)S(1)} %pack_blocks.8), channel_id=1, source_target_pairs={{0,4},{4,0},{8,12},{12,8},{16,20},{20,16},{24,28},{28,24},{1,5},{5... | collective-permute-start | bytes 3145736 | tf_op jit(solution)/shard_map/ppermute | solution.py:431
  147.8 6.9 %collective-permute-start.15 = (bf16[1536,128]{1,0:T(8,128)(2,1)S(1)}, bf16[1536,128]{1,0:T(8,128)(2,1)S(1)}, u32[]{:S(2)}, u32[]{:S(2)}) collective-permute-start(bf16[1536,128]{1,0:T(8,128)(2,1)S(1)} %copy-done.31), channel_id=1, source_target_pairs={{0,12},{1,13},{2,14},{3,15}} | collective-permute-start | bytes 1179656 | tf_op jit(solution)/shard_map/ppermute | solution.py:437
  150.1 15.3 %collective-permute-start.14 = (bf16[1536,128]{1,0:T(8,128)(2,1)S(1)}, bf16[1536,128]{1,0:T(8,128)(2,1)S(1)}, u32[]{:S(2)}, u32[]{:S(2)}) collective-permute-start(bf16[1536,128]{1,0:T(8,128)(2,1)S(1)} %pack_blocks.9), channel_id=1, source_target_pairs={{12,0},{13,1},{14,2},{15,3}} | collective-permute-start | bytes 1179656 | tf_op jit(solution)/shard_map/ppermute | solution.py:437
  161.0 57.2 %collective-permute-start.17 = (bf16[2048,128]{1,0:T(8,128)(2,1)}, bf16[2048,128]{1,0:T(8,128)(2,1)S(1)}, u32[]{:S(2)}, u32[]{:S(2)}) collective-permute-start(bf16[2048,128]{1,0:T(8,128)(2,1)} %get-tuple-element.43), channel_id=1, source_target_pairs={{0,16},{4,20},{8,24},{12,28},{16,0},{20,4},{24,8},{28,12},{1,17},{... | collective-permute-start | bytes 1572872 | tf_op jit(solution)/shard_map/ppermute | solution.py:427
  161.0 58.6 %collective-permute-start.18 = (bf16[2048,128]{1,0:T(8,128)(2,1)}, bf16[2048,128]{1,0:T(8,128)(2,1)S(1)}, u32[]{:S(2)}, u32[]{:S(2)}) collective-permute-start(bf16[2048,128]{1,0:T(8,128)(2,1)} %get-tuple-element.44), channel_id=1, source_target_pairs={{0,8},{4,12},{8,16},{12,20},{16,24},{20,28},{24,0},{28,4},{1,9},{5... | collective-permute-start | bytes 1572872 | tf_op jit(solution)/shard_map/ppermute | solution.py:427
  161.0 58.6 %collective-permute-start.16 = (bf16[2048,128]{1,0:T(8,128)(2,1)}, bf16[2048,128]{1,0:T(8,128)(2,1)S(1)}, u32[]{:S(2)}, u32[]{:S(2)}) collective-permute-start(bf16[2048,128]{1,0:T(8,128)(2,1)} %get-tuple-element.39.refs_10_), channel_id=1, source_target_pairs={{0,24},{4,28},{8,0},{12,4},{16,8},{20,12},{24,16},{28,20},{1,25},{... | collective-permute-start | bytes 1572872 | tf_op jit(solution)/shard_map/ppermute | solution.py:427
  216.7 24.8 %copy-start.22 = (f32[2048,128]{1,0:T(8,128)S(1)}, f32[2048,128]{1,0:T(8,128)}, u32[]{:S(2)}) copy-start(f32[2048,128]{1,0:T(8,128)} %get-tuple-element.42) | copy-start | bytes 3145732
  216.8 14.9 %collective-permute-start.19 = (bf16[2048,128]{1,0:T(8,128)(2,1)}, bf16[2048,128]{1,0:T(8,128)(2,1)S(1)}, u32[]{:S(2)}, u32[]{:S(2)}) collective-permute-start(bf16[2048,128]{1,0:T(8,128)(2,1)} %get-tuple-element.46), channel_id=1, source_target_pairs={{0,4},{4,0},{8,12},{12,8},{16,20},{20,16},{24,28},{28,24},{1,5},{5... | collective-permute-start | bytes 1572872 | tf_op jit(solution)/shard_map/ppermute | solution.py:431
  216.8 7.1 %collective-permute-start.20 = (bf16[1536,128]{1,0:T(8,128)(2,1)}, bf16[1536,128]{1,0:T(8,128)(2,1)S(1)}, u32[]{:S(2)}, u32[]{:S(2)}) collective-permute-start(bf16[1536,128]{1,0:T(8,128)(2,1)} %get-tuple-element.47), channel_id=1, source_target_pairs={{0,12},{1,13},{2,14},{3,15}} | collective-permute-start | bytes 1179656 | tf_op jit(solution)/shard_map/ppermute | solution.py:437
  218.3 13.4 %copy-start.18 = (bf16[2048,128]{1,0:T(8,128)(2,1)}, bf16[2048,128]{1,0:T(8,128)(2,1)S(1)}, u32[]{:S(2)}) copy-start(bf16[2048,128]{1,0:T(8,128)(2,1)S(1)} %collective-permute-done.17.refs_4_) | copy-start | bytes 1572868
  218.3 29.2 %collective-permute-start.24 = (bf16[2048,128]{1,0:T(8,128)(2,1)}, bf16[2048,128]{1,0:T(8,128)(2,1)S(1)}, u32[]{:S(2)}, u32[]{:S(2)}) collective-permute-start(bf16[2048,128]{1,0:T(8,128)(2,1)} %get-tuple-element.53), channel_id=1, source_target_pairs={{0,4},{4,0},{8,12},{12,8},{16,20},{20,16},{24,28},{28,24},{1,5},{5... | collective-permute-start | bytes 1572872 | tf_op jit(solution)/shard_map/ppermute | solution.py:431
  219.6 12.0 %copy-start.19 = (bf16[2048,128]{1,0:T(8,128)(2,1)}, bf16[2048,128]{1,0:T(8,128)(2,1)S(1)}, u32[]{:S(2)}) copy-start(bf16[2048,128]{1,0:T(8,128)(2,1)S(1)} %collective-permute-done.18.refs_5_) | copy-start | bytes 1572868
  219.6 12.0 %copy-start.20 = (bf16[2048,128]{1,0:T(8,128)(2,1)}, bf16[2048,128]{1,0:T(8,128)(2,1)S(1)}, u32[]{:S(2)}) copy-start(bf16[2048,128]{1,0:T(8,128)(2,1)S(1)} %collective-permute-done.16.refs_3_) | copy-start | bytes 1572868
  236.3 19.7 %collective-permute-start.21 = (bf16[1024,128]{1,0:T(8,128)(2,1)}, bf16[1024,128]{1,0:T(8,128)(2,1)S(1)}, u32[]{:S(2)}, u32[]{:S(2)}) collective-permute-start(bf16[1024,128]{1,0:T(8,128)(2,1)} %get-tuple-element.49), channel_id=1, source_target_pairs={{0,24},{4,28},{8,0},{12,4},{16,8},{20,12},{24,16},{28,20},{1,25},{... | collective-permute-start | bytes 786440 | tf_op jit(solution)/shard_map/ppermute | solution.py:427
  236.3 20.8 %collective-permute-start.22 = (bf16[1024,128]{1,0:T(8,128)(2,1)}, bf16[1024,128]{1,0:T(8,128)(2,1)S(1)}, u32[]{:S(2)}, u32[]{:S(2)}) collective-permute-start(bf16[1024,128]{1,0:T(8,128)(2,1)} %get-tuple-element.50), channel_id=1, source_target_pairs={{0,16},{4,20},{8,24},{12,28},{16,0},{20,4},{24,8},{28,12},{1,17},{... | collective-permute-start | bytes 786440 | tf_op jit(solution)/shard_map/ppermute | solution.py:427
  241.5 15.5 %collective-permute-start.23 = (bf16[1024,128]{1,0:T(8,128)(2,1)}, bf16[1024,128]{1,0:T(8,128)(2,1)S(1)}, u32[]{:S(2)}, u32[]{:S(2)}) collective-permute-start(bf16[1024,128]{1,0:T(8,128)(2,1)} %get-tuple-element.51), channel_id=1, source_target_pairs={{0,8},{4,12},{8,16},{12,20},{16,24},{20,28},{24,0},{28,4},{1,9},{5... | collective-permute-start | bytes 786440 | tf_op jit(solution)/shard_map/ppermute | solution.py:427
  241.5 15.5 %copy-start.24 = (f32[1024,128]{1,0:T(8,128)S(1)}, f32[1024,128]{1,0:T(8,128)}, u32[]{:S(2)}) copy-start(f32[1024,128]{1,0:T(8,128)} %get-tuple-element.48) | copy-start | bytes 1572868
  244.0 13.9 %all-to-all-start.3 = ((bf16[4,2,256,128]{3,2,1,0:T(8,128)(2,1)}), bf16[4,2,256,128]{3,2,1,0:T(8,128)(2,1)S(1)}, u32[]{:S(2)}, u32[]{:S(2)}) async-start(bf16[4,2,256,128]{3,2,1,0:T(8,128)(2,1)} %bitcast.42), calls=%async_computation.3 | async-start | bytes 1048576 | tf_op jit(solution)/shard_map/all_to_all | solution.py:450
  252.2 12.2 %collective-permute-start.25 = (bf16[1024,128]{1,0:T(8,128)(2,1)}, bf16[1024,128]{1,0:T(8,128)(2,1)S(1)}, u32[]{:S(2)}, u32[]{:S(2)}) collective-permute-start(bf16[1024,128]{1,0:T(8,128)(2,1)} %get-tuple-element.55), channel_id=1, source_target_pairs={{0,24},{4,28},{8,0},{12,4},{16,8},{20,12},{24,16},{28,20},{1,25},{... | collective-permute-start | bytes 786440 | tf_op jit(solution)/shard_map/ppermute | solution.py:427
  256.0 22.8 %collective-permute-start.26 = (bf16[1024,128]{1,0:T(8,128)(2,1)}, bf16[1024,128]{1,0:T(8,128)(2,1)S(1)}, u32[]{:S(2)}, u32[]{:S(2)}) collective-permute-start(bf16[1024,128]{1,0:T(8,128)(2,1)} %get-tuple-element.56), channel_id=1, source_target_pairs={{0,16},{4,20},{8,24},{12,28},{16,0},{20,4},{24,8},{28,12},{1,17},{... | collective-permute-start | bytes 786440 | tf_op jit(solution)/shard_map/ppermute | solution.py:427
  256.0 22.8 %collective-permute-start.27 = (bf16[1024,128]{1,0:T(8,128)(2,1)}, bf16[1024,128]{1,0:T(8,128)(2,1)S(1)}, u32[]{:S(2)}, u32[]{:S(2)}) collective-permute-start(bf16[1024,128]{1,0:T(8,128)(2,1)} %get-tuple-element.57), channel_id=1, source_target_pairs={{0,8},{4,12},{8,16},{12,20},{16,24},{20,28},{24,0},{28,4},{1,9},{5... | collective-permute-start | bytes 786440 | tf_op jit(solution)/shard_map/ppermute | solution.py:427
  257.9 22.7 %all-to-all-start.4 = ((bf16[4,1,256,128]{3,2,1,0:T(8,128)(2,1)}), bf16[4,1,256,128]{3,2,1,0:T(8,128)(2,1)S(1)}, u32[]{:S(2)}, u32[]{:S(2)}) async-start(bf16[4,1,256,128]{3,2,1,0:T(8,128)(2,1)} %bitcast.18), calls=%async_computation.4 | async-start | bytes 524288 | tf_op jit(solution)/shard_map/all_to_all | solution.py:450
  280.6 10.7 %all-to-all-start.5 = ((bf16[4,1,256,128]{3,2,1,0:T(8,128)(2,1)}), bf16[4,1,256,128]{3,2,1,0:T(8,128)(2,1)S(1)}, u32[]{:S(2)}, u32[]{:S(2)}) async-start(bf16[4,1,256,128]{3,2,1,0:T(8,128)(2,1)} %bitcast.24), calls=%async_computation.5 | async-start | bytes 524288 | tf_op jit(solution)/shard_map/all_to_all | solution.py:450
  (17 other events, 54.7 us)

commit v3 on v2

--- a/solution.py
+++ b/solution.py
@@ -45,6 +45,16 @@
             most = max(len(there) for there in over)
         self.slots = 2 + GLOB + min(query_blocks * rand, per_owner * most)
         self.direct_slots = 0 if self.direct is None else min(query_blocks, per_owner)
+        self.row_slots = {}
+        for step in range(1, self.depth):
+            most_here = 0
+            for device in range(ctx):
+                row = (device // self.lanes - step) % self.depth
+                inside = [s for s in range(ctx) if s // self.lanes == row]
+                size = GLOB * (row == 0) + sum(abs(s - device) == 1 for s in inside)
+                size += min(query_blocks * rand, per_owner * sum(s > 0 and abs(s - device) > 1 for s in inside))
+                most_here = max(most_here, size)
+            self.row_slots[step] = most_here
         self.own = self.depth * query_blocks
         self.far = (self.lanes - 1) * self.slots + self.direct_slots
         self.pool = self.own + self.far
@@ -171,6 +181,112 @@
         cost_estimate=COST,
         name="list_tables",
     )(where, named)
+
+
+def row_tables_kernel(where, named, table, walk, counts, *, plan):
+    qb, rand, lanes, depth, ctx = plan.qb, plan.rand, plan.lanes, plan.depth, plan.ctx
+    sel, named_each = plan.sel, plan.qb * plan.rand
+    me = where[0]
+    mine, row = lax.rem(me, lanes), me // lanes
+
+    def in_row(owner, offset):
+        return lax.rem(lax.rem(owner, lanes) - mine + lanes, lanes) * qb + offset
+
+    def walk_list(device, there, visit):
+        for j in range(GLOB):
+            pl.when(there == 0)(functools.partial(visit, jnp.int32(0), j, 3 + j))
+        pl.when((device >= 1) & ((device - 1) // lanes == there))(functools.partial(visit, device - 1, qb - 1, 0))
+        right = (device + 1 < ctx) & ((device + 1) // lanes == there)
+        pl.when(right)(functools.partial(visit, device + 1, 0, (qb - 1) * sel + 2))
+
+        def entry(n, carry):
+            block = named[device * named_each + n]
+            owner = block // qb
+            at = (n // rand) * sel + 3 + GLOB + lax.rem(n, rand)
+            pl.when(owner // lanes == there)(functools.partial(visit, owner, lax.rem(block, qb), at))
+            return carry
+
+        lax.fori_loop(0, named_each, entry, 0)
+
+    for i in range(qb):
+        table[i * sel] = jnp.int32(max(i - 1, 0))
+        table[i * sel + 1] = jnp.int32(i)
+        table[i * sel + 2] = jnp.int32(min(i + 1, qb - 1))
+
+    def beside(owner, offset, at):
+        table[at] = in_row(owner, offset)
+
+    walk_list(me, row, beside)
+    base, begin = lanes * qb, 0
+    for step, slots in plan.row_slots.items():
+        counts[0] = jnp.int32(0)
+
+        def found(owner, offset, at, base=base):
+            table[at] = base + counts[0]
+            counts[0] = counts[0] + 1
+
+        walk_list(me, lax.rem(row - step + depth, depth), found)
+        counts[0] = jnp.int32(0)
+        for n in range(slots):
+            walk[begin + n] = jnp.int32(0)
+
+        def asked(owner, offset, at, begin=begin):
+            walk[begin + counts[0]] = in_row(owner, offset)
+            counts[0] = counts[0] + 1
+
+        walk_list(lax.rem(row + step, depth) * lanes + mine, row, asked)
+        base, begin = base + slots, begin + slots
+    for i in range(1, qb):
+        for j in range(GLOB):
+            table[i * sel + 3 + j] = table[3 + j]
+
+
+def row_tables(plan, where, named):
+    smem = pl.BlockSpec(memory_space=pltpu.SMEM)
+    return pl.pallas_call(
+        functools.partial(row_tables_kernel, plan=plan),
+        in_specs=[smem, smem],
+        out_specs=[smem, smem],
+        out_shape=[
+            jax.ShapeDtypeStruct((plan.qb * plan.sel,), jnp.int32),
+            jax.ShapeDtypeStruct((sum(plan.row_slots.values()),), jnp.int32),
+        ],
+        scratch_shapes=[pltpu.SMEM((1,), jnp.int32)],
+        cost_estimate=COST,
+        name="row_tables",
+    )(where, named)
+
+
+def pack_rows_kernel(walk, *refs, plan):
+    shards, outs, pool = refs[: plan.lanes], refs[-plan.depth : -1], refs[-1]
+    rows = plan.qb * BLK
+    for t in range(2):
+        for lane, shard in enumerate(shards):
+            pool[lane * rows : (lane + 1) * rows, :] = shard[t * rows : (t + 1) * rows, :]
+        begin = 0
+        for out, slots in zip(outs, plan.row_slots.values()):
+            for slot in range(slots):
+                place = rows_of(walk[begin + slot])
+                out[(t * slots + slot) * BLK : (t * slots + slot + 1) * BLK, :] = pool[place, :]
+            begin += slots
+
+
+def pack_rows(plan, walk, shards, waits):
+    shapes = [jax.ShapeDtypeStruct((2 * slots * BLK, HD), jnp.bfloat16) for slots in plan.row_slots.values()]
+    return pl.pallas_call(
+        functools.partial(pack_rows_kernel, plan=plan),
+        grid_spec=pltpu.PrefetchScalarGridSpec(
+            num_scalar_prefetch=1,
+            grid=(1,),
+            in_specs=[whole(a) for a in shards] + [ANYWHERE] * len(waits),
+            out_specs=[whole(s) for s in shapes],
+            scratch_shapes=[pltpu.VMEM((plan.lanes * plan.qb * BLK, HD), jnp.bfloat16)],
+        ),
+        out_shape=shapes,
+        compiler_params=pltpu.CompilerParams(vmem_limit_bytes=SMALL_VMEM),
+        cost_estimate=COST,
+        name="pack_rows",
+    )(walk, *shards, *waits)
 
 
 def whole(a):
@@ -237,7 +353,7 @@
 def merge_kernel(walk, *refs, plan, halves, direct_first):
     rows = plan.qb * BLK
     columns, refs = refs[:halves], refs[halves:]
-    packs, refs = refs[: plan.lanes - 1], refs[plan.lanes - 1 :]
+    packs, refs = refs[: halves * (plan.lanes - 1)], refs[halves * (plan.lanes - 1) :]
     direct = refs[0]
     outs, total = refs[-1 - plan.depth : -1], refs[-1]
     for t in range(halves):
@@ -249,7 +365,7 @@
                 total[rows_of(walk[base + slot]), :] += given[at : at + BLK, :].astype(jnp.float32)
 
         for step in range(1, plan.lanes):
-            add(packs[step - 1], plan.slots, t * plan.slots, (step - 1) * plan.slots)
+            add(packs[t * (plan.lanes - 1) + step - 1], plan.slots, 0, (step - 1) * plan.slots)
         if plan.direct is not None:
             add(direct, plan.direct_slots, (direct_first + t) * plan.direct_slots, (plan.lanes - 1) * plan.slots)
         for k in range(plan.depth):
@@ -260,7 +376,7 @@
     halves = len(columns)
     shape = (halves * plan.qb * BLK, HD)
     kinds = [jnp.float32] + [jnp.bfloat16] * (plan.depth - 1)
-    args = list(columns) + list(packs) + ([] if direct is None else [direct])
+    args = list(columns) + [a for some in packs for a in some] + ([] if direct is None else [direct])
     return pl.pallas_call(
         functools.partial(
             merge_kernel, plan=plan, halves=halves, direct_first=direct_first
@@ -279,29 +395,52 @@
     )(walk, *args, *waits)
 
 
-def attend_kernel(table, *refs, plan, qpk, per, given, sources, split):
+def attend_kernel(found, table, *refs, plan, qpk, per, given, sources, split, first, ends):
     q_ref, do_ref = refs[:2]
     parts, refs = refs[2 : 2 + given], refs[2 + given :]
-    refs = refs[-(12 + (2 if split else 1) * (plan.lanes - 1) + (plan.direct is not None)) :]
-    o_ref, dq_ref, dk_col, dv_col = refs[:4]
-    packed, refs = refs[4:-8], refs[-8:]
-    kpool, vpool, keys, values, dk_sum, dv_sum, dk_far, dv_far = refs
-    i = pl.program_id(0)
+    before = refs[: 2 if first else 0]
+    if ends:
+        refs = refs[-(12 + (2 if split else 1) * (plan.lanes - 1) + (plan.direct is not None)) :]
+        o_ref, dq_ref, dk_col, dv_col = refs[:4]
+        packed, refs = refs[4:-8], refs[-8:]
+        kpool, vpool, keys, values, dk_sum, dv_sum, dk_far, dv_far = refs
+    else:
+        o_ref, dq_ref, dk_sum, dv_sum, kpool, vpool, keys, values = refs[-8:]
+    n = pl.program_id(0)
+    i = n + first
     sel = plan.sel
     scale = HD ** -0.5
 
-    @pl.when(i == 0)
+    def add(i, k_terms, v_terms, base):
+        for j in range(sel):
+            place = table[i * sel + j]
+            part = slice(base + j * BLK, base + (j + 1) * BLK)
+
+            @pl.when(place < plan.own)
+            def _():
+                dk_col[rows_of(place), :] += k_terms[part, :]
+                dv_col[rows_of(place), :] += v_terms[part, :]
+
+            @pl.when(place >= plan.own)
+            def _():
+                dk_far[rows_of(place - plan.own), :] += k_terms[part, :]
+                dv_far[rows_of(place - plan.own), :] += v_terms[part, :]
+
+    @pl.when(n == 0)
     def _():
         for pool, some in zip((kpool, vpool), sources):
             at = 0
             for source, start, size in some:
                 pool[at : at + size, :] = parts[source][start : start + size, :]
                 at += size
-        for total in (dk_col, dv_col, dk_far, dv_far):
-            total[...] = jnp.zeros_like(total)
+        if ends:
+            for total in (dk_col, dv_col, dk_far, dv_far):
+                total[...] = jnp.zeros_like(total)
+        for done in range(first):
+            add(done, *before, done * sel * BLK)
 
     for j in range(sel):
-        place = rows_of(table[i * sel + j])
+        place = rows_of(found[i * sel + j])
         keys[j * BLK : (j + 1) * BLK, :] = kpool[place, :]
         values[j * BLK : (j + 1) * BLK, :] = vpool[place, :]
     counted = [table[plan.qb * sel + i * 3 + j] != 0 for j in range(3)]
@@ -340,19 +479,9 @@
         else:
             dk_sum[...] += key_grad
             dv_sum[...] += value_grad
-    for j in range(sel):
-        place = table[i * sel + j]
-        part = slice(j * BLK, (j + 1) * BLK)
-
-        @pl.when(place < plan.own)
-        def _():
-            dk_col[rows_of(place), :] += dk_sum[part, :]
-            dv_col[rows_of(place), :] += dv_sum[part, :]
-
-        @pl.when(place >= plan.own)
-        def _():
-            dk_far[rows_of(place - plan.own), :] += dk_sum[part, :]
-            dv_far[rows_of(place - plan.own), :] += dv_sum[part, :]
+    if not ends:
+        return
+    add(i, dk_sum, dv_sum, 0)
 
     @pl.when(i == plan.qb - 1)
     def _():
@@ -371,54 +500,55 @@
             packed[-1][plan.direct_slots * BLK :, :] = dv_far[rest, :].astype(jnp.bfloat16)
 
 
-def attend(plan, table, queries, out_grad, units, packs, direct, group, qpk, outs, split, waits=()):
+def attend(plan, found, table, queries, out_grad, pieces, group, qpk, outs, split, first, count, terms=(), waits=()):
     width = qpk * HD
-    rows, size = plan.qb * BLK, plan.slots * BLK
     parts, sources = [], [[], []]
-    for u, (unit, some) in enumerate(zip(units, packs)):
-        for array, step in [(a, rows) for a in unit] + [(a, size) for a in some]:
-            for half in range(array.shape[0] // step):
-                sources[u + half].append((len(parts), half * step, step))
-            parts.append(array)
-    if direct is not None:
-        step = plan.direct_slots * BLK
+    for array, kind, step in pieces:
         for half in range(2):
-            sources[half].append((len(parts), half * step, step))
-        parts.append(direct)
-    q_spec = pl.BlockSpec((BLK, width), lambda n, *_: (n, group))
+            if kind == half:
+                sources[half].append((len(parts), 0, step))
+            elif kind == 2:
+                sources[half] += [(len(parts), at + half * step, step) for at in range(0, array.shape[0], 2 * step)]
+        parts.append(array)
+    pool = pltpu.VMEM((sum(step for _, _, step in sources[0]), HD), jnp.bfloat16)
+    q_spec = pl.BlockSpec((BLK, width), lambda n, *_: (n + first, group))
     shape = lambda blocks, kind: jax.ShapeDtypeStruct((blocks * BLK, HD), kind)
     o_shape = jax.ShapeDtypeStruct(queries.shape, jnp.bfloat16)
-    out_shape = [o_shape, o_shape] + [shape(plan.own, jnp.float32)] * 2
-    out_shape += [shape(plan.slots, jnp.bfloat16)] * (2 * (plan.lanes - 1)) if split else [
-        shape(2 * plan.slots, jnp.bfloat16)
-    ] * (plan.lanes - 1)
-    if plan.direct is not None:
+    ends = first + count == plan.qb
+    out_shape = [o_shape, o_shape] + [shape(plan.own if ends else count * plan.sel, jnp.float32)] * 2
+    if ends:
+        out_shape += [shape((1 if split else 2) * plan.slots, jnp.bfloat16)] * ((2 if split else 1) * (plan.lanes - 1))
+    if ends and plan.direct is not None:
         out_shape.append(shape(2 * plan.direct_slots, jnp.bfloat16))
-    args = [queries, out_grad, *parts]
+    args = [queries, out_grad, *parts, *terms]
     in_specs = [q_spec, q_spec] + [whole(a) for a in args[2:]]
-    aliases = {1 + len(args) + t: t for t in range(len(outs))}
+    aliases = {2 + len(args) + t: t for t in range(len(outs))}
     listed = pltpu.VMEM((plan.sel * BLK, HD), jnp.bfloat16)
+    term_spec = pl.BlockSpec((plan.sel * BLK, HD), lambda n, *_: (n, 0))
     listed_sum = pltpu.VMEM((plan.sel * BLK, HD), jnp.float32)
     out = pl.pallas_call(
         functools.partial(
-            attend_kernel, plan=plan, qpk=qpk, per=4 if qpk % 4 == 0 else 1, given=len(parts), sources=sources, split=split
+            attend_kernel, plan=plan, qpk=qpk, per=4 if qpk % 4 == 0 else 1, given=len(parts), sources=sources, split=split,
+            first=first, ends=ends,
         ),
         grid_spec=pltpu.PrefetchScalarGridSpec(
-            num_scalar_prefetch=1,
-            grid=(plan.qb,),
+            num_scalar_prefetch=2,
+            grid=(count,),
             in_specs=in_specs + [ANYWHERE] * (len(outs) + len(waits)),
-            out_specs=[q_spec, q_spec] + [whole(s) for s in out_shape[2:]],
-            scratch_shapes=[pltpu.VMEM((plan.pool * BLK, HD), jnp.bfloat16)] * 2
-            + [listed, listed, listed_sum, listed_sum]
-            + [pltpu.VMEM((plan.far * BLK, HD), jnp.float32)] * 2,
+            out_specs=[q_spec, q_spec] + ([whole(s) for s in out_shape[2:]] if ends else [term_spec] * 2),
+            scratch_shapes=[pool] * 2
+            + [listed, listed]
+            + ([listed_sum, listed_sum] + [pltpu.VMEM((plan.far * BLK, HD), jnp.float32)] * 2 if ends else []),
         ),
         out_shape=out_shape,
         input_output_aliases=aliases,
         compiler_params=pltpu.CompilerParams(vmem_limit_bytes=VMEM_LIMIT),
         cost_estimate=COST,
         name="attend_head",
-    )(table, *args, *outs, *waits)
+    )(found, table, *args, *outs, *waits)
     outs, columns, far = out[:2], out[2:4], list(out[4:])
+    if not ends:
+        return outs, columns, None
     straight = far.pop() if plan.direct is not None else None
     return outs, columns, ([far[: plan.lanes - 1], far[plan.lanes - 1 :]] if split else [far], straight)
 
@@ -437,11 +567,45 @@
     return lax.ppermute(array, "ctx", [(there, back)])
 
 
-def to_heads(arrays, group, groups):
+def cut_kernel(keys, values, out, *, size, groups):
+    for n in range(size):
+        for g in range(groups):
+            part = slice((n * groups + g) * HD, (n * groups + g + 1) * HD)
+            out[n, 2 * g] = keys[:, part]
+            out[n, 2 * g + 1] = values[:, part]
+
+
+def join_kernel(parts, *outs, size, groups):
+    rows = parts.shape[2]
+    for n in range(size):
+        for g in range(groups):
+            for t in range(2):
+                out, at = (outs[t], 0) if g == 0 else (outs[1 + g], t * size * rows)
+                out[at + n * rows : at + (n + 1) * rows, :] = parts[n, 2 * g + t]
+
+
+def to_heads(keys, values, groups):
     size = lax.axis_size("kvh")
-    parts = jnp.stack([a.reshape(a.shape[0], size, groups, HD)[:, :, group] for a in arrays])
-    parts = lax.all_to_all(parts.transpose(2, 0, 1, 3), "kvh", split_axis=0, concat_axis=0, tiled=True)
-    return jnp.moveaxis(parts, 1, 0).reshape(-1, HD)
+    rows = keys.shape[0]
+    vmem = pl.BlockSpec(memory_space=pltpu.VMEM)
+    parts = pl.pallas_call(
+        functools.partial(cut_kernel, size=size, groups=groups),
+        in_specs=[vmem, vmem],
+        out_specs=vmem,
+        out_shape=jax.ShapeDtypeStruct((size, 2 * groups, rows, HD), keys.dtype),
+        cost_estimate=COST,
+        name="cut_heads",
+    )(keys, values)
+    parts = lax.all_to_all(parts, "kvh", split_axis=0, concat_axis=0, tiled=True)
+    shapes = [(size * rows, HD)] * 2 + [(2 * size * rows, HD)] * (groups - 1)
+    return pl.pallas_call(
+        functools.partial(join_kernel, size=size, groups=groups),
+        in_specs=[vmem],
+        out_specs=[vmem] * len(shapes),
+        out_shape=[jax.ShapeDtypeStruct(shape, keys.dtype) for shape in shapes],
+        cost_estimate=COST,
+        name="join_heads",
+    )(parts)
 
 
 def to_tokens(array, count):
@@ -481,37 +645,49 @@
             total = total + array.astype(jnp.float32)
         return to_tokens(total.astype(jnp.bfloat16), count), arrived
 
-    own = [to_heads([a], 0, groups) for a in (keys, values)]
+    rows, size = qb * BLK, plan.slots * BLK
+    own = to_heads(keys, values, groups)
+    own, joined = own[:2], own[2:]
     units = [spread(a) for a in own]
     direct = straight([[a] for a in own], tuple(units[0][1:]))
-    packs = [across([unit]) for unit in units]
-    homes, outs, waits, arrived = [], [], (), []
+    in_row = [[a] + [row_shift(a, plan, lanes - t) for t in range(1, lanes)] for a in joined]
+    packs = [across([units[0]], tuple(a for some in in_row for a in some[1:]))]
+    packs.append(across([units[1]], (*packs[0], *([] if direct is None else [direct]))))
+    pieces = [(a, t, rows) for t in range(2) for a in units[t]] + [(a, t, size) for t in range(2) for a in packs[t]]
+    if direct is not None:
+        pieces.append((direct, 2, plan.direct_slots * BLK))
+    ready = [a for unit in units for a in unit[1:]]
+    found, homes, outs, arrived, waits = table, [], [], [], ()
+    if groups > 1:
+        row_found, row_walk = row_tables(plan, where, random_blocks.reshape(-1))
     for g in range(groups):
         last = g + 1 == groups
         if not last:
-            ready = [a for unit in units for a in unit[1:]]
-            coming = gate(to_heads([keys, values], g + 1, groups), *ready)
-            coming_units = [spread(coming)]
-            coming_direct = straight([[coming]])
-        outs, columns, (far, far_direct) = attend(
-            plan, table, queries, out_grad, units, packs, direct, g, qpk, outs, last, waits
-        )
+            sent = pack_rows(plan, row_walk, in_row[g], tuple(ready))
+            waits = (sent[0],)
+            ready = [column_shift(a, plan, step) for a, step in zip(sent, plan.row_slots)]
+        run = functools.partial(attend, plan, found, table, queries, out_grad, pieces, g, qpk)
+        if not g:
+            outs, columns, (far, far_direct) = run(outs, True, 0, qb, (), waits)
+        else:
+            before = merge(plan, walk, *before, waits=tuple(a for a, _, _ in pieces))
+            total, arrived = home(before, 2)
+            homes.append(total)
+            outs, columns, (far, far_direct) = run(outs, True, 0, qb, (), (before[1],))
+        if arrived:
+            far[1] = [gate(a, *arrived) for a in far[1]]
+            far_direct = far_direct if far_direct is None else gate(far_direct, *arrived)
         if far_direct is not None:
             far_direct = straight_shift(far_direct, plan, 0, plan.direct)
-        if not last:
-            far = [[gate(a, *coming_units[0][1:]) for a in far[0]]]
         backs = [send_back(some) for some in far]
         if last:
             for t in range(2):
-                terms = merge(plan, walk, [columns[t]], backs[t], far_direct, direct_first=t, waits=tuple(arrived))
+                terms = merge(plan, walk, [columns[t]], [backs[t]], far_direct, direct_first=t)
                 homes.append(home(terms, 1)[0])
         else:
-            terms = merge(plan, walk, columns, backs[0], far_direct, waits=tuple(arrived))
-            total, arrived = home(terms, 2)
-            homes.append(total)
-            waits = (terms[1],)
-            units, direct = coming_units, coming_direct
-            packs = [across(units, tuple(backs[0]))]
+            before = columns, backs, far_direct
+            found, pieces = row_found, [(a, 2, rows) for a in in_row[g]]
+            pieces += [(a, 2, slots * BLK) for a, slots in zip(ready, plan.row_slots.values())]
     homes[-2:] = [homes[-2] + homes[-1]]
     key_grad, value_grad = (
         jnp.stack([some[n] for some in homes], axis=2).transpose(1, 0, 2, 3).reshape(keys.shape) for n in range(2)

time: 294 us -> 291 us (0.990)
  Pallas kernels: 99 us -> 110 us
  waiting for transfers between devices: 101 us -> 90.8 us
  blocking collectives: 10.1 us -> 19.4 us
  local copies, waits for them, and re-layouts: 18 us -> 10.2 us
  starting transfers between devices: 59.4 us -> 54.4 us
    ppermute x6 -> x7, waiting for transfers between devices: 46.8 us -> 30.3 us  [row_shift(): lax.ppermute(array, 'ctx', [(n, n - n % plan.lanes + (n + lanes) % plan.l...]
    ppermute x18, waiting for transfers between devices: 39.7 us -> 50.4 us  [column_shift(): lax.ppermute(array, 'ctx', [(n, (n + rows * plan.lanes) % plan.ctx) for n...]
    pallas_call x0 -> x4, Pallas kernels: none -> 10.3 us  [the longest x1 4.78 us: row_tables(): pl.pallas_call(functools.partial(row_tables_kernel, plan=plan), in_specs=...]
    all_to_all x1, blocking collectives: 10.1 us -> 19.4 us  [to_heads(): lax.all_to_all(parts, 'kvh', split_axis=0, concat_axis=0, tiled=True)]
    all_to_all x2 -> x0, starting transfers between devices: 6.88 us -> none  [to_heads(): lax.all_to_all(parts.transpose(2, 0, 1, 3), 'kvh', split_axis=0, concat_a...]
    unnamed x71 -> x69, local copies, waits for them, and re-layouts: 13.2 us -> 8.34 us
    all_to_all x3, starting transfers between devices: 14.6 us -> 10.3 us  [to_tokens(): lax.all_to_all(parts, 'kvh', split_axis=0, concat_axis=0, tiled=True)]
    ppermute x18, starting transfers between devices: 25.1 us -> 29.1 us  [column_shift(): lax.ppermute(array, 'ctx', [(n, (n + rows * plan.lanes) % plan.ctx) for n...]
  transfers between devices with their start and end apart: 33 -> 31, of which waited for: 13 -> 11; matrix products, arithmetic and copies ran while one was open for 3% -> 2% of each run, Pallas kernels for 34% -> 34%
where the time goes in v3:
time: 291 us; the launch traced here: 290 us
  Pallas kernels  110 us (38%)
  waiting for transfers between devices  90.8 us (31%)
  starting transfers between devices  54.4 us (19%)
  blocking collectives  19.4 us (7%)
  local copies, waits for them, and re-layouts  10.2 us (4%)
  other arithmetic  4.07 us (1%)
    pallas_call x2, Pallas kernels, attend(): pl.pallas_call(functools.partial(attend_kernel, plan=plan, qpk=qpk, per=4...  78 us
    ppermute x18, waiting for transfers between devices, column_shift(): lax.ppermute(array, 'ctx', [(n, (n + rows * plan.lanes) % plan.ctx) for n...  50.4 us
    ppermute x7, waiting for transfers between devices, row_shift(): lax.ppermute(array, 'ctx', [(n, n - n % plan.lanes + (n + lanes) % plan.l...  30.3 us
    ppermute x18, starting transfers between devices, column_shift(): lax.ppermute(array, 'ctx', [(n, (n + rows * plan.lanes) % plan.ctx) for n...  29.1 us
    all_to_all x1, blocking collectives, to_heads(): lax.all_to_all(parts, 'kvh', split_axis=0, concat_axis=0, tiled=True)  19.4 us
    pallas_call x3, Pallas kernels, merge(): pl.pallas_call(functools.partial(merge_kernel, plan=plan, halves=halves,...  13.3 us
    ppermute x7, starting transfers between devices, row_shift(): lax.ppermute(array, 'ctx', [(n, n - n % plan.lanes + (n + lanes) % plan.l...  11 us
    all_to_all x3, starting transfers between devices, to_tokens(): lax.all_to_all(parts, 'kvh', split_axis=0, concat_axis=0, tiled=True)  10.3 us
  transfers between devices with their start and end apart: 31, of which 11 were waited for; matrix products, arithmetic and copies ran while one was open for 2% of the time, Pallas kernels for 34%

profile of v3, /device:TPU:0, one launch (start us, length us, event | category | flops | bytes accessed | tf_op | source)
XLA Modules:
  0.0 289.7 jit_solution(12288010889366042656)
XLA Ops:
  0.6 2.4 cut_heads.1
  3.0 19.4 %all_to_all.20.parts = bf16[4,4,256,128]{3,2,1,0:T(8,128)(2,1)} all-to-all(bf16[4,4,256,128]{3,2,1,0:T(8,128)(2,1)} %cut_heads.1), channel_id=1, replica_groups=mesh['ctx'=8,'kvh'=4] {'kvh'}, dimensions={0} | all-to-all | bytes 2097152 | tf_op jit(solution)/shard_map/all_to_all | solution.py:599
  22.4 2.2 join_heads.1
  24.6 2.3 collective-permute-start
  26.9 3.6 %collective-permute-start.3 = (bf16[1024,128]{1,0:T(8,128)(2,1)}, bf16[1024,128]{1,0:T(8,128)(2,1)S(1)}, u32[]{:S(2)}, u32[]{:S(2)}) collective-permute-start(bf16[1024,128]{1,0:T(8,128)(2,1)} %get-tuple-element.44.refs_0_.refs_2_), channel_id=1, source_target_pairs={{0,24},{4,28},{8,0},{12,4},{16,8},{20,12},{24,16},{28,20},{1,25},{... | collective-permute-start | bytes 786440 | tf_op jit(solution)/shard_map/ppermute | solution.py:557
  30.5 1.0 collective-permute-start.1
  32.4 2.7 list_tables.1
  35.1 2.6 collective-permute-done.3.refs_4_.refs_3_.refs_5_
  37.7 14.8 %collective-permute-done.2.refs_3_.refs_2_.refs_4_ = bf16[1024,128]{1,0:T(8,128)(2,1)S(1)} collective-permute-done((bf16[1024,128]{1,0:T(8,128)(2,1)}, bf16[1024,128]{1,0:T(8,128)(2,1)S(1)}, u32[]{:S(2)}, u32[]{:S(2)}) %collective-permute-start.2) | collective-permute-done | bytes 262176 | tf_op jit(solution)/shard_map/ppermute | solution.py:557
  52.4 1.1 copy-done.5
  54.2 1.4 pack_blocks.3
  56.2 2.3 pack_blocks.4
  58.5 1.3 collective-permute-start.11
  59.9 2.2 collective-permute-start.5
  62.1 1.9 collective-permute-start.4
  64.0 4.8 %row_tables.1 = (s32[64]{0:T(128)}, s32[36]{0:T(128)}) custom-call(s32[1]{0:T(128)} %bitcast.where, s32[192]{0:T(256)} %reshape.25.named), custom_call_target="tpu_custom_call" | custom-call | bytes 1024 | tf_op jit(solution)/shard_map/row_tables/pallas_call | solution.py:246
  68.8 15.6 %collective-permute-done.5.refs_6_.refs_2_.refs_8_ = bf16[1024,128]{1,0:T(8,128)(2,1)S(1)} collective-permute-done((bf16[1024,128]{1,0:T(8,128)(2,1)}, bf16[1024,128]{1,0:T(8,128)(2,1)S(1)}, u32[]{:S(2)}, u32[]{:S(2)}) %collective-permute-start.5) | collective-permute-done | bytes 262176 | tf_op jit(solution)/shard_map/ppermute | solution.py:557
  86.2 1.6 pack_blocks.5
  87.8 3.6 %collective-permute-start.12 = (bf16[2048,128]{1,0:T(8,128)(2,1)S(1)}, bf16[2048,128]{1,0:T(8,128)(2,1)S(1)}, u32[]{:S(2)}, u32[]{:S(2)}) collective-permute-start(bf16[2048,128]{1,0:T(8,128)(2,1)S(1)} %pack_blocks.5), channel_id=1, source_target_pairs={{0,4},{4,0},{8,12},{12,8},{16,20},{20,16},{24,28},{28,24},{1,5},{5... | collective-permute-start | bytes 1572872 | tf_op jit(solution)/shard_map/ppermute | solution.py:561
  91.4 2.0 collective-permute-start.9
  93.5 7.8 %collective-permute-done.12.refs_11_ = bf16[2048,128]{1,0:T(8,128)(2,1)S(1)} collective-permute-done((bf16[2048,128]{1,0:T(8,128)(2,1)S(1)}, bf16[2048,128]{1,0:T(8,128)(2,1)S(1)}, u32[]{:S(2)}, u32[]{:S(2)}) %collective-permute-start.12) | collective-permute-done | bytes 524320 | tf_op jit(solution)/shard_map/ppermute | solution.py:561
  102.1 39.1 %attend_head.2 = (bf16[1024,2048]{1,0:T(8,128)(2,1)}, bf16[1024,2048]{1,0:T(8,128)(2,1)}, f32[4096,128]{1,0:T(8,128)}, f32[4096,128]{1,0:T(8,128)}, bf16[2048,12...) custom-call(s32[88]{0:T(128)} %get-tuple-element.41.found.table, ...), custom_call_target="tpu_custom_call" | custom-call | bytes 1024 | tf_op jit(solution)/shard_map/attend_head/pallas_call | solution.py:529
  142.2 1.1 collective-permute-start.14
  143.3 1.3 collective-permute-start.15
  144.7 5.6 %collective-permute-done.15.refs_4_ = bf16[1536,128]{1,0:T(8,128)(2,1)S(1)} collective-permute-done((bf16[1536,128]{1,0:T(8,128)(2,1)}, bf16[1536,128]{1,0:T(8,128)(2,1)S(1)}, u32[]{:S(2)}, u32[]{:S(2)}) %collective-permute-start.15) | collective-permute-done | bytes 393248 | tf_op jit(solution)/shard_map/ppermute | solution.py:567
  150.3 6.1 %collective-permute-done.13.refs_2_ = bf16[2048,128]{1,0:T(8,128)(2,1)S(1)} collective-permute-done((bf16[2048,128]{1,0:T(8,128)(2,1)}, bf16[2048,128]{1,0:T(8,128)(2,1)S(1)}, u32[]{:S(2)}, u32[]{:S(2)}) %collective-permute-start.13) | collective-permute-done | bytes 524320 | tf_op jit(solution)/shard_map/ppermute | solution.py:561
  156.3 7.3 %collective-permute-done.14.refs_3_ = bf16[2048,128]{1,0:T(8,128)(2,1)S(1)} collective-permute-done((bf16[2048,128]{1,0:T(8,128)(2,1)}, bf16[2048,128]{1,0:T(8,128)(2,1)S(1)}, u32[]{:S(2)}, u32[]{:S(2)}) %collective-permute-start.14) | collective-permute-done | bytes 524320 | tf_op jit(solution)/shard_map/ppermute | solution.py:561
  164.4 5.6 %merge_terms.3 = (f32[2048,128]{1,0:T(8,128)}, bf16[2048,128]{1,0:T(8,128)(2,1)}, bf16[2048,128]{1,0:T(8,128)(2,1)}, bf16[2048,128]{1,0:T(8,128)(2,1)}) custom-call(s32[22]{0:T(128)} %get-tuple-element.49.walk, f32[4096,128]{1,0:T(8,128)} %get-tuple-element.52.refs_0_, f32[4096,128]{1,0:T(8,128)} %get-tuple-element.53.refs_1_, bf16[2048,128]{1,0:T(8,128)(2,1)} %copy-done.27, ...), custom_call_target="tpu_custom_call" | custom-call | bytes 1024 | tf_op jit(solution)/shard_map/merge_terms/pallas_call | solution.py:380
  170.0 3.7 %collective-permute-start.18 = (bf16[2048,128]{1,0:T(8,128)(2,1)}, bf16[2048,128]{1,0:T(8,128)(2,1)S(1)}, u32[]{:S(2)}, u32[]{:S(2)}) collective-permute-start(bf16[2048,128]{1,0:T(8,128)(2,1)} %get-tuple-element.62), channel_id=1, source_target_pairs={{0,8},{4,12},{8,16},{12,20},{16,24},{20,28},{24,0},{28,4},{1,9},{5... | collective-permute-start | bytes 1572872 | tf_op jit(solution)/shard_map/ppermute | solution.py:557
  173.7 2.4 collective-permute-start.16
  176.1 38.9 %attend_head.3 = (bf16[1024,2048]{1,0:T(8,128)(2,1)}, bf16[1024,2048]{1,0:T(8,128)(2,1)}, f32[4096,128]{1,0:T(8,128)}, f32[4096,128]{1,0:T(8,128)}, bf16[2048,12...) custom-call(s32[64]{0:T(128)} %get-tuple-element.40.found, ...), custom_call_target="tpu_custom_call", output_to_operand_aliasing={{0}: (9, {}), {1}: (10, {})} | custom-call | bytes 1024 | tf_op jit(solution)/shard_map/attend_head/pallas_call | solution.py:529
  215.0 2.4 collective-permute-start.19
  218.6 1.4 collective-permute-start.20
  220.1 9.2 %collective-permute-done.19.refs_1_ = bf16[2048,128]{1,0:T(8,128)(2,1)} collective-permute-done((bf16[2048,128]{1,0:T(8,128)(2,1)}, bf16[2048,128]{1,0:T(8,128)(2,1)}, u32[]{:S(2)}, u32[]{:S(2)}) %collective-permute-start.19) | collective-permute-done | bytes 524320 | tf_op jit(solution)/shard_map/ppermute | solution.py:561
  230.1 3.9 %merge_terms.4 = (f32[1024,128]{1,0:T(8,128)}, bf16[1024,128]{1,0:T(8,128)(2,1)}, bf16[1024,128]{1,0:T(8,128)(2,1)}, bf16[1024,128]{1,0:T(8,128)(2,1)}) custom-call(s32[22]{0:T(128)} %get-tuple-element.49.walk, f32[4096,128]{1,0:T(8,128)} %get-tuple-element.63.refs_0_, bf16[2048,128]{1,0:T(8,128)(2,1)} %collective-permute-done.19.refs_1_, ...), custom_call_target="tpu_custom_call" | custom-call | bytes 1024 | tf_op jit(solution)/shard_map/merge_terms/pallas_call | solution.py:380
  234.0 1.7 collective-permute-start.21
  235.7 6.0 %collective-permute-start.22 = (bf16[1024,128]{1,0:T(8,128)(2,1)}, bf16[1024,128]{1,0:T(8,128)(2,1)}, u32[]{:S(2)}, u32[]{:S(2)}) collective-permute-start(bf16[1024,128]{1,0:T(8,128)(2,1)} %get-tuple-element.68), channel_id=1, source_target_pairs={{0,16},{4,20},{8,24},{12,28},{16,0},{20,4},{24,8},{28,12},{1,17},{... | collective-permute-start | bytes 786440 | tf_op jit(solution)/shard_map/ppermute | solution.py:557
  242.8 3.5 %all-to-all-start.1 = ((bf16[4,2,256,128]{3,2,1,0:T(8,128)(2,1)}), bf16[4,2,256,128]{3,2,1,0:T(8,128)(2,1)S(1)}, u32[]{:S(2)}, u32[]{:S(2)}) async-start(bf16[4,2,256,128]{3,2,1,0:T(8,128)(2,1)} %bitcast.20), calls=%async_computation.1 | async-start | bytes 1048576 | tf_op jit(solution)/shard_map/all_to_all | solution.py:614
  246.3 3.8 %merge_terms.5 = (f32[1024,128]{1,0:T(8,128)}, bf16[1024,128]{1,0:T(8,128)(2,1)}, bf16[1024,128]{1,0:T(8,128)(2,1)}, bf16[1024,128]{1,0:T(8,128)(2,1)}) custom-call(s32[22]{0:T(128)} %get-tuple-element.49.walk, f32[4096,128]{1,0:T(8,128)} %get-tuple-element.70.refs_0_, bf16[2048,128]{1,0:T(8,128)(2,1)} %collective-permute-done.24.refs_1_, ...), custom_call_target="tpu_custom_call" | custom-call | bytes 1024 | tf_op jit(solution)/shard_map/merge_terms/pallas_call | solution.py:380
  250.1 3.8 %collective-permute-start.25 = (bf16[1024,128]{1,0:T(8,128)(2,1)}, bf16[1024,128]{1,0:T(8,128)(2,1)S(1)}, u32[]{:S(2)}, u32[]{:S(2)}) collective-permute-start(bf16[1024,128]{1,0:T(8,128)(2,1)} %get-tuple-element.73), channel_id=1, source_target_pairs={{0,24},{4,28},{8,0},{12,4},{16,8},{20,12},{24,16},{28,20},{1,25},{... | collective-permute-start | bytes 786440 | tf_op jit(solution)/shard_map/ppermute | solution.py:557
  254.5 1.5 collective-permute-done.22
  256.0 1.9 add_convert_fusion.2
  257.9 3.4 %all-to-all-start.2 = ((bf16[4,1,256,128]{3,2,1,0:T(8,128)(2,1)}), bf16[4,1,256,128]{3,2,1,0:T(8,128)(2,1)S(1)}, u32[]{:S(2)}, u32[]{:S(2)}) async-start(bf16[4,1,256,128]{3,2,1,0:T(8,128)(2,1)} %bitcast.5), calls=%async_computation.2 | async-start | bytes 524288 | tf_op jit(solution)/shard_map/all_to_all | solution.py:614
  261.3 15.9 %collective-permute-done.26 = bf16[1024,128]{1,0:T(8,128)(2,1)S(1)} collective-permute-done((bf16[1024,128]{1,0:T(8,128)(2,1)}, bf16[1024,128]{1,0:T(8,128)(2,1)S(1)}, u32[]{:S(2)}, u32[]{:S(2)}) %collective-permute-start.26) | collective-permute-done | bytes 262176 | tf_op jit(solution)/shard_map/ppermute | solution.py:557
  277.2 1.9 add_convert_fusion.1
  279.0 3.4 %all-to-all-start.3 = ((bf16[4,1,256,128]{3,2,1,0:T(8,128)(2,1)}), bf16[4,1,256,128]{3,2,1,0:T(8,128)(2,1)S(1)}, u32[]{:S(2)}, u32[]{:S(2)}) async-start(bf16[4,1,256,128]{3,2,1,0:T(8,128)(2,1)} %bitcast.11), calls=%async_computation.3 | async-start | bytes 524288 | tf_op jit(solution)/shard_map/all_to_all | solution.py:614
  283.0 1.0 copy.30
  284.0 4.4 %all-to-all-done.3 = bf16[4,1,256,128]{3,2,1,0:T(8,128)(2,1)S(1)} async-done(((bf16[4,1,256,128]{3,2,1,0:T(8,128)(2,1)}), bf16[4,1,256,128]{3,2,1,0:T(8,128)(2,1)S(1)}, u32[]{:S(2)}, u32[]{:S(2)}) %all-to-all-start.3) | async-done | bytes 262176 | tf_op jit(solution)/shard_map/all_to_all | solution.py:614
  (109 shorter events, 11.8 us)
Async XLA Ops:
  0.6 30.9 %copy-start.31 = (s32[64,3]{0,1:T(4,128)S(1)}, s32[64,3]{0,1:T(4,128)}, u32[]{:S(2)}) copy-start(s32[64,3]{0,1:T(4,128)} %param.9) | copy-start | bytes 2308
  24.6 59.8 %copy-start.1 = (bf16[2048,128]{1,0:T(8,128)(2,1)S(1)}, bf16[2048,128]{1,0:T(8,128)(2,1)}, u32[]{:S(2)}) copy-start(bf16[2048,128]{1,0:T(8,128)(2,1)} %get-tuple-element.42.refs_0_.refs_5_.refs_2_) | copy-start | bytes 1572868
  24.6 27.8 %collective-permute-start = (bf16[2048,128]{1,0:T(8,128)(2,1)}, bf16[2048,128]{1,0:T(8,128)(2,1)S(1)}, u32[]{:S(2)}, u32[]{:S(2)}) collective-permute-start(bf16[2048,128]{1,0:T(8,128)(2,1)} %get-tuple-element.42.refs_0_.refs_5_.refs_2_), channel_id=1, source_target_pairs={{0,4},{4,0},{8,12},{12,8},{16,20},{20,16},{24,28},{28,24},{1,5},{5... | collective-permute-start | bytes 1572872 | tf_op jit(solution)/shard_map/ppermute | solution.py:561
  26.9 10.7 %collective-permute-start.3 = (bf16[1024,128]{1,0:T(8,128)(2,1)}, bf16[1024,128]{1,0:T(8,128)(2,1)S(1)}, u32[]{:S(2)}, u32[]{:S(2)}) collective-permute-start(bf16[1024,128]{1,0:T(8,128)(2,1)} %get-tuple-element.44.refs_0_.refs_2_), channel_id=1, source_target_pairs={{0,24},{4,28},{8,0},{12,4},{16,8},{20,12},{24,16},{28,20},{1,25},{... | collective-permute-start | bytes 786440 | tf_op jit(solution)/shard_map/ppermute | solution.py:557
  30.5 21.9 %collective-permute-start.2 = (bf16[1024,128]{1,0:T(8,128)(2,1)}, bf16[1024,128]{1,0:T(8,128)(2,1)S(1)}, u32[]{:S(2)}, u32[]{:S(2)}) collective-permute-start(bf16[1024,128]{1,0:T(8,128)(2,1)} %get-tuple-element.44.refs_0_.refs_2_), channel_id=1, source_target_pairs={{0,16},{4,20},{8,24},{12,28},{16,0},{20,4},{24,8},{28,12},{1,17},{... | collective-permute-start | bytes 786440 | tf_op jit(solution)/shard_map/ppermute | solution.py:557
  30.5 21.9 %collective-permute-start.1 = (bf16[1024,128]{1,0:T(8,128)(2,1)}, bf16[1024,128]{1,0:T(8,128)(2,1)S(1)}, u32[]{:S(2)}, u32[]{:S(2)}) collective-permute-start(bf16[1024,128]{1,0:T(8,128)(2,1)} %get-tuple-element.44.refs_0_.refs_2_), channel_id=1, source_target_pairs={{0,8},{4,12},{8,16},{12,20},{16,24},{20,28},{24,0},{28,4},{1,9},{5... | collective-permute-start | bytes 786440 | tf_op jit(solution)/shard_map/ppermute | solution.py:557
  37.6 50.1 %copy-start.2 = (bf16[1024,128]{1,0:T(8,128)(2,1)}, bf16[1024,128]{1,0:T(8,128)(2,1)S(1)}, u32[]{:S(2)}) copy-start(bf16[1024,128]{1,0:T(8,128)(2,1)S(1)} %collective-permute-done.3.refs_4_.refs_3_.refs_5_) | copy-start | bytes 786436
  52.4 35.4 %copy-start.3 = (bf16[1024,128]{1,0:T(8,128)(2,1)}, bf16[1024,128]{1,0:T(8,128)(2,1)S(1)}, u32[]{:S(2)}) copy-start(bf16[1024,128]{1,0:T(8,128)(2,1)S(1)} %collective-permute-done.2.refs_3_.refs_2_.refs_4_) | copy-start | bytes 786436
  52.4 35.4 %copy-start.4 = (bf16[1024,128]{1,0:T(8,128)(2,1)}, bf16[1024,128]{1,0:T(8,128)(2,1)S(1)}, u32[]{:S(2)}) copy-start(bf16[1024,128]{1,0:T(8,128)(2,1)S(1)} %collective-permute-done.1.refs_2_.refs_1_.refs_3_) | copy-start | bytes 786436
  52.4 35.4 %copy-start = (bf16[2048,128]{1,0:T(8,128)(2,1)}, bf16[2048,128]{1,0:T(8,128)(2,1)S(1)}, u32[]{:S(2)}) copy-start(bf16[2048,128]{1,0:T(8,128)(2,1)S(1)} %collective-permute-done.refs_1_.refs_4_.refs_6_.refs_3_) | copy-start | bytes 1572868
  54.2 32.0 %copy-start.13 = (s32[22]{0:T(128)S(1)}, s32[22]{0:T(128)}, u32[]{:S(2)}) copy-start(s32[22]{0:T(128)} %get-tuple-element.49.walk) | copy-start | bytes 268
  55.6 30.5 %collective-permute-start.10 = (bf16[2048,128]{1,0:T(8,128)(2,1)}, bf16[2048,128]{1,0:T(8,128)(2,1)S(1)}, u32[]{:S(2)}, u32[]{:S(2)}) collective-permute-start(bf16[2048,128]{1,0:T(8,128)(2,1)} %pack_blocks.3), channel_id=1, source_target_pairs={{0,4},{4,0},{8,12},{12,8},{16,20},{20,16},{24,28},{28,24},{1,5},{5... | collective-permute-start | bytes 1572872 | tf_op jit(solution)/shard_map/ppermute | solution.py:561
  58.5 27.6 %collective-permute-start.11 = (bf16[1536,128]{1,0:T(8,128)(2,1)}, bf16[1536,128]{1,0:T(8,128)(2,1)S(1)}, u32[]{:S(2)}, u32[]{:S(2)}) collective-permute-start(bf16[1536,128]{1,0:T(8,128)(2,1)} %pack_blocks.4), channel_id=1, source_target_pairs={{12,0},{13,1},{14,2},{15,3}} | collective-permute-start | bytes 1179656 | tf_op jit(solution)/shard_map/ppermute | solution.py:567
  59.8 9.0 %collective-permute-start.6 = (bf16[1024,128]{1,0:T(8,128)(2,1)}, bf16[1024,128]{1,0:T(8,128)(2,1)S(1)}, u32[]{:S(2)}, u32[]{:S(2)}) collective-permute-start(bf16[1024,128]{1,0:T(8,128)(2,1)} %get-tuple-element.45.refs_1_.refs_0_.refs_6_), channel_id=1, source_target_pairs={{0,24},{4,28},{8,0},{12,4},{16,8},{20,12},{24,16},{28,20},{1,25},{... | collective-permute-start | bytes 786440 | tf_op jit(solution)/shard_map/ppermute | solution.py:557
  59.9 24.6 %collective-permute-start.5 = (bf16[1024,128]{1,0:T(8,128)(2,1)}, bf16[1024,128]{1,0:T(8,128)(2,1)S(1)}, u32[]{:S(2)}, u32[]{:S(2)}) collective-permute-start(bf16[1024,128]{1,0:T(8,128)(2,1)} %get-tuple-element.45.refs_1_.refs_0_.refs_6_), channel_id=1, source_target_pairs={{0,16},{4,20},{8,24},{12,28},{16,0},{20,4},{24,8},{28,12},{1,17},{... | collective-permute-start | bytes 786440 | tf_op jit(solution)/shard_map/ppermute | solution.py:557
  62.1 22.4 %collective-permute-start.4 = (bf16[1024,128]{1,0:T(8,128)(2,1)}, bf16[1024,128]{1,0:T(8,128)(2,1)S(1)}, u32[]{:S(2)}, u32[]{:S(2)}) collective-permute-start(bf16[1024,128]{1,0:T(8,128)(2,1)} %get-tuple-element.45.refs_1_.refs_0_.refs_6_), channel_id=1, source_target_pairs={{0,8},{4,12},{8,16},{12,20},{16,24},{20,28},{24,0},{28,4},{1,9},{5... | collective-permute-start | bytes 786440 | tf_op jit(solution)/shard_map/ppermute | solution.py:557
  68.8 33.3 %copy-start.6 = (bf16[1024,128]{1,0:T(8,128)(2,1)}, bf16[1024,128]{1,0:T(8,128)(2,1)S(1)}, u32[]{:S(2)}) copy-start(bf16[1024,128]{1,0:T(8,128)(2,1)S(1)} %collective-permute-done.6.refs_7_.refs_3_.refs_9_) | copy-start | bytes 786436
  84.5 17.6 %copy-start.7 = (bf16[1024,128]{1,0:T(8,128)(2,1)}, bf16[1024,128]{1,0:T(8,128)(2,1)S(1)}, u32[]{:S(2)}) copy-start(bf16[1024,128]{1,0:T(8,128)(2,1)S(1)} %collective-permute-done.5.refs_6_.refs_2_.refs_8_) | copy-start | bytes 786436
  86.1 57.2 %collective-permute-start.8 = (bf16[3072,128]{1,0:T(8,128)(2,1)S(1)}, bf16[3072,128]{1,0:T(8,128)(2,1)S(1)}, u32[]{:S(2)}, u32[]{:S(2)}) collective-permute-start(bf16[3072,128]{1,0:T(8,128)(2,1)S(1)} %get-tuple-element.47), channel_id=1, source_target_pairs={{0,16},{4,20},{8,24},{12,28},{16,0},{20,4},{24,8},{28,12},{1,17},{... | collective-permute-start | bytes 2359304 | tf_op jit(solution)/shard_map/ppermute | solution.py:557
  87.8 13.4 %collective-permute-start.12 = (bf16[2048,128]{1,0:T(8,128)(2,1)S(1)}, bf16[2048,128]{1,0:T(8,128)(2,1)S(1)}, u32[]{:S(2)}, u32[]{:S(2)}) collective-permute-start(bf16[2048,128]{1,0:T(8,128)(2,1)S(1)} %pack_blocks.5), channel_id=1, source_target_pairs={{0,4},{4,0},{8,12},{12,8},{16,20},{20,16},{24,28},{28,24},{1,5},{5... | collective-permute-start | bytes 1572872 | tf_op jit(solution)/shard_map/ppermute | solution.py:561
  91.4 53.2 %collective-permute-start.9 = (bf16[3072,128]{1,0:T(8,128)(2,1)S(1)}, bf16[3072,128]{1,0:T(8,128)(2,1)S(1)}, u32[]{:S(2)}, u32[]{:S(2)}) collective-permute-start(bf16[3072,128]{1,0:T(8,128)(2,1)S(1)} %get-tuple-element.48), channel_id=1, source_target_pairs={{0,24},{4,28},{8,0},{12,4},{16,8},{20,12},{24,16},{28,20},{1,25},{... | collective-permute-start | bytes 2359304 | tf_op jit(solution)/shard_map/ppermute | solution.py:557
  93.4 51.2 %collective-permute-start.7 = (bf16[3072,128]{1,0:T(8,128)(2,1)S(1)}, bf16[3072,128]{1,0:T(8,128)(2,1)S(1)}, u32[]{:S(2)}, u32[]{:S(2)}) collective-permute-start(bf16[3072,128]{1,0:T(8,128)(2,1)S(1)} %get-tuple-element.46.refs_13_), channel_id=1, source_target_pairs={{0,8},{4,12},{8,16},{12,20},{16,24},{20,28},{24,0},{28,4},{1,9},{5... | collective-permute-start | bytes 2359304 | tf_op jit(solution)/shard_map/ppermute | solution.py:557
  141.2 15.1 %collective-permute-start.13 = (bf16[2048,128]{1,0:T(8,128)(2,1)}, bf16[2048,128]{1,0:T(8,128)(2,1)S(1)}, u32[]{:S(2)}, u32[]{:S(2)}) collective-permute-start(bf16[2048,128]{1,0:T(8,128)(2,1)} %get-tuple-element.54), channel_id=1, source_target_pairs={{0,4},{4,0},{8,12},{12,8},{16,20},{20,16},{24,28},{28,24},{1,5},{5... | collective-permute-start | bytes 1572872 | tf_op jit(solution)/shard_map/ppermute | solution.py:561
  142.2 21.4 %collective-permute-start.14 = (bf16[2048,128]{1,0:T(8,128)(2,1)}, bf16[2048,128]{1,0:T(8,128)(2,1)S(1)}, u32[]{:S(2)}, u32[]{:S(2)}) collective-permute-start(bf16[2048,128]{1,0:T(8,128)(2,1)} %get-tuple-element.55), channel_id=1, source_target_pairs={{0,4},{4,0},{8,12},{12,8},{16,20},{20,16},{24,28},{28,24},{1,5},{5... | collective-permute-start | bytes 1572872 | tf_op jit(solution)/shard_map/ppermute | solution.py:561
  143.3 20.3 %copy-start.21 = (bf16[3072,128]{1,0:T(8,128)(2,1)}, bf16[3072,128]{1,0:T(8,128)(2,1)S(1)}, u32[]{:S(2)}) copy-start(bf16[3072,128]{1,0:T(8,128)(2,1)S(1)} %collective-permute-done.8.refs_8_.refs_5_) | copy-start | bytes 2359300
  143.3 7.0 %collective-permute-start.15 = (bf16[1536,128]{1,0:T(8,128)(2,1)}, bf16[1536,128]{1,0:T(8,128)(2,1)S(1)}, u32[]{:S(2)}, u32[]{:S(2)}) collective-permute-start(bf16[1536,128]{1,0:T(8,128)(2,1)} %get-tuple-element.56), channel_id=1, source_target_pairs={{0,12},{1,13},{2,14},{3,15}} | collective-permute-start | bytes 1179656 | tf_op jit(solution)/shard_map/ppermute | solution.py:567
  144.6 19.0 %copy-start.22 = (bf16[3072,128]{1,0:T(8,128)(2,1)}, bf16[3072,128]{1,0:T(8,128)(2,1)S(1)}, u32[]{:S(2)}) copy-start(bf16[3072,128]{1,0:T(8,128)(2,1)S(1)} %collective-permute-done.9.refs_9_.refs_6_) | copy-start | bytes 2359300
  144.6 19.0 %copy-start.23 = (bf16[3072,128]{1,0:T(8,128)(2,1)}, bf16[3072,128]{1,0:T(8,128)(2,1)S(1)}, u32[]{:S(2)}) copy-start(bf16[3072,128]{1,0:T(8,128)(2,1)S(1)} %collective-permute-done.7.refs_7_.refs_4_) | copy-start | bytes 2359300
  170.0 47.5 %collective-permute-start.17 = (bf16[2048,128]{1,0:T(8,128)(2,1)}, bf16[2048,128]{1,0:T(8,128)(2,1)S(1)}, u32[]{:S(2)}, u32[]{:S(2)}) collective-permute-start(bf16[2048,128]{1,0:T(8,128)(2,1)} %get-tuple-element.61), channel_id=1, source_target_pairs={{0,16},{4,20},{8,24},{12,28},{16,0},{20,4},{24,8},{28,12},{1,17},{... | collective-permute-start | bytes 1572872 | tf_op jit(solution)/shard_map/ppermute | solution.py:557
  170.0 47.5 %collective-permute-start.18 = (bf16[2048,128]{1,0:T(8,128)(2,1)}, bf16[2048,128]{1,0:T(8,128)(2,1)S(1)}, u32[]{:S(2)}, u32[]{:S(2)}) collective-permute-start(bf16[2048,128]{1,0:T(8,128)(2,1)} %get-tuple-element.62), channel_id=1, source_target_pairs={{0,8},{4,12},{8,16},{12,20},{16,24},{20,28},{24,0},{28,4},{1,9},{5... | collective-permute-start | bytes 1572872 | tf_op jit(solution)/shard_map/ppermute | solution.py:557
  173.7 43.8 %collective-permute-start.16 = (bf16[2048,128]{1,0:T(8,128)(2,1)}, bf16[2048,128]{1,0:T(8,128)(2,1)S(1)}, u32[]{:S(2)}, u32[]{:S(2)}) collective-permute-start(bf16[2048,128]{1,0:T(8,128)(2,1)} %get-tuple-element.57.refs_9_), channel_id=1, source_target_pairs={{0,24},{4,28},{8,0},{12,4},{16,8},{20,12},{24,16},{28,20},{1,25},{... | collective-permute-start | bytes 1572872 | tf_op jit(solution)/shard_map/ppermute | solution.py:557
  215.0 26.7 %copy-start.25 = (f32[2048,128]{1,0:T(8,128)S(1)}, f32[2048,128]{1,0:T(8,128)}, u32[]{:S(2)}) copy-start(f32[2048,128]{1,0:T(8,128)} %get-tuple-element.60) | copy-start | bytes 3145732
  215.0 14.3 %collective-permute-start.19 = (bf16[2048,128]{1,0:T(8,128)(2,1)}, bf16[2048,128]{1,0:T(8,128)(2,1)}, u32[]{:S(2)}, u32[]{:S(2)}) collective-permute-start(bf16[2048,128]{1,0:T(8,128)(2,1)} %get-tuple-element.64), channel_id=1, source_target_pairs={{0,4},{4,0},{8,12},{12,8},{16,20},{20,16},{24,28},{28,24},{1,5},{5... | collective-permute-start | bytes 1572872 | tf_op jit(solution)/shard_map/ppermute | solution.py:561
  218.6 23.1 %copy-start.16 = (bf16[2048,128]{1,0:T(8,128)(2,1)S(1)}, bf16[2048,128]{1,0:T(8,128)(2,1)}, u32[]{:S(2)}) copy-start(bf16[2048,128]{1,0:T(8,128)(2,1)} %copy-done.15) | copy-start | bytes 1572868
  218.6 23.1 %copy-start.18 = (bf16[2048,128]{1,0:T(8,128)(2,1)S(1)}, bf16[2048,128]{1,0:T(8,128)(2,1)}, u32[]{:S(2)}) copy-start(bf16[2048,128]{1,0:T(8,128)(2,1)} %copy-done.17) | copy-start | bytes 1572868
  218.6 23.1 %copy-start.20 = (bf16[2048,128]{1,0:T(8,128)(2,1)S(1)}, bf16[2048,128]{1,0:T(8,128)(2,1)}, u32[]{:S(2)}) copy-start(bf16[2048,128]{1,0:T(8,128)(2,1)} %copy-done.19) | copy-start | bytes 1572868
  218.6 10.7 %collective-permute-start.20 = (bf16[1536,128]{1,0:T(8,128)(2,1)}, bf16[1536,128]{1,0:T(8,128)(2,1)S(1)}, u32[]{:S(2)}, u32[]{:S(2)}) collective-permute-start(bf16[1536,128]{1,0:T(8,128)(2,1)} %gate.2), channel_id=1, source_target_pairs={{0,12},{1,13},{2,14},{3,15}} | collective-permute-start | bytes 1179656 | tf_op jit(solution)/shard_map/ppermute | solution.py:567
  220.1 26.2 %collective-permute-start.24 = (bf16[2048,128]{1,0:T(8,128)(2,1)}, bf16[2048,128]{1,0:T(8,128)(2,1)}, u32[]{:S(2)}, u32[]{:S(2)}) collective-permute-start(bf16[2048,128]{1,0:T(8,128)(2,1)} %gate.3), channel_id=1, source_target_pairs={{0,4},{4,0},{8,12},{12,8},{16,20},{20,16},{24,28},{28,24},{1,5},{5... | collective-permute-start | bytes 1572872 | tf_op jit(solution)/shard_map/ppermute | solution.py:561
  234.0 22.0 %copy-start.26 = (f32[1024,128]{1,0:T(8,128)S(1)}, f32[1024,128]{1,0:T(8,128)}, u32[]{:S(2)}) copy-start(f32[1024,128]{1,0:T(8,128)} %get-tuple-element.66) | copy-start | bytes 1572868
  234.0 20.0 %collective-permute-start.21 = (bf16[1024,128]{1,0:T(8,128)(2,1)}, bf16[1024,128]{1,0:T(8,128)(2,1)S(1)}, u32[]{:S(2)}, u32[]{:S(2)}) collective-permute-start(bf16[1024,128]{1,0:T(8,128)(2,1)} %get-tuple-element.67), channel_id=1, source_target_pairs={{0,24},{4,28},{8,0},{12,4},{16,8},{20,12},{24,16},{28,20},{1,25},{... | collective-permute-start | bytes 786440 | tf_op jit(solution)/shard_map/ppermute | solution.py:557
  235.7 20.3 %collective-permute-start.22 = (bf16[1024,128]{1,0:T(8,128)(2,1)}, bf16[1024,128]{1,0:T(8,128)(2,1)}, u32[]{:S(2)}, u32[]{:S(2)}) collective-permute-start(bf16[1024,128]{1,0:T(8,128)(2,1)} %get-tuple-element.68), channel_id=1, source_target_pairs={{0,16},{4,20},{8,24},{12,28},{16,0},{20,4},{24,8},{28,12},{1,17},{... | collective-permute-start | bytes 786440 | tf_op jit(solution)/shard_map/ppermute | solution.py:557
  241.7 14.3 %collective-permute-start.23 = (bf16[1024,128]{1,0:T(8,128)(2,1)}, bf16[1024,128]{1,0:T(8,128)(2,1)}, u32[]{:S(2)}, u32[]{:S(2)}) collective-permute-start(bf16[1024,128]{1,0:T(8,128)(2,1)} %get-tuple-element.69), channel_id=1, source_target_pairs={{0,8},{4,12},{8,16},{12,20},{16,24},{20,28},{24,0},{28,4},{1,9},{5... | collective-permute-start | bytes 786440 | tf_op jit(solution)/shard_map/ppermute | solution.py:557
  242.8 15.1 %all-to-all-start.1 = ((bf16[4,2,256,128]{3,2,1,0:T(8,128)(2,1)}), bf16[4,2,256,128]{3,2,1,0:T(8,128)(2,1)S(1)}, u32[]{:S(2)}, u32[]{:S(2)}) async-start(bf16[4,2,256,128]{3,2,1,0:T(8,128)(2,1)} %bitcast.20), calls=%async_computation.1 | async-start | bytes 1048576 | tf_op jit(solution)/shard_map/all_to_all | solution.py:614
  250.1 11.2 %collective-permute-start.25 = (bf16[1024,128]{1,0:T(8,128)(2,1)}, bf16[1024,128]{1,0:T(8,128)(2,1)S(1)}, u32[]{:S(2)}, u32[]{:S(2)}) collective-permute-start(bf16[1024,128]{1,0:T(8,128)(2,1)} %get-tuple-element.73), channel_id=1, source_target_pairs={{0,24},{4,28},{8,0},{12,4},{16,8},{20,12},{24,16},{28,20},{1,25},{... | collective-permute-start | bytes 786440 | tf_op jit(solution)/shard_map/ppermute | solution.py:557
  253.9 23.2 %collective-permute-start.26 = (bf16[1024,128]{1,0:T(8,128)(2,1)}, bf16[1024,128]{1,0:T(8,128)(2,1)S(1)}, u32[]{:S(2)}, u32[]{:S(2)}) collective-permute-start(bf16[1024,128]{1,0:T(8,128)(2,1)} %get-tuple-element.74), channel_id=1, source_target_pairs={{0,16},{4,20},{8,24},{12,28},{16,0},{20,4},{24,8},{28,12},{1,17},{... | collective-permute-start | bytes 786440 | tf_op jit(solution)/shard_map/ppermute | solution.py:557
  253.9 23.2 %collective-permute-start.27 = (bf16[1024,128]{1,0:T(8,128)(2,1)}, bf16[1024,128]{1,0:T(8,128)(2,1)S(1)}, u32[]{:S(2)}, u32[]{:S(2)}) collective-permute-start(bf16[1024,128]{1,0:T(8,128)(2,1)} %get-tuple-element.75), channel_id=1, source_target_pairs={{0,8},{4,12},{8,16},{12,20},{16,24},{20,28},{24,0},{28,4},{1,9},{5... | collective-permute-start | bytes 786440 | tf_op jit(solution)/shard_map/ppermute | solution.py:557
  257.9 21.2 %all-to-all-start.2 = ((bf16[4,1,256,128]{3,2,1,0:T(8,128)(2,1)}), bf16[4,1,256,128]{3,2,1,0:T(8,128)(2,1)S(1)}, u32[]{:S(2)}, u32[]{:S(2)}) async-start(bf16[4,1,256,128]{3,2,1,0:T(8,128)(2,1)} %bitcast.5), calls=%async_computation.2 | async-start | bytes 524288 | tf_op jit(solution)/shard_map/all_to_all | solution.py:614
  279.0 9.4 %all-to-all-start.3 = ((bf16[4,1,256,128]{3,2,1,0:T(8,128)(2,1)}), bf16[4,1,256,128]{3,2,1,0:T(8,128)(2,1)S(1)}, u32[]{:S(2)}, u32[]{:S(2)}) async-start(bf16[4,1,256,128]{3,2,1,0:T(8,128)(2,1)} %bitcast.11), calls=%async_computation.3 | async-start | bytes 524288 | tf_op jit(solution)/shard_map/all_to_all | solution.py:614
  (15 other events, 93.8 us)

commit v4 on v3

--- a/solution.py
+++ b/solution.py
@@ -357,7 +357,7 @@
     direct = refs[0]
     outs, total = refs[-1 - plan.depth : -1], refs[-1]
     for t in range(halves):
-        total[...] = columns[t][...]
+        total[...] = columns[t][...].astype(jnp.float32)
 
         def add(given, slots, first, base):
             for slot in range(slots):
@@ -400,10 +400,10 @@
     parts, refs = refs[2 : 2 + given], refs[2 + given :]
     before = refs[: 2 if first else 0]
     if ends:
-        refs = refs[-(12 + (2 if split else 1) * (plan.lanes - 1) + (plan.direct is not None)) :]
-        o_ref, dq_ref, dk_col, dv_col = refs[:4]
-        packed, refs = refs[4:-8], refs[-8:]
-        kpool, vpool, keys, values, dk_sum, dv_sum, dk_far, dv_far = refs
+        refs = refs[-(14 + (2 if split else 1) * (plan.lanes - 1) + (plan.direct is not None)) :]
+        o_ref, dq_ref, dk_out, dv_out = refs[:4]
+        packed, refs = refs[4:-10], refs[-10:]
+        kpool, vpool, keys, values, dk_sum, dv_sum, dk_far, dv_far, dk_col, dv_col = refs
     else:
         o_ref, dq_ref, dk_sum, dv_sum, kpool, vpool, keys, values = refs[-8:]
     n = pl.program_id(0)
@@ -485,6 +485,8 @@
 
     @pl.when(i == plan.qb - 1)
     def _():
+        dk_out[...] = dk_col[...].astype(jnp.bfloat16)
+        dv_out[...] = dv_col[...].astype(jnp.bfloat16)
         size = plan.slots * BLK
         for t in range(plan.lanes - 1):
             part = slice(t * size, (t + 1) * size)
@@ -515,7 +517,8 @@
     shape = lambda blocks, kind: jax.ShapeDtypeStruct((blocks * BLK, HD), kind)
     o_shape = jax.ShapeDtypeStruct(queries.shape, jnp.bfloat16)
     ends = first + count == plan.qb
-    out_shape = [o_shape, o_shape] + [shape(plan.own if ends else count * plan.sel, jnp.float32)] * 2
+    term_shape = shape(plan.own, jnp.bfloat16) if ends else shape(count * plan.sel, jnp.float32)
+    out_shape = [o_shape, o_shape, term_shape, term_shape]
     if ends:
         out_shape += [shape((1 if split else 2) * plan.slots, jnp.bfloat16)] * ((2 if split else 1) * (plan.lanes - 1))
     if ends and plan.direct is not None:
@@ -538,7 +541,7 @@
             out_specs=[q_spec, q_spec] + ([whole(s) for s in out_shape[2:]] if ends else [term_spec] * 2),
             scratch_shapes=[pool] * 2
             + [listed, listed]
-            + ([listed_sum, listed_sum] + [pltpu.VMEM((plan.far * BLK, HD), jnp.float32)] * 2 if ends else []),
+            + ([listed_sum, listed_sum] + [pltpu.VMEM((blocks * BLK, HD), jnp.float32) for blocks in (plan.far, plan.far, plan.own, plan.own)] if ends else []),
         ),
         out_shape=out_shape,
         input_output_aliases=aliases,

time: 291 us -> 289 us (level)
  Pallas kernels: 110 us -> 107 us
  transfers between devices with their start and end apart: 31 -> 31, of which waited for: 11 -> 11; matrix products, arithmetic and copies ran while one was open for 2% -> 2% of each run, Pallas kernels for 34% -> 33%
where the time goes in v4:
time: 289 us; the launch traced here: 288 us
  Pallas kernels  107 us (37%)
  waiting for transfers between devices  91.1 us (32%)
  starting transfers between devices  54.8 us (19%)
  blocking collectives  19.4 us (7%)
  local copies, waits for them, and re-layouts  10.3 us (4%)
  other arithmetic  4.06 us (1%)
    pallas_call x2, Pallas kernels, attend(): pl.pallas_call(functools.partial(attend_kernel, plan=plan, qpk=qpk, per=4...  77 us
    ppermute x18, waiting for transfers between devices, column_shift(): lax.ppermute(array, 'ctx', [(n, (n + rows * plan.lanes) % plan.ctx) for n...  50.7 us
    ppermute x7, waiting for transfers between devices, row_shift(): lax.ppermute(array, 'ctx', [(n, n - n % plan.lanes + (n + lanes) % plan.l...  30.3 us
    ppermute x18, starting transfers between devices, column_shift(): lax.ppermute(array, 'ctx', [(n, (n + rows * plan.lanes) % plan.ctx) for n...  29.4 us
    all_to_all x1, blocking collectives, to_heads(): lax.all_to_all(parts, 'kvh', split_axis=0, concat_axis=0, tiled=True)  19.4 us
    pallas_call x3, Pallas kernels, merge(): pl.pallas_call(functools.partial(merge_kernel, plan=plan, halves=halves,...  12.1 us
    ppermute x7, starting transfers between devices, row_shift(): lax.ppermute(array, 'ctx', [(n, n - n % plan.lanes + (n + lanes) % plan.l...  11.1 us
    all_to_all x3, starting transfers between devices, to_tokens(): lax.all_to_all(parts, 'kvh', split_axis=0, concat_axis=0, tiled=True)  10.3 us
  transfers between devices with their start and end apart: 31, of which 11 were waited for; matrix products, arithmetic and copies ran while one was open for 2% of the time, Pallas kernels for 33%

profile of v4, /device:TPU:0, one launch (start us, length us, event | category | flops | bytes accessed | tf_op | source)
XLA Modules:
  0.0 288.2 jit_solution(17219360874384267238)
XLA Ops:
  0.6 2.4 cut_heads.1
  3.0 19.4 %all_to_all.20.parts = bf16[4,4,256,128]{3,2,1,0:T(8,128)(2,1)} all-to-all(bf16[4,4,256,128]{3,2,1,0:T(8,128)(2,1)} %cut_heads.1), channel_id=1, replica_groups=mesh['ctx'=8,'kvh'=4] {'kvh'}, dimensions={0} | all-to-all | bytes 2097152 | tf_op jit(solution)/shard_map/all_to_all | solution.py:602
  22.4 2.2 join_heads.1
  24.6 2.3 collective-permute-start
  26.9 3.6 %collective-permute-start.3 = (bf16[1024,128]{1,0:T(8,128)(2,1)}, bf16[1024,128]{1,0:T(8,128)(2,1)S(1)}, u32[]{:S(2)}, u32[]{:S(2)}) collective-permute-start(bf16[1024,128]{1,0:T(8,128)(2,1)} %get-tuple-element.44.refs_0_.refs_2_), channel_id=1, source_target_pairs={{0,24},{4,28},{8,0},{12,4},{16,8},{20,12},{24,16},{28,20},{1,25},{... | collective-permute-start | bytes 786440 | tf_op jit(solution)/shard_map/ppermute | solution.py:560
  30.5 1.0 collective-permute-start.1
  32.4 2.7 list_tables.1
  35.1 2.6 collective-permute-done.3.refs_4_.refs_3_.refs_5_
  37.7 14.8 %collective-permute-done.2.refs_3_.refs_2_.refs_4_ = bf16[1024,128]{1,0:T(8,128)(2,1)S(1)} collective-permute-done((bf16[1024,128]{1,0:T(8,128)(2,1)}, bf16[1024,128]{1,0:T(8,128)(2,1)S(1)}, u32[]{:S(2)}, u32[]{:S(2)}) %collective-permute-start.2) | collective-permute-done | bytes 262176 | tf_op jit(solution)/shard_map/ppermute | solution.py:560
  52.4 1.1 copy-done.5
  54.3 1.4 pack_blocks.3
  56.2 2.3 pack_blocks.4
  58.6 1.3 collective-permute-start.11
  59.9 2.2 collective-permute-start.5
  62.1 1.9 collective-permute-start.4
  64.1 4.8 %row_tables.1 = (s32[64]{0:T(128)}, s32[36]{0:T(128)}) custom-call(s32[1]{0:T(128)} %bitcast.where, s32[192]{0:T(256)} %reshape.25.named), custom_call_target="tpu_custom_call" | custom-call | bytes 1024 | tf_op jit(solution)/shard_map/row_tables/pallas_call | solution.py:246
  68.9 15.6 %collective-permute-done.5.refs_6_.refs_2_.refs_8_ = bf16[1024,128]{1,0:T(8,128)(2,1)S(1)} collective-permute-done((bf16[1024,128]{1,0:T(8,128)(2,1)}, bf16[1024,128]{1,0:T(8,128)(2,1)S(1)}, u32[]{:S(2)}, u32[]{:S(2)}) %collective-permute-start.5) | collective-permute-done | bytes 262176 | tf_op jit(solution)/shard_map/ppermute | solution.py:560
  86.2 1.6 pack_blocks.5
  87.8 3.6 %collective-permute-start.12 = (bf16[2048,128]{1,0:T(8,128)(2,1)S(1)}, bf16[2048,128]{1,0:T(8,128)(2,1)S(1)}, u32[]{:S(2)}, u32[]{:S(2)}) collective-permute-start(bf16[2048,128]{1,0:T(8,128)(2,1)S(1)} %pack_blocks.5), channel_id=1, source_target_pairs={{0,4},{4,0},{8,12},{12,8},{16,20},{20,16},{24,28},{28,24},{1,5},{5... | collective-permute-start | bytes 1572872 | tf_op jit(solution)/shard_map/ppermute | solution.py:564
  91.4 2.0 collective-permute-start.9
  93.5 7.8 %collective-permute-done.12.refs_11_ = bf16[2048,128]{1,0:T(8,128)(2,1)S(1)} collective-permute-done((bf16[2048,128]{1,0:T(8,128)(2,1)S(1)}, bf16[2048,128]{1,0:T(8,128)(2,1)S(1)}, u32[]{:S(2)}, u32[]{:S(2)}) %collective-permute-start.12) | collective-permute-done | bytes 524320 | tf_op jit(solution)/shard_map/ppermute | solution.py:564
  102.1 38.6 %attend_head.2 = (bf16[1024,2048]{1,0:T(8,128)(2,1)}, bf16[1024,2048]{1,0:T(8,128)(2,1)}, bf16[4096,128]{1,0:T(8,128)(2,1)}, bf16[4096,128]{1,0:T(8,128)(2,1)}, ...) custom-call(s32[88]{0:T(128)} %get-tuple-element.41.found.table, ...), custom_call_target="tpu_custom_call" | custom-call | bytes 1024 | tf_op jit(solution)/shard_map/attend_head/pallas_call | solution.py:532
  141.7 1.1 collective-permute-start.14
  142.8 1.3 collective-permute-start.15
  144.1 5.6 %collective-permute-done.15.refs_4_ = bf16[1536,128]{1,0:T(8,128)(2,1)S(1)} collective-permute-done((bf16[1536,128]{1,0:T(8,128)(2,1)}, bf16[1536,128]{1,0:T(8,128)(2,1)S(1)}, u32[]{:S(2)}, u32[]{:S(2)}) %collective-permute-start.15) | collective-permute-done | bytes 393248 | tf_op jit(solution)/shard_map/ppermute | solution.py:570
  149.8 6.1 %collective-permute-done.13.refs_2_ = bf16[2048,128]{1,0:T(8,128)(2,1)S(1)} collective-permute-done((bf16[2048,128]{1,0:T(8,128)(2,1)}, bf16[2048,128]{1,0:T(8,128)(2,1)S(1)}, u32[]{:S(2)}, u32[]{:S(2)}) %collective-permute-start.13) | collective-permute-done | bytes 524320 | tf_op jit(solution)/shard_map/ppermute | solution.py:564
  155.8 7.3 %collective-permute-done.14.refs_3_ = bf16[2048,128]{1,0:T(8,128)(2,1)S(1)} collective-permute-done((bf16[2048,128]{1,0:T(8,128)(2,1)}, bf16[2048,128]{1,0:T(8,128)(2,1)S(1)}, u32[]{:S(2)}, u32[]{:S(2)}) %collective-permute-start.14) | collective-permute-done | bytes 524320 | tf_op jit(solution)/shard_map/ppermute | solution.py:564
  164.0 5.0 %merge_terms.3 = (f32[2048,128]{1,0:T(8,128)}, bf16[2048,128]{1,0:T(8,128)(2,1)}, bf16[2048,128]{1,0:T(8,128)(2,1)}, bf16[2048,128]{1,0:T(8,128)(2,1)}) custom-call(s32[22]{0:T(128)} %get-tuple-element.49.walk, bf16[4096,128]{1,0:T(8,128)(2,1)} %get-tuple-element.52.refs_0_, bf16[4096,128]{1,0:T(8,128)(2,1)} %get-tuple-element.53.refs_1_, ...), custom_call_target="tpu_custom_call" | custom-call | bytes 1024 | tf_op jit(solution)/shard_map/merge_terms/pallas_call | solution.py:380
  169.0 3.7 %collective-permute-start.18 = (bf16[2048,128]{1,0:T(8,128)(2,1)}, bf16[2048,128]{1,0:T(8,128)(2,1)S(1)}, u32[]{:S(2)}, u32[]{:S(2)}) collective-permute-start(bf16[2048,128]{1,0:T(8,128)(2,1)} %get-tuple-element.62), channel_id=1, source_target_pairs={{0,8},{4,12},{8,16},{12,20},{16,24},{20,28},{24,0},{28,4},{1,9},{5... | collective-permute-start | bytes 1572872 | tf_op jit(solution)/shard_map/ppermute | solution.py:560
  172.7 2.4 collective-permute-start.16
  175.1 38.4 %attend_head.3 = (bf16[1024,2048]{1,0:T(8,128)(2,1)}, bf16[1024,2048]{1,0:T(8,128)(2,1)}, bf16[4096,128]{1,0:T(8,128)(2,1)}, bf16[4096,128]{1,0:T(8,128)(2,1)}, ...) custom-call(s32[64]{0:T(128)} %get-tuple-element.40.found, ...), custom_call_target="tpu_custom_call", output_to_operand_aliasing={{0}: (9, {}), {1}: (10, {})} | custom-call | bytes 1024 | tf_op jit(solution)/shard_map/attend_head/pallas_call | solution.py:532
  213.5 2.5 collective-permute-start.19
  217.1 1.4 collective-permute-start.20
  218.6 9.2 %collective-permute-done.19.refs_1_ = bf16[2048,128]{1,0:T(8,128)(2,1)} collective-permute-done((bf16[2048,128]{1,0:T(8,128)(2,1)}, bf16[2048,128]{1,0:T(8,128)(2,1)}, u32[]{:S(2)}, u32[]{:S(2)}) %collective-permute-start.19) | collective-permute-done | bytes 524320 | tf_op jit(solution)/shard_map/ppermute | solution.py:564
  228.6 3.5 %merge_terms.4 = (f32[1024,128]{1,0:T(8,128)}, bf16[1024,128]{1,0:T(8,128)(2,1)}, bf16[1024,128]{1,0:T(8,128)(2,1)}, bf16[1024,128]{1,0:T(8,128)(2,1)}) custom-call(s32[22]{0:T(128)} %get-tuple-element.49.walk, bf16[4096,128]{1,0:T(8,128)(2,1)} %get-tuple-element.63.refs_0_, bf16[2048,128]{1,0:T(8,128)(2,1)} %collective-permute-done.19.refs_1_, ...), custom_call_target="tpu_custom_call" | custom-call | bytes 1024 | tf_op jit(solution)/shard_map/merge_terms/pallas_call | solution.py:380
  232.1 1.8 collective-permute-start.21
  233.9 6.3 %collective-permute-start.22 = (bf16[1024,128]{1,0:T(8,128)(2,1)}, bf16[1024,128]{1,0:T(8,128)(2,1)}, u32[]{:S(2)}, u32[]{:S(2)}) collective-permute-start(bf16[1024,128]{1,0:T(8,128)(2,1)} %get-tuple-element.68), channel_id=1, source_target_pairs={{0,16},{4,20},{8,24},{12,28},{16,0},{20,4},{24,8},{28,12},{1,17},{... | collective-permute-start | bytes 786440 | tf_op jit(solution)/shard_map/ppermute | solution.py:560
  241.3 3.5 %all-to-all-start.1 = ((bf16[4,2,256,128]{3,2,1,0:T(8,128)(2,1)}), bf16[4,2,256,128]{3,2,1,0:T(8,128)(2,1)S(1)}, u32[]{:S(2)}, u32[]{:S(2)}) async-start(bf16[4,2,256,128]{3,2,1,0:T(8,128)(2,1)} %bitcast.20), calls=%async_computation.1 | async-start | bytes 1048576 | tf_op jit(solution)/shard_map/all_to_all | solution.py:617
  244.8 3.5 %merge_terms.5 = (f32[1024,128]{1,0:T(8,128)}, bf16[1024,128]{1,0:T(8,128)(2,1)}, bf16[1024,128]{1,0:T(8,128)(2,1)}, bf16[1024,128]{1,0:T(8,128)(2,1)}) custom-call(s32[22]{0:T(128)} %get-tuple-element.49.walk, bf16[4096,128]{1,0:T(8,128)(2,1)} %get-tuple-element.70.refs_0_, bf16[2048,128]{1,0:T(8,128)(2,1)} %collective-permute-done.24.refs_1_, ...), custom_call_target="tpu_custom_call" | custom-call | bytes 1024 | tf_op jit(solution)/shard_map/merge_terms/pallas_call | solution.py:380
  248.4 3.8 %collective-permute-start.25 = (bf16[1024,128]{1,0:T(8,128)(2,1)}, bf16[1024,128]{1,0:T(8,128)(2,1)S(1)}, u32[]{:S(2)}, u32[]{:S(2)}) collective-permute-start(bf16[1024,128]{1,0:T(8,128)(2,1)} %get-tuple-element.73), channel_id=1, source_target_pairs={{0,24},{4,28},{8,0},{12,4},{16,8},{20,12},{24,16},{28,20},{1,25},{... | collective-permute-start | bytes 786440 | tf_op jit(solution)/shard_map/ppermute | solution.py:560
  252.7 2.1 collective-permute-done.22
  254.8 1.8 add_convert_fusion.2
  256.7 3.4 %all-to-all-start.2 = ((bf16[4,1,256,128]{3,2,1,0:T(8,128)(2,1)}), bf16[4,1,256,128]{3,2,1,0:T(8,128)(2,1)S(1)}, u32[]{:S(2)}, u32[]{:S(2)}) async-start(bf16[4,1,256,128]{3,2,1,0:T(8,128)(2,1)} %bitcast.5), calls=%async_computation.2 | async-start | bytes 524288 | tf_op jit(solution)/shard_map/all_to_all | solution.py:617
  260.1 15.6 %collective-permute-done.26 = bf16[1024,128]{1,0:T(8,128)(2,1)S(1)} collective-permute-done((bf16[1024,128]{1,0:T(8,128)(2,1)}, bf16[1024,128]{1,0:T(8,128)(2,1)S(1)}, u32[]{:S(2)}, u32[]{:S(2)}) %collective-permute-start.26) | collective-permute-done | bytes 262176 | tf_op jit(solution)/shard_map/ppermute | solution.py:560
  275.7 1.9 add_convert_fusion.1
  277.5 3.4 %all-to-all-start.3 = ((bf16[4,1,256,128]{3,2,1,0:T(8,128)(2,1)}), bf16[4,1,256,128]{3,2,1,0:T(8,128)(2,1)S(1)}, u32[]{:S(2)}, u32[]{:S(2)}) async-start(bf16[4,1,256,128]{3,2,1,0:T(8,128)(2,1)} %bitcast.11), calls=%async_computation.3 | async-start | bytes 524288 | tf_op jit(solution)/shard_map/all_to_all | solution.py:617
  281.5 1.0 copy.30
  282.5 4.4 %all-to-all-done.3 = bf16[4,1,256,128]{3,2,1,0:T(8,128)(2,1)S(1)} async-done(((bf16[4,1,256,128]{3,2,1,0:T(8,128)(2,1)}), bf16[4,1,256,128]{3,2,1,0:T(8,128)(2,1)S(1)}, u32[]{:S(2)}, u32[]{:S(2)}) %all-to-all-start.3) | async-done | bytes 262176 | tf_op jit(solution)/shard_map/all_to_all | solution.py:617
  (109 shorter events, 11.8 us)
Async XLA Ops:
  0.6 30.9 %copy-start.31 = (s32[64,3]{0,1:T(4,128)S(1)}, s32[64,3]{0,1:T(4,128)}, u32[]{:S(2)}) copy-start(s32[64,3]{0,1:T(4,128)} %param.9) | copy-start | bytes 2308
  24.6 59.9 %copy-start.1 = (bf16[2048,128]{1,0:T(8,128)(2,1)S(1)}, bf16[2048,128]{1,0:T(8,128)(2,1)}, u32[]{:S(2)}) copy-start(bf16[2048,128]{1,0:T(8,128)(2,1)} %get-tuple-element.42.refs_0_.refs_5_.refs_2_) | copy-start | bytes 1572868
  24.6 27.8 %collective-permute-start = (bf16[2048,128]{1,0:T(8,128)(2,1)}, bf16[2048,128]{1,0:T(8,128)(2,1)S(1)}, u32[]{:S(2)}, u32[]{:S(2)}) collective-permute-start(bf16[2048,128]{1,0:T(8,128)(2,1)} %get-tuple-element.42.refs_0_.refs_5_.refs_2_), channel_id=1, source_target_pairs={{0,4},{4,0},{8,12},{12,8},{16,20},{20,16},{24,28},{28,24},{1,5},{5... | collective-permute-start | bytes 1572872 | tf_op jit(solution)/shard_map/ppermute | solution.py:564
  26.9 10.7 %collective-permute-start.3 = (bf16[1024,128]{1,0:T(8,128)(2,1)}, bf16[1024,128]{1,0:T(8,128)(2,1)S(1)}, u32[]{:S(2)}, u32[]{:S(2)}) collective-permute-start(bf16[1024,128]{1,0:T(8,128)(2,1)} %get-tuple-element.44.refs_0_.refs_2_), channel_id=1, source_target_pairs={{0,24},{4,28},{8,0},{12,4},{16,8},{20,12},{24,16},{28,20},{1,25},{... | collective-permute-start | bytes 786440 | tf_op jit(solution)/shard_map/ppermute | solution.py:560
  30.5 21.9 %collective-permute-start.2 = (bf16[1024,128]{1,0:T(8,128)(2,1)}, bf16[1024,128]{1,0:T(8,128)(2,1)S(1)}, u32[]{:S(2)}, u32[]{:S(2)}) collective-permute-start(bf16[1024,128]{1,0:T(8,128)(2,1)} %get-tuple-element.44.refs_0_.refs_2_), channel_id=1, source_target_pairs={{0,16},{4,20},{8,24},{12,28},{16,0},{20,4},{24,8},{28,12},{1,17},{... | collective-permute-start | bytes 786440 | tf_op jit(solution)/shard_map/ppermute | solution.py:560
  30.5 21.9 %collective-permute-start.1 = (bf16[1024,128]{1,0:T(8,128)(2,1)}, bf16[1024,128]{1,0:T(8,128)(2,1)S(1)}, u32[]{:S(2)}, u32[]{:S(2)}) collective-permute-start(bf16[1024,128]{1,0:T(8,128)(2,1)} %get-tuple-element.44.refs_0_.refs_2_), channel_id=1, source_target_pairs={{0,8},{4,12},{8,16},{12,20},{16,24},{20,28},{24,0},{28,4},{1,9},{5... | collective-permute-start | bytes 786440 | tf_op jit(solution)/shard_map/ppermute | solution.py:560
  37.6 50.1 %copy-start.2 = (bf16[1024,128]{1,0:T(8,128)(2,1)}, bf16[1024,128]{1,0:T(8,128)(2,1)S(1)}, u32[]{:S(2)}) copy-start(bf16[1024,128]{1,0:T(8,128)(2,1)S(1)} %collective-permute-done.3.refs_4_.refs_3_.refs_5_) | copy-start | bytes 786436
  52.4 35.4 %copy-start.3 = (bf16[1024,128]{1,0:T(8,128)(2,1)}, bf16[1024,128]{1,0:T(8,128)(2,1)S(1)}, u32[]{:S(2)}) copy-start(bf16[1024,128]{1,0:T(8,128)(2,1)S(1)} %collective-permute-done.2.refs_3_.refs_2_.refs_4_) | copy-start | bytes 786436
  52.4 35.4 %copy-start.4 = (bf16[1024,128]{1,0:T(8,128)(2,1)}, bf16[1024,128]{1,0:T(8,128)(2,1)S(1)}, u32[]{:S(2)}) copy-start(bf16[1024,128]{1,0:T(8,128)(2,1)S(1)} %collective-permute-done.1.refs_2_.refs_1_.refs_3_) | copy-start | bytes 786436
  52.4 35.4 %copy-start = (bf16[2048,128]{1,0:T(8,128)(2,1)}, bf16[2048,128]{1,0:T(8,128)(2,1)S(1)}, u32[]{:S(2)}) copy-start(bf16[2048,128]{1,0:T(8,128)(2,1)S(1)} %collective-permute-done.refs_1_.refs_4_.refs_6_.refs_3_) | copy-start | bytes 1572868
  54.3 31.9 %copy-start.13 = (s32[22]{0:T(128)S(1)}, s32[22]{0:T(128)}, u32[]{:S(2)}) copy-start(s32[22]{0:T(128)} %get-tuple-element.49.walk) | copy-start | bytes 268
  55.7 30.5 %collective-permute-start.10 = (bf16[2048,128]{1,0:T(8,128)(2,1)}, bf16[2048,128]{1,0:T(8,128)(2,1)S(1)}, u32[]{:S(2)}, u32[]{:S(2)}) collective-permute-start(bf16[2048,128]{1,0:T(8,128)(2,1)} %pack_blocks.3), channel_id=1, source_target_pairs={{0,4},{4,0},{8,12},{12,8},{16,20},{20,16},{24,28},{28,24},{1,5},{5... | collective-permute-start | bytes 1572872 | tf_op jit(solution)/shard_map/ppermute | solution.py:564
  58.6 27.6 %collective-permute-start.11 = (bf16[1536,128]{1,0:T(8,128)(2,1)}, bf16[1536,128]{1,0:T(8,128)(2,1)S(1)}, u32[]{:S(2)}, u32[]{:S(2)}) collective-permute-start(bf16[1536,128]{1,0:T(8,128)(2,1)} %pack_blocks.4), channel_id=1, source_target_pairs={{12,0},{13,1},{14,2},{15,3}} | collective-permute-start | bytes 1179656 | tf_op jit(solution)/shard_map/ppermute | solution.py:570
  59.8 9.0 %collective-permute-start.6 = (bf16[1024,128]{1,0:T(8,128)(2,1)}, bf16[1024,128]{1,0:T(8,128)(2,1)S(1)}, u32[]{:S(2)}, u32[]{:S(2)}) collective-permute-start(bf16[1024,128]{1,0:T(8,128)(2,1)} %get-tuple-element.45.refs_1_.refs_0_.refs_6_), channel_id=1, source_target_pairs={{0,24},{4,28},{8,0},{12,4},{16,8},{20,12},{24,16},{28,20},{1,25},{... | collective-permute-start | bytes 786440 | tf_op jit(solution)/shard_map/ppermute | solution.py:560
  59.9 24.6 %collective-permute-start.5 = (bf16[1024,128]{1,0:T(8,128)(2,1)}, bf16[1024,128]{1,0:T(8,128)(2,1)S(1)}, u32[]{:S(2)}, u32[]{:S(2)}) collective-permute-start(bf16[1024,128]{1,0:T(8,128)(2,1)} %get-tuple-element.45.refs_1_.refs_0_.refs_6_), channel_id=1, source_target_pairs={{0,16},{4,20},{8,24},{12,28},{16,0},{20,4},{24,8},{28,12},{1,17},{... | collective-permute-start | bytes 786440 | tf_op jit(solution)/shard_map/ppermute | solution.py:560
  62.1 22.4 %collective-permute-start.4 = (bf16[1024,128]{1,0:T(8,128)(2,1)}, bf16[1024,128]{1,0:T(8,128)(2,1)S(1)}, u32[]{:S(2)}, u32[]{:S(2)}) collective-permute-start(bf16[1024,128]{1,0:T(8,128)(2,1)} %get-tuple-element.45.refs_1_.refs_0_.refs_6_), channel_id=1, source_target_pairs={{0,8},{4,12},{8,16},{12,20},{16,24},{20,28},{24,0},{28,4},{1,9},{5... | collective-permute-start | bytes 786440 | tf_op jit(solution)/shard_map/ppermute | solution.py:560
  68.9 33.2 %copy-start.6 = (bf16[1024,128]{1,0:T(8,128)(2,1)}, bf16[1024,128]{1,0:T(8,128)(2,1)S(1)}, u32[]{:S(2)}) copy-start(bf16[1024,128]{1,0:T(8,128)(2,1)S(1)} %collective-permute-done.6.refs_7_.refs_3_.refs_9_) | copy-start | bytes 786436
  84.5 17.5 %copy-start.7 = (bf16[1024,128]{1,0:T(8,128)(2,1)}, bf16[1024,128]{1,0:T(8,128)(2,1)S(1)}, u32[]{:S(2)}) copy-start(bf16[1024,128]{1,0:T(8,128)(2,1)S(1)} %collective-permute-done.5.refs_6_.refs_2_.refs_8_) | copy-start | bytes 786436
  86.1 56.7 %collective-permute-start.8 = (bf16[3072,128]{1,0:T(8,128)(2,1)S(1)}, bf16[3072,128]{1,0:T(8,128)(2,1)S(1)}, u32[]{:S(2)}, u32[]{:S(2)}) collective-permute-start(bf16[3072,128]{1,0:T(8,128)(2,1)S(1)} %get-tuple-element.47), channel_id=1, source_target_pairs={{0,16},{4,20},{8,24},{12,28},{16,0},{20,4},{24,8},{28,12},{1,17},{... | collective-permute-start | bytes 2359304 | tf_op jit(solution)/shard_map/ppermute | solution.py:560
  87.8 13.4 %collective-permute-start.12 = (bf16[2048,128]{1,0:T(8,128)(2,1)S(1)}, bf16[2048,128]{1,0:T(8,128)(2,1)S(1)}, u32[]{:S(2)}, u32[]{:S(2)}) collective-permute-start(bf16[2048,128]{1,0:T(8,128)(2,1)S(1)} %pack_blocks.5), channel_id=1, source_target_pairs={{0,4},{4,0},{8,12},{12,8},{16,20},{20,16},{24,28},{28,24},{1,5},{5... | collective-permute-start | bytes 1572872 | tf_op jit(solution)/shard_map/ppermute | solution.py:564
  91.4 52.7 %collective-permute-start.9 = (bf16[3072,128]{1,0:T(8,128)(2,1)S(1)}, bf16[3072,128]{1,0:T(8,128)(2,1)S(1)}, u32[]{:S(2)}, u32[]{:S(2)}) collective-permute-start(bf16[3072,128]{1,0:T(8,128)(2,1)S(1)} %get-tuple-element.48), channel_id=1, source_target_pairs={{0,24},{4,28},{8,0},{12,4},{16,8},{20,12},{24,16},{28,20},{1,25},{... | collective-permute-start | bytes 2359304 | tf_op jit(solution)/shard_map/ppermute | solution.py:560
  93.4 50.7 %collective-permute-start.7 = (bf16[3072,128]{1,0:T(8,128)(2,1)S(1)}, bf16[3072,128]{1,0:T(8,128)(2,1)S(1)}, u32[]{:S(2)}, u32[]{:S(2)}) collective-permute-start(bf16[3072,128]{1,0:T(8,128)(2,1)S(1)} %get-tuple-element.46.refs_13_), channel_id=1, source_target_pairs={{0,8},{4,12},{8,16},{12,20},{16,24},{20,28},{24,0},{28,4},{1,9},{5... | collective-permute-start | bytes 2359304 | tf_op jit(solution)/shard_map/ppermute | solution.py:560
  140.7 15.1 %collective-permute-start.13 = (bf16[2048,128]{1,0:T(8,128)(2,1)}, bf16[2048,128]{1,0:T(8,128)(2,1)S(1)}, u32[]{:S(2)}, u32[]{:S(2)}) collective-permute-start(bf16[2048,128]{1,0:T(8,128)(2,1)} %get-tuple-element.54), channel_id=1, source_target_pairs={{0,4},{4,0},{8,12},{12,8},{16,20},{20,16},{24,28},{28,24},{1,5},{5... | collective-permute-start | bytes 1572872 | tf_op jit(solution)/shard_map/ppermute | solution.py:564
  141.7 21.4 %collective-permute-start.14 = (bf16[2048,128]{1,0:T(8,128)(2,1)}, bf16[2048,128]{1,0:T(8,128)(2,1)S(1)}, u32[]{:S(2)}, u32[]{:S(2)}) collective-permute-start(bf16[2048,128]{1,0:T(8,128)(2,1)} %get-tuple-element.55), channel_id=1, source_target_pairs={{0,4},{4,0},{8,12},{12,8},{16,20},{20,16},{24,28},{28,24},{1,5},{5... | collective-permute-start | bytes 1572872 | tf_op jit(solution)/shard_map/ppermute | solution.py:564
  142.8 20.3 %copy-start.21 = (bf16[3072,128]{1,0:T(8,128)(2,1)}, bf16[3072,128]{1,0:T(8,128)(2,1)S(1)}, u32[]{:S(2)}) copy-start(bf16[3072,128]{1,0:T(8,128)(2,1)S(1)} %collective-permute-done.8.refs_8_.refs_5_) | copy-start | bytes 2359300
  142.8 7.0 %collective-permute-start.15 = (bf16[1536,128]{1,0:T(8,128)(2,1)}, bf16[1536,128]{1,0:T(8,128)(2,1)S(1)}, u32[]{:S(2)}, u32[]{:S(2)}) collective-permute-start(bf16[1536,128]{1,0:T(8,128)(2,1)} %get-tuple-element.56), channel_id=1, source_target_pairs={{0,12},{1,13},{2,14},{3,15}} | collective-permute-start | bytes 1179656 | tf_op jit(solution)/shard_map/ppermute | solution.py:570
  144.1 19.0 %copy-start.22 = (bf16[3072,128]{1,0:T(8,128)(2,1)}, bf16[3072,128]{1,0:T(8,128)(2,1)S(1)}, u32[]{:S(2)}) copy-start(bf16[3072,128]{1,0:T(8,128)(2,1)S(1)} %collective-permute-done.9.refs_9_.refs_6_) | copy-start | bytes 2359300
  144.1 19.0 %copy-start.23 = (bf16[3072,128]{1,0:T(8,128)(2,1)}, bf16[3072,128]{1,0:T(8,128)(2,1)S(1)}, u32[]{:S(2)}) copy-start(bf16[3072,128]{1,0:T(8,128)(2,1)S(1)} %collective-permute-done.7.refs_7_.refs_4_) | copy-start | bytes 2359300
  169.0 47.0 %collective-permute-start.17 = (bf16[2048,128]{1,0:T(8,128)(2,1)}, bf16[2048,128]{1,0:T(8,128)(2,1)S(1)}, u32[]{:S(2)}, u32[]{:S(2)}) collective-permute-start(bf16[2048,128]{1,0:T(8,128)(2,1)} %get-tuple-element.61), channel_id=1, source_target_pairs={{0,16},{4,20},{8,24},{12,28},{16,0},{20,4},{24,8},{28,12},{1,17},{... | collective-permute-start | bytes 1572872 | tf_op jit(solution)/shard_map/ppermute | solution.py:560
  169.0 47.0 %collective-permute-start.18 = (bf16[2048,128]{1,0:T(8,128)(2,1)}, bf16[2048,128]{1,0:T(8,128)(2,1)S(1)}, u32[]{:S(2)}, u32[]{:S(2)}) collective-permute-start(bf16[2048,128]{1,0:T(8,128)(2,1)} %get-tuple-element.62), channel_id=1, source_target_pairs={{0,8},{4,12},{8,16},{12,20},{16,24},{20,28},{24,0},{28,4},{1,9},{5... | collective-permute-start | bytes 1572872 | tf_op jit(solution)/shard_map/ppermute | solution.py:560
  172.7 43.3 %collective-permute-start.16 = (bf16[2048,128]{1,0:T(8,128)(2,1)}, bf16[2048,128]{1,0:T(8,128)(2,1)S(1)}, u32[]{:S(2)}, u32[]{:S(2)}) collective-permute-start(bf16[2048,128]{1,0:T(8,128)(2,1)} %get-tuple-element.57.refs_9_), channel_id=1, source_target_pairs={{0,24},{4,28},{8,0},{12,4},{16,8},{20,12},{24,16},{28,20},{1,25},{... | collective-permute-start | bytes 1572872 | tf_op jit(solution)/shard_map/ppermute | solution.py:560
  213.5 26.8 %copy-start.25 = (f32[2048,128]{1,0:T(8,128)S(1)}, f32[2048,128]{1,0:T(8,128)}, u32[]{:S(2)}) copy-start(f32[2048,128]{1,0:T(8,128)} %get-tuple-element.60) | copy-start | bytes 3145732
  213.5 14.3 %collective-permute-start.19 = (bf16[2048,128]{1,0:T(8,128)(2,1)}, bf16[2048,128]{1,0:T(8,128)(2,1)}, u32[]{:S(2)}, u32[]{:S(2)}) collective-permute-start(bf16[2048,128]{1,0:T(8,128)(2,1)} %get-tuple-element.64), channel_id=1, source_target_pairs={{0,4},{4,0},{8,12},{12,8},{16,20},{20,16},{24,28},{28,24},{1,5},{5... | collective-permute-start | bytes 1572872 | tf_op jit(solution)/shard_map/ppermute | solution.py:564
  217.1 23.1 %copy-start.16 = (bf16[2048,128]{1,0:T(8,128)(2,1)S(1)}, bf16[2048,128]{1,0:T(8,128)(2,1)}, u32[]{:S(2)}) copy-start(bf16[2048,128]{1,0:T(8,128)(2,1)} %copy-done.15) | copy-start | bytes 1572868
  217.1 23.1 %copy-start.18 = (bf16[2048,128]{1,0:T(8,128)(2,1)S(1)}, bf16[2048,128]{1,0:T(8,128)(2,1)}, u32[]{:S(2)}) copy-start(bf16[2048,128]{1,0:T(8,128)(2,1)} %copy-done.17) | copy-start | bytes 1572868
  217.1 23.1 %copy-start.20 = (bf16[2048,128]{1,0:T(8,128)(2,1)S(1)}, bf16[2048,128]{1,0:T(8,128)(2,1)}, u32[]{:S(2)}) copy-start(bf16[2048,128]{1,0:T(8,128)(2,1)} %copy-done.19) | copy-start | bytes 1572868
  217.1 10.7 %collective-permute-start.20 = (bf16[1536,128]{1,0:T(8,128)(2,1)}, bf16[1536,128]{1,0:T(8,128)(2,1)S(1)}, u32[]{:S(2)}, u32[]{:S(2)}) collective-permute-start(bf16[1536,128]{1,0:T(8,128)(2,1)} %gate.2), channel_id=1, source_target_pairs={{0,12},{1,13},{2,14},{3,15}} | collective-permute-start | bytes 1179656 | tf_op jit(solution)/shard_map/ppermute | solution.py:570
  218.6 26.3 %collective-permute-start.24 = (bf16[2048,128]{1,0:T(8,128)(2,1)}, bf16[2048,128]{1,0:T(8,128)(2,1)}, u32[]{:S(2)}, u32[]{:S(2)}) collective-permute-start(bf16[2048,128]{1,0:T(8,128)(2,1)} %gate.3), channel_id=1, source_target_pairs={{0,4},{4,0},{8,12},{12,8},{16,20},{20,16},{24,28},{28,24},{1,5},{5... | collective-permute-start | bytes 1572872 | tf_op jit(solution)/shard_map/ppermute | solution.py:564
  232.1 22.7 %copy-start.26 = (f32[1024,128]{1,0:T(8,128)S(1)}, f32[1024,128]{1,0:T(8,128)}, u32[]{:S(2)}) copy-start(f32[1024,128]{1,0:T(8,128)} %get-tuple-element.66) | copy-start | bytes 1572868
  232.1 20.0 %collective-permute-start.21 = (bf16[1024,128]{1,0:T(8,128)(2,1)}, bf16[1024,128]{1,0:T(8,128)(2,1)S(1)}, u32[]{:S(2)}, u32[]{:S(2)}) collective-permute-start(bf16[1024,128]{1,0:T(8,128)(2,1)} %get-tuple-element.67), channel_id=1, source_target_pairs={{0,24},{4,28},{8,0},{12,4},{16,8},{20,12},{24,16},{28,20},{1,25},{... | collective-permute-start | bytes 786440 | tf_op jit(solution)/shard_map/ppermute | solution.py:560
  233.9 20.9 %collective-permute-start.22 = (bf16[1024,128]{1,0:T(8,128)(2,1)}, bf16[1024,128]{1,0:T(8,128)(2,1)}, u32[]{:S(2)}, u32[]{:S(2)}) collective-permute-start(bf16[1024,128]{1,0:T(8,128)(2,1)} %get-tuple-element.68), channel_id=1, source_target_pairs={{0,16},{4,20},{8,24},{12,28},{16,0},{20,4},{24,8},{28,12},{1,17},{... | collective-permute-start | bytes 786440 | tf_op jit(solution)/shard_map/ppermute | solution.py:560
  240.2 14.6 %collective-permute-start.23 = (bf16[1024,128]{1,0:T(8,128)(2,1)}, bf16[1024,128]{1,0:T(8,128)(2,1)}, u32[]{:S(2)}, u32[]{:S(2)}) collective-permute-start(bf16[1024,128]{1,0:T(8,128)(2,1)} %get-tuple-element.69), channel_id=1, source_target_pairs={{0,8},{4,12},{8,16},{12,20},{16,24},{20,28},{24,0},{28,4},{1,9},{5... | collective-permute-start | bytes 786440 | tf_op jit(solution)/shard_map/ppermute | solution.py:560
  241.3 15.3 %all-to-all-start.1 = ((bf16[4,2,256,128]{3,2,1,0:T(8,128)(2,1)}), bf16[4,2,256,128]{3,2,1,0:T(8,128)(2,1)S(1)}, u32[]{:S(2)}, u32[]{:S(2)}) async-start(bf16[4,2,256,128]{3,2,1,0:T(8,128)(2,1)} %bitcast.20), calls=%async_computation.1 | async-start | bytes 1048576 | tf_op jit(solution)/shard_map/all_to_all | solution.py:617
  248.4 11.7 %collective-permute-start.25 = (bf16[1024,128]{1,0:T(8,128)(2,1)}, bf16[1024,128]{1,0:T(8,128)(2,1)S(1)}, u32[]{:S(2)}, u32[]{:S(2)}) collective-permute-start(bf16[1024,128]{1,0:T(8,128)(2,1)} %get-tuple-element.73), channel_id=1, source_target_pairs={{0,24},{4,28},{8,0},{12,4},{16,8},{20,12},{24,16},{28,20},{1,25},{... | collective-permute-start | bytes 786440 | tf_op jit(solution)/shard_map/ppermute | solution.py:560
  252.2 23.5 %collective-permute-start.26 = (bf16[1024,128]{1,0:T(8,128)(2,1)}, bf16[1024,128]{1,0:T(8,128)(2,1)S(1)}, u32[]{:S(2)}, u32[]{:S(2)}) collective-permute-start(bf16[1024,128]{1,0:T(8,128)(2,1)} %get-tuple-element.74), channel_id=1, source_target_pairs={{0,16},{4,20},{8,24},{12,28},{16,0},{20,4},{24,8},{28,12},{1,17},{... | collective-permute-start | bytes 786440 | tf_op jit(solution)/shard_map/ppermute | solution.py:560
  252.2 23.5 %collective-permute-start.27 = (bf16[1024,128]{1,0:T(8,128)(2,1)}, bf16[1024,128]{1,0:T(8,128)(2,1)S(1)}, u32[]{:S(2)}, u32[]{:S(2)}) collective-permute-start(bf16[1024,128]{1,0:T(8,128)(2,1)} %get-tuple-element.75), channel_id=1, source_target_pairs={{0,8},{4,12},{8,16},{12,20},{16,24},{20,28},{24,0},{28,4},{1,9},{5... | collective-permute-start | bytes 786440 | tf_op jit(solution)/shard_map/ppermute | solution.py:560
  256.7 20.9 %all-to-all-start.2 = ((bf16[4,1,256,128]{3,2,1,0:T(8,128)(2,1)}), bf16[4,1,256,128]{3,2,1,0:T(8,128)(2,1)S(1)}, u32[]{:S(2)}, u32[]{:S(2)}) async-start(bf16[4,1,256,128]{3,2,1,0:T(8,128)(2,1)} %bitcast.5), calls=%async_computation.2 | async-start | bytes 524288 | tf_op jit(solution)/shard_map/all_to_all | solution.py:617
  277.5 9.4 %all-to-all-start.3 = ((bf16[4,1,256,128]{3,2,1,0:T(8,128)(2,1)}), bf16[4,1,256,128]{3,2,1,0:T(8,128)(2,1)S(1)}, u32[]{:S(2)}, u32[]{:S(2)}) async-start(bf16[4,1,256,128]{3,2,1,0:T(8,128)(2,1)} %bitcast.11), calls=%async_computation.3 | async-start | bytes 524288 | tf_op jit(solution)/shard_map/all_to_all | solution.py:617
  (15 other events, 93.8 us)

commit v5 on v4

--- a/solution.py
+++ b/solution.py
@@ -652,10 +652,10 @@
     own = to_heads(keys, values, groups)
     own, joined = own[:2], own[2:]
     units = [spread(a) for a in own]
-    direct = straight([[a] for a in own], tuple(units[0][1:]))
     in_row = [[a] + [row_shift(a, plan, lanes - t) for t in range(1, lanes)] for a in joined]
     packs = [across([units[0]], tuple(a for some in in_row for a in some[1:]))]
-    packs.append(across([units[1]], (*packs[0], *([] if direct is None else [direct]))))
+    packs.append(across([units[1]], tuple(packs[0])))
+    direct = straight([[a] for a in own], tuple(units[1][1:]))
     pieces = [(a, t, rows) for t in range(2) for a in units[t]] + [(a, t, size) for t in range(2) for a in packs[t]]
     if direct is not None:
         pieces.append((direct, 2, plan.direct_slots * BLK))

time: 289 us -> 298 us (1.031)
  starting transfers between devices: 54.8 us -> 64 us
    ppermute x3, waiting for transfers between devices: 5.63 us -> 18.8 us  [straight_shift(): return lax.ppermute(array, 'ctx', [(there, back)])]
    all_to_all x3, starting transfers between devices: 10.3 us -> 22.5 us  [to_tokens(): lax.all_to_all(parts, 'kvh', split_axis=0, concat_axis=0, tiled=True)]
    ppermute x18, waiting for transfers between devices: 50.7 us -> 39.4 us  [column_shift(): lax.ppermute(array, 'ctx', [(n, (n + rows * plan.lanes) % plan.ctx) for n...]
    ppermute x7, waiting for transfers between devices: 30.3 us -> 25.4 us  [row_shift(): lax.ppermute(array, 'ctx', [(n, n - n % plan.lanes + (n + lanes) % plan.l...]
    ppermute x7, starting transfers between devices: 11.1 us -> 7.14 us  [row_shift(): lax.ppermute(array, 'ctx', [(n, n - n % plan.lanes + (n + lanes) % plan.l...]
    all_to_all x3, waiting for transfers between devices: 4.45 us -> 7.57 us  [to_tokens(): lax.all_to_all(parts, 'kvh', split_axis=0, concat_axis=0, tiled=True)]
    unnamed x69 -> x73, local copies, waits for them, and re-layouts: 8.4 us -> 9.67 us
  transfers between devices with their start and end apart: 31 -> 31, of which waited for: 11 -> 14; matrix products, arithmetic and copies ran while one was open for 2% -> 2% of each run, Pallas kernels for 33% -> 32%
where the time goes in v5:
time: 298 us; the launch traced here: 296 us
  Pallas kernels  105 us (35%)
  waiting for transfers between devices  91.1 us (31%)
  starting transfers between devices  64 us (21%)
  blocking collectives  19.4 us (7%)
  local copies, waits for them, and re-layouts  11.5 us (4%)
  other arithmetic  4.06 us (1%)
    pallas_call x2, Pallas kernels, attend(): pl.pallas_call(functools.partial(attend_kernel, plan=plan, qpk=qpk, per=4...  77 us
    ppermute x18, waiting for transfers between devices, column_shift(): lax.ppermute(array, 'ctx', [(n, (n + rows * plan.lanes) % plan.ctx) for n...  39.4 us
    ppermute x18, starting transfers between devices, column_shift(): lax.ppermute(array, 'ctx', [(n, (n + rows * plan.lanes) % plan.ctx) for n...  28.5 us
    ppermute x7, waiting for transfers between devices, row_shift(): lax.ppermute(array, 'ctx', [(n, n - n % plan.lanes + (n + lanes) % plan.l...  25.4 us
    all_to_all x3, starting transfers between devices, to_tokens(): lax.all_to_all(parts, 'kvh', split_axis=0, concat_axis=0, tiled=True)  22.5 us
    all_to_all x1, blocking collectives, to_heads(): lax.all_to_all(parts, 'kvh', split_axis=0, concat_axis=0, tiled=True)  19.4 us
    ppermute x3, waiting for transfers between devices, straight_shift(): return lax.ppermute(array, 'ctx', [(there, back)])  18.8 us
    pallas_call x3, Pallas kernels, merge(): pl.pallas_call(functools.partial(merge_kernel, plan=plan, halves=halves,...  12.1 us
  transfers between devices with their start and end apart: 31, of which 14 were waited for; matrix products, arithmetic and copies ran while one was open for 2% of the time, Pallas kernels for 32%

profile of v5, /device:TPU:0, one launch (start us, length us, event | category | flops | bytes accessed | tf_op | source)
XLA Modules:
  0.0 296.0 jit_solution(3757644363390151672)
XLA Ops:
  0.6 2.4 cut_heads.1
  3.0 19.4 %all_to_all.20.parts = bf16[4,4,256,128]{3,2,1,0:T(8,128)(2,1)} all-to-all(bf16[4,4,256,128]{3,2,1,0:T(8,128)(2,1)} %cut_heads.1), channel_id=1, replica_groups=mesh['ctx'=8,'kvh'=4] {'kvh'}, dimensions={0} | all-to-all | bytes 2097152 | tf_op jit(solution)/shard_map/all_to_all | solution.py:602
  22.4 2.2 join_heads.1
  24.6 2.3 collective-permute-start
  26.9 3.6 %collective-permute-start.3 = (bf16[1024,128]{1,0:T(8,128)(2,1)}, bf16[1024,128]{1,0:T(8,128)(2,1)S(1)}, u32[]{:S(2)}, u32[]{:S(2)}) collective-permute-start(bf16[1024,128]{1,0:T(8,128)(2,1)} %get-tuple-element.44.refs_0_.refs_2_), channel_id=1, source_target_pairs={{0,24},{4,28},{8,0},{12,4},{16,8},{20,12},{24,16},{28,20},{1,25},{... | collective-permute-start | bytes 786440 | tf_op jit(solution)/shard_map/ppermute | solution.py:560
  30.5 1.0 collective-permute-start.1
  32.4 2.7 list_tables.1
  35.1 2.6 collective-permute-done.3.refs_4_.refs_3_.refs_5_
  37.7 14.8 %collective-permute-done.2.refs_3_.refs_2_.refs_4_ = bf16[1024,128]{1,0:T(8,128)(2,1)S(1)} collective-permute-done((bf16[1024,128]{1,0:T(8,128)(2,1)}, bf16[1024,128]{1,0:T(8,128)(2,1)S(1)}, u32[]{:S(2)}, u32[]{:S(2)}) %collective-permute-start.2) | collective-permute-done | bytes 262176 | tf_op jit(solution)/shard_map/ppermute | solution.py:560
  52.4 1.1 copy-done.5
  54.2 1.4 pack_blocks.3
  56.2 2.7 collective-permute-start.5
  59.0 2.0 collective-permute-start.4
  61.0 4.8 %row_tables.1 = (s32[64]{0:T(128)}, s32[36]{0:T(128)}) custom-call(s32[1]{0:T(128)} %bitcast.where, s32[192]{0:T(256)} %reshape.25.named), custom_call_target="tpu_custom_call" | custom-call | bytes 1024 | tf_op jit(solution)/shard_map/row_tables/pallas_call | solution.py:246
  65.8 15.6 %collective-permute-done.5.refs_6_.refs_2_.refs_3_.refs_8_ = bf16[1024,128]{1,0:T(8,128)(2,1)S(1)} collective-permute-done((bf16[1024,128]{1,0:T(8,128)(2,1)}, bf16[1024,128]{1,0:T(8,128)(2,1)S(1)}, u32[]{:S(2)}, u32[]{:S(2)}) %collective-permute-start.5) | collective-permute-done | bytes 262176 | tf_op jit(solution)/shard_map/ppermute | solution.py:560
  81.4 1.2 copy-done.1
  85.1 1.6 collective-permute-start.11
  87.3 1.3 collective-permute-start.12
  88.7 2.0 collective-permute-start.7
  90.7 12.0 %collective-permute-done.12.refs_12_ = bf16[1536,128]{1,0:T(8,128)(2,1)S(1)} collective-permute-done((bf16[1536,128]{1,0:T(8,128)(2,1)S(1)}, bf16[1536,128]{1,0:T(8,128)(2,1)S(1)}, u32[]{:S(2)}, u32[]{:S(2)}) %collective-permute-start.12) | collective-permute-done | bytes 393248 | tf_op jit(solution)/shard_map/ppermute | solution.py:570
  102.7 3.5 %collective-permute-done.11.refs_11_ = bf16[2048,128]{1,0:T(8,128)(2,1)S(1)} collective-permute-done((bf16[2048,128]{1,0:T(8,128)(2,1)S(1)}, bf16[2048,128]{1,0:T(8,128)(2,1)S(1)}, u32[]{:S(2)}, u32[]{:S(2)}) %collective-permute-start.11) | collective-permute-done | bytes 524320 | tf_op jit(solution)/shard_map/ppermute | solution.py:564
  107.0 38.6 %attend_head.2 = (bf16[1024,2048]{1,0:T(8,128)(2,1)}, bf16[1024,2048]{1,0:T(8,128)(2,1)}, bf16[4096,128]{1,0:T(8,128)(2,1)}, bf16[4096,128]{1,0:T(8,128)(2,1)}, ...) custom-call(s32[88]{0:T(128)} %get-tuple-element.41.found.table, ...), custom_call_target="tpu_custom_call" | custom-call | bytes 1024 | tf_op jit(solution)/shard_map/attend_head/pallas_call | solution.py:532
  145.7 2.0 collective-permute-start.14
  147.7 1.3 collective-permute-start.15
  149.1 6.4 %collective-permute-done.15.refs_4_ = bf16[1536,128]{1,0:T(8,128)(2,1)S(1)} collective-permute-done((bf16[1536,128]{1,0:T(8,128)(2,1)}, bf16[1536,128]{1,0:T(8,128)(2,1)S(1)}, u32[]{:S(2)}, u32[]{:S(2)}) %collective-permute-start.15) | collective-permute-done | bytes 393248 | tf_op jit(solution)/shard_map/ppermute | solution.py:570
  155.5 5.2 %collective-permute-done.13.refs_2_ = bf16[2048,128]{1,0:T(8,128)(2,1)S(1)} collective-permute-done((bf16[2048,128]{1,0:T(8,128)(2,1)}, bf16[2048,128]{1,0:T(8,128)(2,1)S(1)}, u32[]{:S(2)}, u32[]{:S(2)}) %collective-permute-start.13) | collective-permute-done | bytes 524320 | tf_op jit(solution)/shard_map/ppermute | solution.py:564
  160.8 8.1 %collective-permute-done.14.refs_3_ = bf16[2048,128]{1,0:T(8,128)(2,1)S(1)} collective-permute-done((bf16[2048,128]{1,0:T(8,128)(2,1)}, bf16[2048,128]{1,0:T(8,128)(2,1)S(1)}, u32[]{:S(2)}, u32[]{:S(2)}) %collective-permute-start.14) | collective-permute-done | bytes 524320 | tf_op jit(solution)/shard_map/ppermute | solution.py:564
  169.8 5.0 %merge_terms.3 = (f32[2048,128]{1,0:T(8,128)}, bf16[2048,128]{1,0:T(8,128)(2,1)}, bf16[2048,128]{1,0:T(8,128)(2,1)}, bf16[2048,128]{1,0:T(8,128)(2,1)}) custom-call(s32[22]{0:T(128)} %get-tuple-element.49.walk, bf16[4096,128]{1,0:T(8,128)(2,1)} %get-tuple-element.52.refs_0_, bf16[4096,128]{1,0:T(8,128)(2,1)} %get-tuple-element.53.refs_1_, ...), custom_call_target="tpu_custom_call" | custom-call | bytes 1024 | tf_op jit(solution)/shard_map/merge_terms/pallas_call | solution.py:380
  174.8 3.8 %collective-permute-start.16 = (bf16[2048,128]{1,0:T(8,128)(2,1)}, bf16[2048,128]{1,0:T(8,128)(2,1)S(1)}, u32[]{:S(2)}, u32[]{:S(2)}) collective-permute-start(bf16[2048,128]{1,0:T(8,128)(2,1)} %get-tuple-element.57.refs_9_), channel_id=1, source_target_pairs={{0,24},{4,28},{8,0},{12,4},{16,8},{20,12},{24,16},{28,20},{1,25},{... | collective-permute-start | bytes 1572872 | tf_op jit(solution)/shard_map/ppermute | solution.py:560
  178.6 38.4 %attend_head.3 = (bf16[1024,2048]{1,0:T(8,128)(2,1)}, bf16[1024,2048]{1,0:T(8,128)(2,1)}, bf16[4096,128]{1,0:T(8,128)(2,1)}, bf16[4096,128]{1,0:T(8,128)(2,1)}, ...) custom-call(s32[64]{0:T(128)} %get-tuple-element.40.found, ...), custom_call_target="tpu_custom_call", output_to_operand_aliasing={{0}: (9, {}), {1}: (10, {})} | custom-call | bytes 1024 | tf_op jit(solution)/shard_map/attend_head/pallas_call | solution.py:532
  218.8 3.2 %collective-permute-start.20 = (bf16[1536,128]{1,0:T(8,128)(2,1)}, bf16[1536,128]{1,0:T(8,128)(2,1)S(1)}, u32[]{:S(2)}, u32[]{:S(2)}) collective-permute-start(bf16[1536,128]{1,0:T(8,128)(2,1)} %gate.2), channel_id=1, source_target_pairs={{0,12},{1,13},{2,14},{3,15}} | collective-permute-start | bytes 1179656 | tf_op jit(solution)/shard_map/ppermute | solution.py:570
  222.1 8.5 %collective-permute-done.19.refs_1_ = bf16[2048,128]{1,0:T(8,128)(2,1)} collective-permute-done((bf16[2048,128]{1,0:T(8,128)(2,1)}, bf16[2048,128]{1,0:T(8,128)(2,1)}, u32[]{:S(2)}, u32[]{:S(2)}) %collective-permute-start.19) | collective-permute-done | bytes 524320 | tf_op jit(solution)/shard_map/ppermute | solution.py:564
  231.6 3.6 %merge_terms.4 = (f32[1024,128]{1,0:T(8,128)}, bf16[1024,128]{1,0:T(8,128)(2,1)}, bf16[1024,128]{1,0:T(8,128)(2,1)}, bf16[1024,128]{1,0:T(8,128)(2,1)}) custom-call(s32[22]{0:T(128)} %get-tuple-element.49.walk, bf16[4096,128]{1,0:T(8,128)(2,1)} %get-tuple-element.63.refs_0_, bf16[2048,128]{1,0:T(8,128)(2,1)} %collective-permute-done.19.refs_1_, ...), custom_call_target="tpu_custom_call" | custom-call | bytes 1024 | tf_op jit(solution)/shard_map/merge_terms/pallas_call | solution.py:380
  235.2 2.0 collective-permute-start.21
  237.2 5.5 %collective-permute-start.22 = (bf16[1024,128]{1,0:T(8,128)(2,1)}, bf16[1024,128]{1,0:T(8,128)(2,1)}, u32[]{:S(2)}, u32[]{:S(2)}) collective-permute-start(bf16[1024,128]{1,0:T(8,128)(2,1)} %get-tuple-element.68), channel_id=1, source_target_pairs={{0,16},{4,20},{8,24},{12,28},{16,0},{20,4},{24,8},{28,12},{1,17},{... | collective-permute-start | bytes 786440 | tf_op jit(solution)/shard_map/ppermute | solution.py:560
  243.7 3.5 %all-to-all-start.1 = ((bf16[4,2,256,128]{3,2,1,0:T(8,128)(2,1)}), bf16[4,2,256,128]{3,2,1,0:T(8,128)(2,1)S(1)}, u32[]{:S(2)}, u32[]{:S(2)}) async-start(bf16[4,2,256,128]{3,2,1,0:T(8,128)(2,1)} %bitcast.20), calls=%async_computation.1 | async-start | bytes 1048576 | tf_op jit(solution)/shard_map/all_to_all | solution.py:617
  247.2 3.5 %merge_terms.5 = (f32[1024,128]{1,0:T(8,128)}, bf16[1024,128]{1,0:T(8,128)(2,1)}, bf16[1024,128]{1,0:T(8,128)(2,1)}, bf16[1024,128]{1,0:T(8,128)(2,1)}) custom-call(s32[22]{0:T(128)} %get-tuple-element.49.walk, bf16[4096,128]{1,0:T(8,128)(2,1)} %get-tuple-element.70.refs_0_, bf16[2048,128]{1,0:T(8,128)(2,1)} %collective-permute-done.24.refs_1_, ...), custom_call_target="tpu_custom_call" | custom-call | bytes 1024 | tf_op jit(solution)/shard_map/merge_terms/pallas_call | solution.py:380
  250.8 3.8 %collective-permute-start.25 = (bf16[1024,128]{1,0:T(8,128)(2,1)}, bf16[1024,128]{1,0:T(8,128)(2,1)S(1)}, u32[]{:S(2)}, u32[]{:S(2)}) collective-permute-start(bf16[1024,128]{1,0:T(8,128)(2,1)} %get-tuple-element.73), channel_id=1, source_target_pairs={{0,24},{4,28},{8,0},{12,4},{16,8},{20,12},{24,16},{28,20},{1,25},{... | collective-permute-start | bytes 786440 | tf_op jit(solution)/shard_map/ppermute | solution.py:560
  254.6 1.9 collective-permute-start.27
  256.5 5.3 %collective-permute-done.22 = bf16[1024,128]{1,0:T(8,128)(2,1)} collective-permute-done((bf16[1024,128]{1,0:T(8,128)(2,1)}, bf16[1024,128]{1,0:T(8,128)(2,1)}, u32[]{:S(2)}, u32[]{:S(2)}) %collective-permute-start.22) | collective-permute-done | bytes 262176 | tf_op jit(solution)/shard_map/ppermute | solution.py:560
  261.8 1.8 add_convert_fusion.2
  263.7 15.6 %all-to-all-start.2 = ((bf16[4,1,256,128]{3,2,1,0:T(8,128)(2,1)}), bf16[4,1,256,128]{3,2,1,0:T(8,128)(2,1)S(1)}, u32[]{:S(2)}, u32[]{:S(2)}) async-start(bf16[4,1,256,128]{3,2,1,0:T(8,128)(2,1)} %bitcast.5), calls=%async_computation.2 | async-start | bytes 524288 | tf_op jit(solution)/shard_map/all_to_all | solution.py:617
  279.3 1.0 collective-permute-done.26
  280.4 1.9 add_convert_fusion.1
  282.2 3.1 %all-to-all-done.2 = bf16[4,1,256,128]{3,2,1,0:T(8,128)(2,1)S(1)} async-done(((bf16[4,1,256,128]{3,2,1,0:T(8,128)(2,1)}), bf16[4,1,256,128]{3,2,1,0:T(8,128)(2,1)S(1)}, u32[]{:S(2)}, u32[]{:S(2)}) %all-to-all-start.2) | async-done | bytes 262176 | tf_op jit(solution)/shard_map/all_to_all | solution.py:617
  285.4 3.4 %all-to-all-start.3 = ((bf16[4,1,256,128]{3,2,1,0:T(8,128)(2,1)}), bf16[4,1,256,128]{3,2,1,0:T(8,128)(2,1)S(1)}, u32[]{:S(2)}, u32[]{:S(2)}) async-start(bf16[4,1,256,128]{3,2,1,0:T(8,128)(2,1)} %bitcast.11), calls=%async_computation.3 | async-start | bytes 524288 | tf_op jit(solution)/shard_map/all_to_all | solution.py:617
  290.3 4.4 %all-to-all-done.3 = bf16[4,1,256,128]{3,2,1,0:T(8,128)(2,1)S(1)} async-done(((bf16[4,1,256,128]{3,2,1,0:T(8,128)(2,1)}), bf16[4,1,256,128]{3,2,1,0:T(8,128)(2,1)S(1)}, u32[]{:S(2)}, u32[]{:S(2)}) %all-to-all-start.3) | async-done | bytes 262176 | tf_op jit(solution)/shard_map/all_to_all | solution.py:617
  295.0 1.0 copy.31
  (113 shorter events, 12.5 us)
Async XLA Ops:
  0.6 30.9 %copy-start.33 = (s32[64,3]{0,1:T(4,128)S(1)}, s32[64,3]{0,1:T(4,128)}, u32[]{:S(2)}) copy-start(s32[64,3]{0,1:T(4,128)} %param.9) | copy-start | bytes 2308
  24.6 27.8 %collective-permute-start = (bf16[2048,128]{1,0:T(8,128)(2,1)}, bf16[2048,128]{1,0:T(8,128)(2,1)S(1)}, u32[]{:S(2)}, u32[]{:S(2)}) collective-permute-start(bf16[2048,128]{1,0:T(8,128)(2,1)} %get-tuple-element.42.refs_0_.refs_5_.refs_2_), channel_id=1, source_target_pairs={{0,4},{4,0},{8,12},{12,8},{16,20},{20,16},{24,28},{28,24},{1,5},{5... | collective-permute-start | bytes 1572872 | tf_op jit(solution)/shard_map/ppermute | solution.py:564
  26.9 10.7 %collective-permute-start.3 = (bf16[1024,128]{1,0:T(8,128)(2,1)}, bf16[1024,128]{1,0:T(8,128)(2,1)S(1)}, u32[]{:S(2)}, u32[]{:S(2)}) collective-permute-start(bf16[1024,128]{1,0:T(8,128)(2,1)} %get-tuple-element.44.refs_0_.refs_2_), channel_id=1, source_target_pairs={{0,24},{4,28},{8,0},{12,4},{16,8},{20,12},{24,16},{28,20},{1,25},{... | collective-permute-start | bytes 786440 | tf_op jit(solution)/shard_map/ppermute | solution.py:560
  30.5 21.9 %collective-permute-start.2 = (bf16[1024,128]{1,0:T(8,128)(2,1)}, bf16[1024,128]{1,0:T(8,128)(2,1)S(1)}, u32[]{:S(2)}, u32[]{:S(2)}) collective-permute-start(bf16[1024,128]{1,0:T(8,128)(2,1)} %get-tuple-element.44.refs_0_.refs_2_), channel_id=1, source_target_pairs={{0,16},{4,20},{8,24},{12,28},{16,0},{20,4},{24,8},{28,12},{1,17},{... | collective-permute-start | bytes 786440 | tf_op jit(solution)/shard_map/ppermute | solution.py:560
  30.5 21.9 %collective-permute-start.1 = (bf16[1024,128]{1,0:T(8,128)(2,1)}, bf16[1024,128]{1,0:T(8,128)(2,1)S(1)}, u32[]{:S(2)}, u32[]{:S(2)}) collective-permute-start(bf16[1024,128]{1,0:T(8,128)(2,1)} %get-tuple-element.44.refs_0_.refs_2_), channel_id=1, source_target_pairs={{0,8},{4,12},{8,16},{12,20},{16,24},{20,28},{24,0},{28,4},{1,9},{5... | collective-permute-start | bytes 786440 | tf_op jit(solution)/shard_map/ppermute | solution.py:560
  35.1 49.3 %copy-start.14 = (s32[22]{0:T(128)S(1)}, s32[22]{0:T(128)}, u32[]{:S(2)}) copy-start(s32[22]{0:T(128)} %get-tuple-element.49.walk) | copy-start | bytes 268
  37.7 49.6 %copy-start.8 = (bf16[1024,128]{1,0:T(8,128)(2,1)}, bf16[1024,128]{1,0:T(8,128)(2,1)S(1)}, u32[]{:S(2)}) copy-start(bf16[1024,128]{1,0:T(8,128)(2,1)S(1)} %collective-permute-done.3.refs_4_.refs_3_.refs_5_) | copy-start | bytes 786436
  52.4 34.9 %copy-start.9 = (bf16[1024,128]{1,0:T(8,128)(2,1)}, bf16[1024,128]{1,0:T(8,128)(2,1)S(1)}, u32[]{:S(2)}) copy-start(bf16[1024,128]{1,0:T(8,128)(2,1)S(1)} %collective-permute-done.2.refs_3_.refs_2_.refs_4_) | copy-start | bytes 786436
  52.4 34.9 %copy-start.10 = (bf16[1024,128]{1,0:T(8,128)(2,1)}, bf16[1024,128]{1,0:T(8,128)(2,1)S(1)}, u32[]{:S(2)}) copy-start(bf16[1024,128]{1,0:T(8,128)(2,1)S(1)} %collective-permute-done.1.refs_2_.refs_1_.refs_3_) | copy-start | bytes 786436
  52.4 34.9 %copy-start = (bf16[2048,128]{1,0:T(8,128)(2,1)}, bf16[2048,128]{1,0:T(8,128)(2,1)S(1)}, u32[]{:S(2)}) copy-start(bf16[2048,128]{1,0:T(8,128)(2,1)S(1)} %collective-permute-done.refs_1_.refs_4_.refs_6_.refs_3_) | copy-start | bytes 1572868
  54.2 30.2 %copy-start.7 = (bf16[1024,128]{1,0:T(8,128)(2,1)S(1)}, bf16[1024,128]{1,0:T(8,128)(2,1)}, u32[]{:S(2)}) copy-start(bf16[1024,128]{1,0:T(8,128)(2,1)} %get-tuple-element.45.refs_0_.refs_1_.refs_6_) | copy-start | bytes 786436
  54.2 32.4 %copy-start.6 = (bf16[1024,128]{1,0:T(8,128)(2,1)S(1)}, bf16[1024,128]{1,0:T(8,128)(2,1)}, u32[]{:S(2)}) copy-start(bf16[1024,128]{1,0:T(8,128)(2,1)} %get-tuple-element.44.refs_0_.refs_2_) | copy-start | bytes 786436
  55.7 28.7 %collective-permute-start.10 = (bf16[2048,128]{1,0:T(8,128)(2,1)}, bf16[2048,128]{1,0:T(8,128)(2,1)S(1)}, u32[]{:S(2)}, u32[]{:S(2)}) collective-permute-start(bf16[2048,128]{1,0:T(8,128)(2,1)} %pack_blocks.3), channel_id=1, source_target_pairs={{0,4},{4,0},{8,12},{12,8},{16,20},{20,16},{24,28},{28,24},{1,5},{5... | collective-permute-start | bytes 1572872 | tf_op jit(solution)/shard_map/ppermute | solution.py:564
  56.2 9.6 %collective-permute-start.6 = (bf16[1024,128]{1,0:T(8,128)(2,1)}, bf16[1024,128]{1,0:T(8,128)(2,1)S(1)}, u32[]{:S(2)}, u32[]{:S(2)}) collective-permute-start(bf16[1024,128]{1,0:T(8,128)(2,1)} %get-tuple-element.45.refs_0_.refs_1_.refs_6_), channel_id=1, source_target_pairs={{0,24},{4,28},{8,0},{12,4},{16,8},{20,12},{24,16},{28,20},{1,25},{... | collective-permute-start | bytes 786440 | tf_op jit(solution)/shard_map/ppermute | solution.py:560
  56.2 25.2 %collective-permute-start.5 = (bf16[1024,128]{1,0:T(8,128)(2,1)}, bf16[1024,128]{1,0:T(8,128)(2,1)S(1)}, u32[]{:S(2)}, u32[]{:S(2)}) collective-permute-start(bf16[1024,128]{1,0:T(8,128)(2,1)} %get-tuple-element.45.refs_0_.refs_1_.refs_6_), channel_id=1, source_target_pairs={{0,16},{4,20},{8,24},{12,28},{16,0},{20,4},{24,8},{28,12},{1,17},{... | collective-permute-start | bytes 786440 | tf_op jit(solution)/shard_map/ppermute | solution.py:560
  59.0 22.5 %collective-permute-start.4 = (bf16[1024,128]{1,0:T(8,128)(2,1)}, bf16[1024,128]{1,0:T(8,128)(2,1)S(1)}, u32[]{:S(2)}, u32[]{:S(2)}) collective-permute-start(bf16[1024,128]{1,0:T(8,128)(2,1)} %get-tuple-element.45.refs_0_.refs_1_.refs_6_), channel_id=1, source_target_pairs={{0,8},{4,12},{8,16},{12,20},{16,24},{20,28},{24,0},{28,4},{1,9},{5... | collective-permute-start | bytes 786440 | tf_op jit(solution)/shard_map/ppermute | solution.py:560
  65.8 41.2 %copy-start.2 = (bf16[1024,128]{1,0:T(8,128)(2,1)}, bf16[1024,128]{1,0:T(8,128)(2,1)S(1)}, u32[]{:S(2)}) copy-start(bf16[1024,128]{1,0:T(8,128)(2,1)S(1)} %collective-permute-done.6.refs_7_.refs_3_.refs_4_.refs_9_) | copy-start | bytes 786436
  81.4 25.6 %copy-start.3 = (bf16[1024,128]{1,0:T(8,128)(2,1)}, bf16[1024,128]{1,0:T(8,128)(2,1)S(1)}, u32[]{:S(2)}) copy-start(bf16[1024,128]{1,0:T(8,128)(2,1)S(1)} %collective-permute-done.5.refs_6_.refs_2_.refs_3_.refs_8_) | copy-start | bytes 786436
  81.4 25.6 %copy-start.4 = (bf16[1024,128]{1,0:T(8,128)(2,1)}, bf16[1024,128]{1,0:T(8,128)(2,1)S(1)}, u32[]{:S(2)}) copy-start(bf16[1024,128]{1,0:T(8,128)(2,1)S(1)} %collective-permute-done.4.refs_5_.refs_1_.refs_2_.refs_7_) | copy-start | bytes 786436
  84.3 22.7 %copy-start.12 = (bf16[3072,128]{1,0:T(8,128)(2,1)}, bf16[3072,128]{1,0:T(8,128)(2,1)S(1)}, u32[]{:S(2)}) copy-start(bf16[3072,128]{1,0:T(8,128)(2,1)S(1)} %get-tuple-element.46.refs_13_) | copy-start | bytes 2359300
  84.3 63.4 %collective-permute-start.8 = (bf16[3072,128]{1,0:T(8,128)(2,1)S(1)}, bf16[3072,128]{1,0:T(8,128)(2,1)S(1)}, u32[]{:S(2)}, u32[]{:S(2)}) collective-permute-start(bf16[3072,128]{1,0:T(8,128)(2,1)S(1)} %get-tuple-element.47), channel_id=1, source_target_pairs={{0,16},{4,20},{8,24},{12,28},{16,0},{20,4},{24,8},{28,12},{1,17},{... | collective-permute-start | bytes 2359304 | tf_op jit(solution)/shard_map/ppermute | solution.py:560
  85.1 21.2 %collective-permute-start.11 = (bf16[2048,128]{1,0:T(8,128)(2,1)S(1)}, bf16[2048,128]{1,0:T(8,128)(2,1)S(1)}, u32[]{:S(2)}, u32[]{:S(2)}) collective-permute-start(bf16[2048,128]{1,0:T(8,128)(2,1)S(1)} %pack_blocks.4), channel_id=1, source_target_pairs={{0,4},{4,0},{8,12},{12,8},{16,20},{20,16},{24,28},{28,24},{1,5},{5... | collective-permute-start | bytes 1572872 | tf_op jit(solution)/shard_map/ppermute | solution.py:564
  87.3 15.4 %collective-permute-start.12 = (bf16[1536,128]{1,0:T(8,128)(2,1)S(1)}, bf16[1536,128]{1,0:T(8,128)(2,1)S(1)}, u32[]{:S(2)}, u32[]{:S(2)}) collective-permute-start(bf16[1536,128]{1,0:T(8,128)(2,1)S(1)} %pack_blocks.5), channel_id=1, source_target_pairs={{12,0},{13,1},{14,2},{15,3}} | collective-permute-start | bytes 1179656 | tf_op jit(solution)/shard_map/ppermute | solution.py:570
  88.6 60.5 %collective-permute-start.9 = (bf16[3072,128]{1,0:T(8,128)(2,1)S(1)}, bf16[3072,128]{1,0:T(8,128)(2,1)S(1)}, u32[]{:S(2)}, u32[]{:S(2)}) collective-permute-start(bf16[3072,128]{1,0:T(8,128)(2,1)S(1)} %get-tuple-element.48), channel_id=1, source_target_pairs={{0,24},{4,28},{8,0},{12,4},{16,8},{20,12},{24,16},{28,20},{1,25},{... | collective-permute-start | bytes 2359304 | tf_op jit(solution)/shard_map/ppermute | solution.py:560
  88.7 60.4 %collective-permute-start.7 = (bf16[3072,128]{1,0:T(8,128)(2,1)S(1)}, bf16[3072,128]{1,0:T(8,128)(2,1)S(1)}, u32[]{:S(2)}, u32[]{:S(2)}) collective-permute-start(bf16[3072,128]{1,0:T(8,128)(2,1)S(1)} %get-tuple-element.46.refs_13_), channel_id=1, source_target_pairs={{0,8},{4,12},{8,16},{12,20},{16,24},{20,28},{24,0},{28,4},{1,9},{5... | collective-permute-start | bytes 2359304 | tf_op jit(solution)/shard_map/ppermute | solution.py:560
  145.6 15.1 %collective-permute-start.13 = (bf16[2048,128]{1,0:T(8,128)(2,1)}, bf16[2048,128]{1,0:T(8,128)(2,1)S(1)}, u32[]{:S(2)}, u32[]{:S(2)}) collective-permute-start(bf16[2048,128]{1,0:T(8,128)(2,1)} %get-tuple-element.54), channel_id=1, source_target_pairs={{0,4},{4,0},{8,12},{12,8},{16,20},{20,16},{24,28},{28,24},{1,5},{5... | collective-permute-start | bytes 1572872 | tf_op jit(solution)/shard_map/ppermute | solution.py:564
  145.7 23.2 %collective-permute-start.14 = (bf16[2048,128]{1,0:T(8,128)(2,1)}, bf16[2048,128]{1,0:T(8,128)(2,1)S(1)}, u32[]{:S(2)}, u32[]{:S(2)}) collective-permute-start(bf16[2048,128]{1,0:T(8,128)(2,1)} %get-tuple-element.55), channel_id=1, source_target_pairs={{0,4},{4,0},{8,12},{12,8},{16,20},{20,16},{24,28},{28,24},{1,5},{5... | collective-permute-start | bytes 1572872 | tf_op jit(solution)/shard_map/ppermute | solution.py:564
  147.7 7.8 %collective-permute-start.15 = (bf16[1536,128]{1,0:T(8,128)(2,1)}, bf16[1536,128]{1,0:T(8,128)(2,1)S(1)}, u32[]{:S(2)}, u32[]{:S(2)}) collective-permute-start(bf16[1536,128]{1,0:T(8,128)(2,1)} %get-tuple-element.56), channel_id=1, source_target_pairs={{0,12},{1,13},{2,14},{3,15}} | collective-permute-start | bytes 1179656 | tf_op jit(solution)/shard_map/ppermute | solution.py:570
  174.8 42.8 %collective-permute-start.17 = (bf16[2048,128]{1,0:T(8,128)(2,1)}, bf16[2048,128]{1,0:T(8,128)(2,1)S(1)}, u32[]{:S(2)}, u32[]{:S(2)}) collective-permute-start(bf16[2048,128]{1,0:T(8,128)(2,1)} %get-tuple-element.61), channel_id=1, source_target_pairs={{0,16},{4,20},{8,24},{12,28},{16,0},{20,4},{24,8},{28,12},{1,17},{... | collective-permute-start | bytes 1572872 | tf_op jit(solution)/shard_map/ppermute | solution.py:560
  174.8 42.8 %collective-permute-start.18 = (bf16[2048,128]{1,0:T(8,128)(2,1)}, bf16[2048,128]{1,0:T(8,128)(2,1)S(1)}, u32[]{:S(2)}, u32[]{:S(2)}) collective-permute-start(bf16[2048,128]{1,0:T(8,128)(2,1)} %get-tuple-element.62), channel_id=1, source_target_pairs={{0,8},{4,12},{8,16},{12,20},{16,24},{20,28},{24,0},{28,4},{1,9},{5... | collective-permute-start | bytes 1572872 | tf_op jit(solution)/shard_map/ppermute | solution.py:560
  174.8 42.9 %collective-permute-start.16 = (bf16[2048,128]{1,0:T(8,128)(2,1)}, bf16[2048,128]{1,0:T(8,128)(2,1)S(1)}, u32[]{:S(2)}, u32[]{:S(2)}) collective-permute-start(bf16[2048,128]{1,0:T(8,128)(2,1)} %get-tuple-element.57.refs_9_), channel_id=1, source_target_pairs={{0,24},{4,28},{8,0},{12,4},{16,8},{20,12},{24,16},{28,20},{1,25},{... | collective-permute-start | bytes 1572872 | tf_op jit(solution)/shard_map/ppermute | solution.py:560
  217.0 25.7 %copy-start.26 = (f32[2048,128]{1,0:T(8,128)S(1)}, f32[2048,128]{1,0:T(8,128)}, u32[]{:S(2)}) copy-start(f32[2048,128]{1,0:T(8,128)} %get-tuple-element.60) | copy-start | bytes 3145732
  217.0 13.5 %collective-permute-start.19 = (bf16[2048,128]{1,0:T(8,128)(2,1)}, bf16[2048,128]{1,0:T(8,128)(2,1)}, u32[]{:S(2)}, u32[]{:S(2)}) collective-permute-start(bf16[2048,128]{1,0:T(8,128)(2,1)} %get-tuple-element.64), channel_id=1, source_target_pairs={{0,4},{4,0},{8,12},{12,8},{16,20},{20,16},{24,28},{28,24},{1,5},{5... | collective-permute-start | bytes 1572872 | tf_op jit(solution)/shard_map/ppermute | solution.py:564
  218.7 23.9 %copy-start.17 = (bf16[2048,128]{1,0:T(8,128)(2,1)S(1)}, bf16[2048,128]{1,0:T(8,128)(2,1)}, u32[]{:S(2)}) copy-start(bf16[2048,128]{1,0:T(8,128)(2,1)} %copy-done.16) | copy-start | bytes 1572868
  218.7 23.9 %copy-start.19 = (bf16[2048,128]{1,0:T(8,128)(2,1)S(1)}, bf16[2048,128]{1,0:T(8,128)(2,1)}, u32[]{:S(2)}) copy-start(bf16[2048,128]{1,0:T(8,128)(2,1)} %copy-done.18) | copy-start | bytes 1572868
  218.7 23.9 %copy-start.21 = (bf16[2048,128]{1,0:T(8,128)(2,1)S(1)}, bf16[2048,128]{1,0:T(8,128)(2,1)}, u32[]{:S(2)}) copy-start(bf16[2048,128]{1,0:T(8,128)(2,1)} %copy-done.20) | copy-start | bytes 1572868
  218.8 12.1 %collective-permute-start.20 = (bf16[1536,128]{1,0:T(8,128)(2,1)}, bf16[1536,128]{1,0:T(8,128)(2,1)S(1)}, u32[]{:S(2)}, u32[]{:S(2)}) collective-permute-start(bf16[1536,128]{1,0:T(8,128)(2,1)} %gate.2), channel_id=1, source_target_pairs={{0,12},{1,13},{2,14},{3,15}} | collective-permute-start | bytes 1179656 | tf_op jit(solution)/shard_map/ppermute | solution.py:570
  222.0 25.3 %collective-permute-start.24 = (bf16[2048,128]{1,0:T(8,128)(2,1)}, bf16[2048,128]{1,0:T(8,128)(2,1)}, u32[]{:S(2)}, u32[]{:S(2)}) collective-permute-start(bf16[2048,128]{1,0:T(8,128)(2,1)} %gate.3), channel_id=1, source_target_pairs={{0,4},{4,0},{8,12},{12,8},{16,20},{20,16},{24,28},{28,24},{1,5},{5... | collective-permute-start | bytes 1572872 | tf_op jit(solution)/shard_map/ppermute | solution.py:564
  235.2 26.7 %copy-start.27 = (f32[1024,128]{1,0:T(8,128)S(1)}, f32[1024,128]{1,0:T(8,128)}, u32[]{:S(2)}) copy-start(f32[1024,128]{1,0:T(8,128)} %get-tuple-element.66) | copy-start | bytes 1572868
  235.2 19.4 %collective-permute-start.21 = (bf16[1024,128]{1,0:T(8,128)(2,1)}, bf16[1024,128]{1,0:T(8,128)(2,1)S(1)}, u32[]{:S(2)}, u32[]{:S(2)}) collective-permute-start(bf16[1024,128]{1,0:T(8,128)(2,1)} %get-tuple-element.67), channel_id=1, source_target_pairs={{0,24},{4,28},{8,0},{12,4},{16,8},{20,12},{24,16},{28,20},{1,25},{... | collective-permute-start | bytes 786440 | tf_op jit(solution)/shard_map/ppermute | solution.py:560
  237.2 24.7 %collective-permute-start.22 = (bf16[1024,128]{1,0:T(8,128)(2,1)}, bf16[1024,128]{1,0:T(8,128)(2,1)}, u32[]{:S(2)}, u32[]{:S(2)}) collective-permute-start(bf16[1024,128]{1,0:T(8,128)(2,1)} %get-tuple-element.68), channel_id=1, source_target_pairs={{0,16},{4,20},{8,24},{12,28},{16,0},{20,4},{24,8},{28,12},{1,17},{... | collective-permute-start | bytes 786440 | tf_op jit(solution)/shard_map/ppermute | solution.py:560
  242.6 19.2 %collective-permute-start.23 = (bf16[1024,128]{1,0:T(8,128)(2,1)}, bf16[1024,128]{1,0:T(8,128)(2,1)}, u32[]{:S(2)}, u32[]{:S(2)}) collective-permute-start(bf16[1024,128]{1,0:T(8,128)(2,1)} %get-tuple-element.69), channel_id=1, source_target_pairs={{0,8},{4,12},{8,16},{12,20},{16,24},{20,28},{24,0},{28,4},{1,9},{5... | collective-permute-start | bytes 786440 | tf_op jit(solution)/shard_map/ppermute | solution.py:560
  243.7 20.0 %all-to-all-start.1 = ((bf16[4,2,256,128]{3,2,1,0:T(8,128)(2,1)}), bf16[4,2,256,128]{3,2,1,0:T(8,128)(2,1)S(1)}, u32[]{:S(2)}, u32[]{:S(2)}) async-start(bf16[4,2,256,128]{3,2,1,0:T(8,128)(2,1)} %bitcast.20), calls=%async_computation.1 | async-start | bytes 1048576 | tf_op jit(solution)/shard_map/all_to_all | solution.py:617
  250.8 28.5 %collective-permute-start.25 = (bf16[1024,128]{1,0:T(8,128)(2,1)}, bf16[1024,128]{1,0:T(8,128)(2,1)S(1)}, u32[]{:S(2)}, u32[]{:S(2)}) collective-permute-start(bf16[1024,128]{1,0:T(8,128)(2,1)} %get-tuple-element.73), channel_id=1, source_target_pairs={{0,24},{4,28},{8,0},{12,4},{16,8},{20,12},{24,16},{28,20},{1,25},{... | collective-permute-start | bytes 786440 | tf_op jit(solution)/shard_map/ppermute | solution.py:560
  254.6 25.8 %collective-permute-start.26 = (bf16[1024,128]{1,0:T(8,128)(2,1)}, bf16[1024,128]{1,0:T(8,128)(2,1)S(1)}, u32[]{:S(2)}, u32[]{:S(2)}) collective-permute-start(bf16[1024,128]{1,0:T(8,128)(2,1)} %get-tuple-element.74), channel_id=1, source_target_pairs={{0,16},{4,20},{8,24},{12,28},{16,0},{20,4},{24,8},{28,12},{1,17},{... | collective-permute-start | bytes 786440 | tf_op jit(solution)/shard_map/ppermute | solution.py:560
  254.6 25.8 %collective-permute-start.27 = (bf16[1024,128]{1,0:T(8,128)(2,1)}, bf16[1024,128]{1,0:T(8,128)(2,1)S(1)}, u32[]{:S(2)}, u32[]{:S(2)}) collective-permute-start(bf16[1024,128]{1,0:T(8,128)(2,1)} %get-tuple-element.75), channel_id=1, source_target_pairs={{0,8},{4,12},{8,16},{12,20},{16,24},{20,28},{24,0},{28,4},{1,9},{5... | collective-permute-start | bytes 786440 | tf_op jit(solution)/shard_map/ppermute | solution.py:560
  263.7 21.7 %all-to-all-start.2 = ((bf16[4,1,256,128]{3,2,1,0:T(8,128)(2,1)}), bf16[4,1,256,128]{3,2,1,0:T(8,128)(2,1)S(1)}, u32[]{:S(2)}, u32[]{:S(2)}) async-start(bf16[4,1,256,128]{3,2,1,0:T(8,128)(2,1)} %bitcast.5), calls=%async_computation.2 | async-start | bytes 524288 | tf_op jit(solution)/shard_map/all_to_all | solution.py:617
  285.4 9.4 %all-to-all-start.3 = ((bf16[4,1,256,128]{3,2,1,0:T(8,128)(2,1)}), bf16[4,1,256,128]{3,2,1,0:T(8,128)(2,1)S(1)}, u32[]{:S(2)}, u32[]{:S(2)}) async-start(bf16[4,1,256,128]{3,2,1,0:T(8,128)(2,1)} %bitcast.11), calls=%async_computation.3 | async-start | bytes 524288 | tf_op jit(solution)/shard_map/all_to_all | solution.py:617
  (17 other events, 118.3 us)
